TPU v7x, 32 devices: a whole 2x2x4 slice. The times are simulated.
32 devices in a mesh: dp: 16 (over z, y, core), tap: 2 (over x).
Axes of the slice: x: 2, y: 2, z: 4, core: 2. Of those that a mesh axis runs over, the one named last changes fastest.
Arguments:
- block_input: bfloat16 [32768, 512], P('dp'), may hold values from -6 to 6
- conv_weight: bfloat16 [10, 512, 512], P('tap'), may hold values from -0.09375 to 0.09375
- slot_tap_table: int32 [10], P('tap'), may hold values from 0 to 8, as said below
- conv_bias: float32 [512], replicated, may hold values from -3 to 3
- conv_norm_gain: float32 [512], replicated, may hold values from 0.5 to 1.5
- conv_norm_bias: float32 [512], replicated, may hold values from -3 to 3
- w_in: bfloat16 [512, 2048], replicated, may hold values from -0.25 to 0.25
- b_in: float32 [2048], replicated, may hold values from -3 to 3
- w_out: bfloat16 [2048, 512], replicated, may hold values from -0.125 to 0.125
- b_out: float32 [512], replicated, may hold values from -3 to 3
- ffn_norm_gain: float32 [512], replicated, may hold values from 0.5 to 1.5
- ffn_norm_bias: float32 [512], replicated, may hold values from -3 to 3
- species_id: int32 [64], P('dp'), may hold values from 0 to 15, as said below
- species_count: int32 [16], replicated, may hold values from 1 to 7, as said below
- out_grad: bfloat16 [32768, 512], P(('dp', 'tap')), may hold values from -6 to 6
Outputs:
- block_output: bfloat16 [32768, 512], P(('dp', 'tap'))
- input_grad: float32 [32768, 512], P(('dp', 'tap'))
- conv_weight_grad: float32 [10, 512, 512], P('tap', 'dp')
- conv_bias_grad: float32 [512], P(('dp', 'tap'))
- conv_norm_gain_grad: float32 [512], P(('dp', 'tap'))
- conv_norm_bias_grad: float32 [512], P(('dp', 'tap'))
- w_in_grad: float32 [512, 2048], P(('dp', 'tap'))
- b_in_grad: float32 [2048], P(('dp', 'tap'))
- w_out_grad: float32 [2048, 512], P(('dp', 'tap'))
- b_out_grad: float32 [512], P(('dp', 'tap'))
- ffn_norm_gain_grad: float32 [512], P(('dp', 'tap'))
- ffn_norm_bias_grad: float32 [512], P(('dp', 'tap'))
Inputs may be any that keep to these rules, and one draw needn't show every extreme that they name: `species_id`: windows are grouped by species: ids never fall along the windows, and species s has exactly species_count[s] windows. `species_count`: the counts sum to 64; species 2i and 2i + 1 together have 8 windows. `slot_tap_table`: each of the 9 taps is applied by at least one slot.
All inputs are finite; a program needn't handle non-finite values.
Results may differ from a plain program's by a relative error of at most 0.0065.
Values may be sent and summed in bfloat16 or wider, within the bound.
No kernel may reach another device: no remote copies, remote signals or barrier semaphores. Data moves between devices by JAX's collectives and lax.ppermute only.
A program may use at most 128 MiB of HBM per device.

v0:
```python
import functools

import jax
import jax.numpy as jnp
from jax import lax
from jax.experimental import pallas as pl
from jax.experimental.pallas import tpu as pltpu
from jax.sharding import PartitionSpec as P

KERNEL_TAPS = 9
DILATION_STEP = 16
WINDOW_LENGTH = 512


def layer_norm(values):
    mean_val = jnp.mean(values, axis=-1, keepdims=True)
    center = values - mean_val
    spread = jnp.mean(center * center, axis=-1, keepdims=True)
    return center * lax.rsqrt(spread + 1e-05)


def exact_gelu(values):
    return jax.nn.gelu(values, approximate=False)


def conv_branch(pre_conv, gain_one, bias_one):
    return layer_norm(exact_gelu(pre_conv)) * gain_one + bias_one


def ffn_branch(pre_out, gain_two, bias_two):
    return layer_norm(pre_out) * gain_two + bias_two


def shift_stack(win_rows, tap_table, forward):
    tap_extent = KERNEL_TAPS // 2 * DILATION_STEP
    padded_input = jnp.pad(win_rows, ((0, 0), (tap_extent, tap_extent), (0, 0)))
    pieces = []
    for index_of_slot in range(tap_table.shape[0]):
        if forward:
            tap_offset = tap_table[index_of_slot]
        else:
            tap_offset = KERNEL_TAPS - 1 - tap_table[index_of_slot]
        shifted_input = lax.dynamic_slice_in_dim(
            padded_input, tap_offset * DILATION_STEP, WINDOW_LENGTH, 1
        )
        pieces.append(shifted_input.reshape(-1, win_rows.shape[2]))
    return jnp.stack(pieces)


def contract_rows(left, right):
    return lax.dot_general(
        left, right, (((0,), (0,)), ((), ())), preferred_element_type=jnp.float32
    )


def contract_cols(left, right):
    return lax.dot_general(
        left, right, (((1,), (1,)), ((), ())), preferred_element_type=jnp.float32
    )


def swap_dp(value, bit):
    count = lax.axis_size("dp")
    return lax.ppermute(value, "dp", [(i, i ^ (1 << bit)) for i in range(count)])


def swap_tap(value):
    return lax.ppermute(value, "tap", [(0, 1), (1, 0)])


def halve(part, order, kind):
    dp_bits = (lax.axis_size("dp") - 1).bit_length()
    place = lax.axis_index("dp")
    tap = lax.axis_index("tap")
    labels = ["t"] + list(range(dp_bits - 1, -1, -1))
    for step in order:
        axis = labels.index(step)
        labels.pop(axis)
        mine = tap if step == "t" else (place >> step) & 1
        keep = lax.dynamic_index_in_dim(part, mine, axis, keepdims=False)
        send = lax.dynamic_index_in_dim(part, 1 - mine, axis, keepdims=False).astype(kind)
        got = swap_tap(send) if step == "t" else swap_dp(send, step)
        part = keep + got.astype(jnp.float32)
    return part


def orders(dp_bits):
    rest = list(range(2, dp_bits))
    first = [0, "t", 1] + rest
    second = [0, 1] + rest[:1] + ["t"] + rest[1:]
    third = [0] + rest[:1] + ["t", 1] + rest[1:]
    return first, second, third


def plain_shards(
    block_input,
    conv_weight,
    slot_tap_table,
    conv_bias,
    conv_norm_gain,
    conv_norm_bias,
    w_in,
    b_in,
    w_out,
    b_out,
    ffn_norm_gain,
    ffn_norm_bias,
    species_id,
    species_count,
    out_grad,
):
    tap_count = lax.axis_size("tap")
    my_index = lax.axis_index("tap")
    core = lax.axis_index("dp") & 1
    dp_bits = (lax.axis_size("dp") - 1).bit_length()
    tok_dev, chan_width = block_input.shape
    hid_width = w_in.shape[1]
    half_rows = tok_dev // tap_count
    windows = tok_dev // WINDOW_LENGTH
    my_windows = windows // tap_count
    own_slots = conv_weight.shape[0]
    half_chan = chan_width // 2
    first, second, third = orders(dp_bits)

    other_table = swap_tap(slot_tap_table)
    part_send = lax.dynamic_slice_in_dim(conv_weight, core * half_chan, half_chan, 1)
    part_here = swap_tap(part_send)
    part_mate = swap_dp(part_here, 0)
    low_part = jnp.where(core == 0, part_here, part_mate)
    high_part = jnp.where(core == 0, part_mate, part_here)
    other_weight = jnp.concatenate([low_part, high_part], axis=1)

    my_x = lax.dynamic_slice_in_dim(block_input, my_index * half_rows, half_rows, 0)
    x_windows = my_x.reshape(my_windows, WINDOW_LENGTH, chan_width)
    mine_x = my_x.astype(jnp.float32)
    own_stack = shift_stack(x_windows, slot_tap_table, True)
    other_stack = shift_stack(x_windows, other_table, True)
    conv_out = jnp.einsum("str,sro->to", own_stack, conv_weight, preferred_element_type=jnp.float32)
    conv_out = conv_out + jnp.einsum(
        "str,sro->to", other_stack, other_weight, preferred_element_type=jnp.float32
    )
    pre_conv = conv_out + conv_bias
    norm_one, conv_back = jax.vjp(conv_branch, pre_conv, conv_norm_gain, conv_norm_bias)
    hidden = mine_x + norm_one
    hidden_low = hidden.astype(jnp.bfloat16)
    pre_up = jnp.dot(hidden_low, w_in, preferred_element_type=jnp.float32) + b_in
    activ, activ_back = jax.vjp(exact_gelu, pre_up)
    act_low = activ.astype(jnp.bfloat16)
    pre_out = jnp.dot(act_low, w_out, preferred_element_type=jnp.float32) + b_out
    norm_two, ffn_back = jax.vjp(ffn_branch, pre_out, ffn_norm_gain, ffn_norm_bias)
    block_output = (hidden + norm_two).astype(jnp.bfloat16)
    my_species = lax.dynamic_slice_in_dim(species_id, my_index * my_windows, my_windows, 0)
    species_range = jnp.arange(species_count.shape[0], dtype=jnp.int32)
    matches = my_species[:, None] == species_range[None, :]
    window_count = jnp.sum(jnp.where(matches, species_count[None, :], 0), axis=1)
    window_scale = 4.0 / window_count.astype(jnp.float32)
    grad_y = (
        out_grad.astype(jnp.float32).reshape(my_windows, WINDOW_LENGTH, chan_width)
        * window_scale[:, None, None]
    ).reshape(half_rows, chan_width)
    d_pre_out, d_gain_two, d_bias_two = ffn_back(grad_y)
    d_out_low = d_pre_out.astype(jnp.bfloat16)
    d_w_out = contract_rows(act_low, d_out_low)
    d_b_out = jnp.sum(d_out_low.astype(jnp.float32), axis=0)
    d_activ = contract_cols(d_out_low, w_out)
    (d_pre_up,) = activ_back(d_activ)
    d_up_low = d_pre_up.astype(jnp.bfloat16)
    d_w_in = contract_rows(hidden_low, d_up_low)
    d_b_in = jnp.sum(d_up_low.astype(jnp.float32), axis=0)
    d_hidden = grad_y + contract_cols(d_up_low, w_in)
    d_pre_conv, d_gain_one, d_bias_one = conv_back(d_hidden)
    d_conv_low = d_pre_conv.astype(jnp.bfloat16)
    d_conv_bias = jnp.sum(d_conv_low.astype(jnp.float32), axis=0)
    d_windows = d_conv_low.reshape(my_windows, WINDOW_LENGTH, chan_width)
    own_back = shift_stack(d_windows, slot_tap_table, False)
    other_back = shift_stack(d_windows, other_table, False)
    input_grad = (
        d_hidden
        + jnp.einsum("sto,sro->tr", own_back, conv_weight, preferred_element_type=jnp.float32)
        + jnp.einsum("sto,sro->tr", other_back, other_weight, preferred_element_type=jnp.float32)
    )
    own_terms = jnp.einsum("str,to->sro", own_stack, d_conv_low, preferred_element_type=jnp.float32)
    other_terms = jnp.einsum(
        "str,to->sro", other_stack, d_conv_low, preferred_element_type=jnp.float32
    )
    bits = [2] * dp_bits

    def by_tap(own, other):
        return jnp.where(my_index == 0, jnp.stack([own, other]), jnp.stack([other, own]))

    def conv_part(begin, end, order):
        own = own_terms[begin:end]
        other = other_terms[begin:end]
        both = by_tap(own, other)
        rows = chan_width >> dp_bits
        both = both.reshape([2, end - begin] + bits + [rows, chan_width])
        return halve(jnp.moveaxis(both, 1, 1 + dp_bits), order, jnp.bfloat16)

    cut = own_slots * 2 // 5
    conv_weight_grad = jnp.concatenate(
        [
            conv_part(0, cut, first),
            conv_part(cut, 2 * cut, second),
            conv_part(2 * cut, own_slots, third),
        ]
    )

    def spread(total, order, kind):
        rows = total.shape[0] >> (dp_bits + 1)
        split = total.reshape(bits + [2, rows] + list(total.shape[1:]))
        return halve(jnp.moveaxis(split, dp_bits, 0), order, kind)

    d_w_out_mine = spread(d_w_out, first, jnp.bfloat16)
    d_w_in_mine = spread(d_w_in, second, jnp.bfloat16)
    owners = 2 << dp_bits
    small = [d_b_in, d_b_out, d_conv_bias, d_gain_one, d_bias_one, d_gain_two, d_bias_two]
    joined = jnp.concatenate([v.reshape(owners, -1) for v in small], axis=1)
    joined_mine = spread(joined, third, jnp.float32).reshape(-1)
    vectors = []
    start = 0
    for v in small:
        size = v.shape[0] // owners
        vectors.append(joined_mine[start : start + size])
        start += size
    return (
        block_output,
        input_grad,
        conv_weight_grad,
        vectors[2],
        vectors[3],
        vectors[4],
        d_w_in_mine,
        vectors[0],
        d_w_out_mine,
        vectors[1],
        vectors[5],
        vectors[6],
    )


TILE = 256
COLS = 512
PAD = KERNEL_TAPS // 2 * DILATION_STEP
MIB = 2**20
TABLE_ROWS = 16
F32 = jnp.float32
BF16 = jnp.bfloat16
HBM = pl.BlockSpec(memory_space=pltpu.HBM)
VMEM = pl.BlockSpec(memory_space=pltpu.VMEM)
SMEM = pl.BlockSpec(memory_space=pltpu.SMEM)


def dot_plain(left, right):
    return lax.dot_general(left, right, (((1,), (0,)), ((), ())), preferred_element_type=F32)


def gelu_and_slope(value):
    cdf = 0.5 + 0.5 * lax.erf(value * 0.7071067811865476)
    density = 0.3989422804014327 * jnp.exp(value * value * -0.5)
    return value * cdf, cdf + value * density


def norm_parts(value):
    center = value - jnp.mean(value, axis=-1, keepdims=True)
    spread = jnp.mean(center * center, axis=-1, keepdims=True)
    scale = lax.rsqrt(spread + 1e-05)
    return center * scale, scale


def norm_back(grad, unit):
    return grad - jnp.mean(grad, axis=-1, keepdims=True) - unit * jnp.mean(
        grad * unit, axis=-1, keepdims=True
    )


def fold_rows(value):
    return jnp.sum(value.reshape(value.shape[0] // 8, 8, value.shape[1]), axis=0)


def one_row(value):
    return jnp.sum(value, axis=0, keepdims=True)


def my_bits(dp_bits):
    place = lax.axis_index("dp")
    mine = {bit: (place >> bit) & 1 for bit in range(dp_bits)}
    mine["t"] = lax.axis_index("tap")
    return mine


def relative(order, owner, mine):
    spot = 0
    for label in order:
        spot = spot * 2 + (owner[label] ^ mine[label])
    return spot


def rows_at(start, size):
    return pl.ds(pl.multiple_of(start, 16), size)


def split_copy(source, target, sems, first):
    rows = target.shape[0] // 4
    return [
        pltpu.make_async_copy(
            source.at[at * rows : (at + 1) * rows, :],
            target.at[at * rows : (at + 1) * rows, :],
            sems.at[first + at],
        )
        for at in range(4)
    ]


def wait_all(copies):
    for copy in copies:
        copy.wait()


def clear_pads(pad_ref):
    zeros = jnp.zeros((PAD, pad_ref.shape[2]), pad_ref.dtype)
    for win in range(pad_ref.shape[0]):
        pad_ref[win, 0:PAD, :] = zeros
        pad_ref[win, PAD + WINDOW_LENGTH :, :] = zeros


def each_tile(rows, body, together=1):
    per = WINDOW_LENGTH // TILE

    @pl.loop(0, rows // TILE // together)
    def _(step):
        for member in range(together):
            number = step * together + member
            body(rows_at(number * TILE, TILE), number // per, (number % per) * TILE)


def window_weight(species, counts, win, windows, lanes):
    kind = species[lax.axis_index("tap") * windows + win]
    count = jnp.full((8, lanes), counts[kind], jnp.int32).astype(F32)
    return (4.0 / count)[0:1, :]


def own_conv_kernel(table, x_hbm, weight_hbm, _, x_pad, part, token, weight, sems):
    windows = x_pad.shape[0]
    slots = weight.shape[0]
    base = lax.axis_index("tap") * windows * WINDOW_LENGTH
    copies = []
    for win in range(windows):
        source = x_hbm.at[rows_at(base + win * WINDOW_LENGTH, WINDOW_LENGTH), :]
        copies.append((source, x_pad.at[win, PAD : PAD + WINDOW_LENGTH, :]))
    copies += [(weight_hbm.at[slot], weight.at[slot]) for slot in range(slots)]
    copies = [
        pltpu.make_async_copy(source, target, sems.at[at])
        for at, (source, target) in enumerate(copies)
    ]
    for copy in copies:
        copy.start()
    clear_pads(x_pad)
    token[...] = jnp.zeros(token.shape, token.dtype)
    for copy in copies:
        copy.wait()

    def convolve(rows, win, begin):
        total = None
        for slot in range(slots):
            shifted = rows_at(table[slot] * DILATION_STEP + begin, TILE)
            term = dot_plain(x_pad[win, shifted, :], weight[slot])
            total = term if total is None else total + term
        part[rows, :] = total

    each_tile(part.shape[0], convolve, 2)


def fetch_plan(rows):
    direct = rows // 8
    return direct, (rows - 2 * direct) // 8


def join_pieces(plan, pieces, weight):
    direct, shared = fetch_plan(weight.shape[1])
    place = lax.axis_index("dp")
    for (turn, first), piece in zip(plan, pieces):
        if first is None:
            at = ((place & 1) ^ turn) * direct
            for slot in range(weight.shape[0]):
                part = piece[slot * direct : (slot + 1) * direct, :]
                weight[slot, rows_at(at, direct), :] = part
            continue
        slots = weight.shape[0]
        for begin, place_turn in ((0, turn), (slots, first)):
            if begin < piece.shape[0]:
                at = 2 * direct + ((place & 7) ^ place_turn) * shared
                weight[:, rows_at(at, shared), :] = piece[begin : begin + slots]


def main_kernel(orders, dp_bits, turns, *refs):
    species, counts = refs[:2]
    x_pad, part, grad_hbm, w_in_hbm, w_out_hbm = refs[2:7]
    conv_bias, gain_one, bias_one, b_in, b_out, gain_two, bias_two = refs[7:14]
    pieces = refs[14 : 14 + len(turns)]
    y_hbm, unit, slope, d_up, weight, keep, send, small, grad_in, w_in, table = refs[
        14 + len(turns) : 25 + len(turns)
    ]
    w_out, hidden, low, act, hid_slope, d_out, y_low, result, sums, sem, sems = refs[25 + len(turns) :]
    told = pieces[turns.index((0, None))]
    told_at = told.shape[0] - TABLE_ROWS
    taps = []
    for slot in range(weight.shape[0]):
        line = told[told_at : told_at + TABLE_ROWS, 0:128].astype(F32)
        chosen = lax.broadcasted_iota(jnp.int32, line.shape, 0) == slot
        taps.append(jnp.max(jnp.where(chosen, line, 0.0)).astype(jnp.int32))
        table[slot] = taps[slot]
    mine = my_bits(dp_bits)
    rows_dev, chan = hidden.shape
    hid_width = w_in.shape[1]
    windows = x_pad.shape[0]
    in_copies = split_copy(w_in_hbm, w_in, sems, 0)
    out_copies = split_copy(w_out_hbm, w_out, sems, 4)
    grad_copies = split_copy(grad_hbm, grad_in, sems, 8)
    for copy in in_copies + out_copies + grad_copies:
        copy.start()
    join_pieces(turns, pieces, weight)
    sums[...] = jnp.zeros(sums.shape, F32)

    def first_norm(rows, win, begin):
        total = part[rows, :] + conv_bias[...]
        for slot in range(weight.shape[0]):
            shifted = rows_at(taps[slot] * DILATION_STEP + begin, TILE)
            total = total + dot_plain(x_pad[win, shifted, :], weight[slot])
        value, steep = gelu_and_slope(total)
        normed, scale = norm_parts(value)
        unit[rows, :] = normed
        slope[rows, :] = scale * steep
        here = x_pad[win, rows_at(PAD + begin, TILE), :].astype(F32)
        summed = here + (normed * gain_one[...] + bias_one[...])
        hidden[rows, :] = summed
        low[rows, :] = summed.astype(BF16)

    each_tile(rows_dev, first_norm, 2)
    wait_all(in_copies)

    def go_up(rows, win, begin):
        for at in range(0, hid_width, COLS):
            cols = slice(at, at + COLS)
            up = dot_plain(low[rows, :], w_in[:, cols]) + b_in[:, cols]
            value, steep = gelu_and_slope(up)
            act[rows, cols] = value.astype(BF16)
            hid_slope[rows, cols] = steep

    each_tile(rows_dev, go_up, 2)
    wait_all(out_copies + grad_copies)

    def second_norm(rows, win, begin):
        pre_out = dot_plain(act[rows, :], w_out[...]) + b_out[...]
        normed, scale = norm_parts(pre_out)
        result_rows = hidden[rows, :] + (normed * gain_two[...] + bias_two[...])
        y_low[rows, :] = result_rows.astype(BF16)
        grad_y = grad_in[rows, :].astype(F32) * window_weight(species, counts, win, windows, chan)
        back = (norm_back(grad_y * gain_two[...], normed) * scale).astype(BF16)
        d_out[rows, :] = back
        sums[0] += fold_rows(back.astype(F32))
        sums[1] += fold_rows(grad_y * normed)
        sums[2] += fold_rows(grad_y)

    each_tile(rows_dev, second_norm, 2)
    y_copy = pltpu.make_async_copy(y_low, y_hbm, sem)
    y_copy.start()

    def go_down(rows, win, begin):
        for number, at in enumerate(range(0, hid_width, COLS)):
            cols = slice(at, at + COLS)
            d_act = contract_cols(d_out[rows, :], w_out[cols, :])
            back = (d_act * hid_slope[rows, cols]).astype(BF16)
            d_up[rows, cols] = back
            sums[3 + number] += fold_rows(back.astype(F32))

    each_tile(rows_dev, go_down, 2)
    for number in range(8):
        small[number : number + 1, :] = one_row(sums[number])
    core = mine[0]
    out_block = hid_width >> (dp_bits + 1)
    in_block = chan >> (dp_bits + 1)
    chunks = hid_width // COLS
    half = (out_block + chunks * in_block) // 2

    def hand_out(spot, first_row, block, targets):
        for start in range(0, result.shape[1], 4 * block):
            owner_at = first_row // block + start // block
            for tap in range(2):
                owner = {bit: (owner_at >> (bit + 1)) & 1 for bit in range(1, dp_bits)}
                owner["t"] = tap
                inner = start + tap * block
                for part_at, source, size, shift in targets:
                    spread = relative(orders[part_at], owner, mine) + (part_at << dp_bits)
                    place = rows_at(spread * half + shift, size)
                    mine_at = rows_at(inner + source + core * 2 * block, size)
                    other_at = rows_at(inner + source + (1 - core) * 2 * block, size)
                    keep[place, :] = result[spot, mine_at, :]
                    send[place, :] = result[spot, other_at, :].astype(BF16)

    size = out_block // 2

    @pl.loop(0, chunks // 2)
    def _(pair):
        for spot in range(2):
            at = pl.multiple_of((pair * 2 + spot) * COLS, COLS)
            result[spot] = contract_rows(act[:, pl.ds(at, COLS)], d_out[...])
            hand_out(spot, at, out_block, [(0, 0, size, 0), (1, size, size, 0)])

    @pl.loop(0, chunks // 2)
    def _(step):
        shift = size + step * in_block
        for spot in range(2):
            at = pl.multiple_of((spot * (chunks // 2) + step) * COLS, COLS)
            result[spot] = contract_rows(low[...], d_up[:, pl.ds(at, COLS)])
            hand_out(spot, 0, in_block, [(spot, 0, in_block, shift)])

    y_copy.wait()


def back_kernel(
    species,
    counts,
    grad_in,
    w_in,
    d_up,
    unit,
    slope,
    gain_one,
    small_in,
    d_pad,
    d_hidden,
    small,
    sums,
):
    windows = d_pad.shape[0]
    chan = d_hidden.shape[1]
    clear_pads(d_pad)
    sums[...] = jnp.zeros(sums.shape, F32)

    def through_norm(rows, win, begin):
        grad = grad_in[rows, :].astype(F32) * window_weight(species, counts, win, windows, chan)
        grad = grad + contract_cols(d_up[rows, :], w_in[...])
        d_hidden[rows, :] = grad
        normed = unit[rows, :]
        back = (norm_back(grad * gain_one[...], normed) * slope[rows, :]).astype(BF16)
        d_pad[win, rows_at(PAD + begin, TILE), :] = back
        sums[0] += fold_rows(back.astype(F32))
        sums[1] += fold_rows(grad * normed)
        sums[2] += fold_rows(grad)

    each_tile(d_hidden.shape[0], through_norm, 2)
    small[0:8, :] = small_in[...]
    for number in range(8):
        small[8 + number : 9 + number, :] = one_row(sums[number])


def store_small(total, ref, first):
    count = total.shape[0]
    high = total.astype(BF16)
    ref[first : first + count, :] = high
    ref[first + count : first + 2 * count, :] = (total - high.astype(F32)).astype(BF16)


def load_small(ref, first, count):
    high = ref[first : first + count, :].astype(F32)
    return high + ref[first + count : first + 2 * count, :].astype(F32)


def terms_kernel(slots, orders, dp_bits, with_small, own_table, other_table, x_pad, d_pad, *refs):
    if with_small:
        small, _, keep, send, result = refs
        store_small(small[...], send, keep.shape[0])
    else:
        weight_hbm, _, keep, send, weight, result, sem = refs
        copies = [
            pltpu.make_async_copy(weight_hbm.at[slot], weight.at[slot], sem.at[slot])
            for slot in range(weight.shape[0])
        ]
        for copy in copies:
            copy.start()
    mine = my_bits(dp_bits)
    rows = x_pad.shape[2] >> dp_bits
    core = mine[0]
    tables = (own_table, other_table)
    size = rows // 2

    @pl.loop(0, len(slots))
    def _(number):
        for near_tap in range(2):
            tap = tables[near_tap][slots[0] + number]
            shifted = rows_at((KERNEL_TAPS - 1 - tap) * DILATION_STEP, WINDOW_LENGTH)
            total = None
            for win in range(x_pad.shape[0]):
                term = contract_rows(
                    x_pad[win, PAD : PAD + WINDOW_LENGTH, :], d_pad[win, shifted, :]
                )
                total = term if total is None else total + term
            result[near_tap] = total
            for start in range(0, x_pad.shape[2], 2 * rows):
                owner_at = start // rows
                owner = {bit: (owner_at >> bit) & 1 for bit in range(1, dp_bits)}
                owner["t"] = mine["t"] ^ near_tap
                for part_at in range(2):
                    spread = relative(orders[part_at], owner, mine) + (part_at << dp_bits)
                    place = rows_at((spread * len(slots) + number) * size, size)
                    mine_at = rows_at(start + core * rows + part_at * size, size)
                    other_at = rows_at(start + (1 - core) * rows + part_at * size, size)
                    keep[place, :] = result[near_tap, mine_at, :]
                    send[place, :] = result[near_tap, other_at, :].astype(BF16)

    if not with_small:
        wait_all(copies)


def input_sum(table, d_pad, base, weight, rows, win, begin):
    total = base[rows, :]
    for slot in range(weight.shape[0]):
        shifted = rows_at((KERNEL_TAPS - 1 - table[slot]) * DILATION_STEP + begin, TILE)
        total = total + contract_cols(d_pad[win, shifted, :], weight[slot])
    return total


def input_near_kernel(table, d_pad, base, weight, _, out):
    def gather(rows, win, begin):
        out[rows, :] = input_sum(table, d_pad, base, weight, rows, win, begin)

    each_tile(out.shape[0], gather, 2)


def input_far_kernel(table, d_pad, base, weight, _, out_hbm, token, out, sems):
    token[...] = jnp.zeros(token.shape, token.dtype)

    def copy_of(rows):
        return pltpu.make_async_copy(out.at[rows, :], out_hbm.at[rows, :], sems.at[0])

    def gather(rows, win, begin):
        out[rows, :] = input_sum(table, d_pad, base, weight, rows, win, begin)
        copy_of(rows).start()

    each_tile(out.shape[0], gather, 2)
    pltpu.make_async_copy(out, out_hbm, sems.at[0]).wait()


def step_kernel(joined_in, joined_out, with_small, *refs):
    gots = refs[: 2 - joined_in]
    keep = refs[2 - joined_in]
    outs = refs[4 - joined_in + with_small :]
    rows = keep.shape[0] // 2
    half = rows // 2
    for part in range(2):
        got = gots[0 if joined_in else part]
        base = part * rows if joined_in else 0
        start = part * rows
        sent = keep[start + half : start + rows, :] + got[base + half : base + rows, :].astype(F32)
        if joined_out:
            outs[1][part * half : (part + 1) * half, :] = sent.astype(BF16)
        else:
            outs[1 + part][0:half, :] = sent.astype(BF16)
        kept = keep[start : start + half, :] + got[base : base + half, :].astype(F32)
        outs[0][part * half : (part + 1) * half, :] = kept
    if with_small:
        small = refs[3 - joined_in]
        total = small[...] + load_small(gots[0], rows * (1 + joined_in), small.shape[0])
        outs[3 - joined_out][...] = total
        store_small(total, outs[1], half * (1 + joined_out))


def sum_of(gots, keep, rows):
    total = keep[rows, :]
    for got in gots:
        total = total + got[rows, :].astype(F32)
    return total


def last_ffn_kernel(members, *refs):
    gots = refs[:members]
    keep, _, w_in_out, w_out_out = refs[members:]
    out_rows, chan = w_out_out.shape
    in_rows = w_in_out.shape[0]
    half = keep.shape[0] // 2
    steps = w_in_out.shape[1] // chan // 2
    for part in range(2):
        base = part * half
        size = out_rows // 2
        w_out_out[part * size : (part + 1) * size, :] = sum_of(gots, keep, slice(base, base + size))
        for step in range(steps):
            at = base + size + step * in_rows
            cols = slice((part * steps + step) * chan, (part * steps + step + 1) * chan)
            w_in_out[:, cols] = sum_of(gots, keep, slice(at, at + in_rows))


def last_small_kernel(got, keep, small, _, out, next_small):
    rows = out.shape[0]
    out[...] = keep[...] + got[0:rows, :].astype(F32)
    next_small[...] = small[...] + load_small(got, rows, small.shape[0])


def last_conv_kernel(got, keep, done, out):
    size = out.shape[1] // 2
    first = done.shape[0] // out.shape[1]
    rest = out.shape[0] - first
    for slot in range(out.shape[0]):
        for part in range(2):
            place = slice(part * size, (part + 1) * size)
            if slot < first:
                at = (part * first + slot) * size
                out[slot, place, :] = done[at : at + size, :]
            else:
                at = (part * rest + slot - first) * size
                out[slot, place, :] = keep[at : at + size, :] + got[at : at + size, :].astype(F32)


def params(mib):
    return pltpu.CompilerParams(vmem_limit_bytes=mib * MIB)


def claim(micros):
    return pl.CostEstimate(flops=int(micros * 1.1e9), bytes_accessed=1, transcendentals=0)


def after_kernel(_, token, out):
    del token, out


def after(value, token, claimed=0):
    return pl.pallas_call(
        after_kernel,
        out_shape=pltpu.VMEM(value.shape, value.dtype),
        in_specs=[VMEM] * 2,
        out_specs=VMEM,
        input_output_aliases={0: 0},
        compiler_params=params(4),
        cost_estimate=claim(claimed),
        name="after",
    )(near(value), near(token))


def far(value):
    return pltpu.with_memory_space_constraint(value, pltpu.HBM)


def near(value):
    return pltpu.with_memory_space_constraint(value, pltpu.VMEM)


def step(gots, keep, joined_out, token, small=None):
    lanes = keep.shape[1]
    half = keep.shape[0] // 4
    extra = 0 if small is None else 2 * small.shape[0]
    sent = [2 * half + extra] if joined_out else [half + extra, half]
    outs = [pltpu.VMEM((2 * half, lanes), F32)]
    outs += [pltpu.VMEM((rows, lanes), BF16) for rows in sent]
    operands = [near(got) for got in gots] + [near(keep)]
    if small is not None:
        outs.append(pltpu.VMEM(small.shape, F32))
        operands.append(near(small))
    out = pl.pallas_call(
        functools.partial(step_kernel, len(gots) == 1, joined_out, small is not None),
        out_shape=outs,
        in_specs=[VMEM] * (len(operands) + 1),
        out_specs=[VMEM] * len(outs),
        compiler_params=params(4),
        cost_estimate=claim(0),
        name="step",
    )(*operands, near(token))
    if small is None:
        return out[0], out[1:], None
    return out[0], out[1:-1], out[-1]


def swap(value, mask):
    count = lax.axis_size("dp") * lax.axis_size("tap")
    return lax.ppermute(value, ("dp", "tap"), [(i, i ^ mask) for i in range(count)])


def cut_kernel(table, weight_hbm, shared, direct, sems):
    slots = shared.shape[0]
    rows = (direct.shape[0] - TABLE_ROWS) // slots
    place = lax.axis_index("dp")
    start = 2 * rows + (place & 7) * shared.shape[1]
    near_start = (place & 1) * rows
    copies = []
    for slot in range(slots):
        pair = (
            (weight_hbm.at[slot, rows_at(start, shared.shape[1]), :], shared.at[slot]),
            (
                weight_hbm.at[slot, rows_at(near_start, rows), :],
                direct.at[slot * rows : (slot + 1) * rows, :],
            ),
        )
        for source, target in pair:
            copies.append(pltpu.make_async_copy(source, target, sems.at[len(copies)]))
    for copy in copies:
        copy.start()
    at = lax.broadcasted_iota(jnp.int32, (TABLE_ROWS, direct.shape[1]), 0)
    taps = jnp.zeros(at.shape, jnp.int32)
    for slot in range(slots):
        taps = jnp.where(at == slot, table[slot], taps)
    direct[slots * rows :, :] = taps.astype(F32).astype(BF16)
    for copy in copies:
        copy.wait()


def cut_pieces(table, conv_weight):
    slots, chan, width = conv_weight.shape
    direct, shared = fetch_plan(chan)
    return pl.pallas_call(
        cut_kernel,
        out_shape=[
            pltpu.VMEM((slots, shared, width), BF16),
            pltpu.VMEM((slots * direct + TABLE_ROWS, width), BF16),
        ],
        in_specs=[SMEM, HBM],
        out_specs=[VMEM] * 2,
        scratch_shapes=[pltpu.SemaphoreType.DMA((2 * slots,))],
        compiler_params=params(4),
        cost_estimate=claim(0),
        name="cut_pieces",
    )(table, far(conv_weight))


def pick_kernel(over_one, over_two, _, low, high, both):
    slots = over_one.shape[0]
    low[...] = over_two[0 : low.shape[0]]
    high[...] = over_one[low.shape[0] :]
    both[0:slots] = over_one[...]
    both[slots:] = over_two[...]


def pair_up_kernel(low, high, both):
    both[0 : low.shape[0]] = low[...]
    both[low.shape[0] :] = high[...]


def vmem_call(kernel, shapes, operands, name):
    return pl.pallas_call(
        kernel,
        out_shape=[pltpu.VMEM(shape, BF16) for shape in shapes],
        in_specs=[VMEM] * len(operands),
        out_specs=[VMEM] * len(shapes),
        compiler_params=params(4),
        cost_estimate=claim(0),
        name=name,
    )(*[near(operand) for operand in operands])


def fetch_pieces(first, direct, token):
    over_one = swap_dp(first, 1)
    over_two = swap_dp(first, 2)
    straight = swap_tap(after(direct, first))
    slots = first.shape[0]
    cut = (slots + 1) // 2
    rest = first.shape[1:]
    shapes = [(count,) + rest for count in (cut, slots - cut, 2 * slots)]
    low, high, both = vmem_call(pick_kernel, shapes, [over_one, over_two, token], "pick")
    (last,) = vmem_call(
        pair_up_kernel, [first.shape], [swap_dp(low, 1), swap_dp(high, 2)], "pair_up"
    )
    straight = after(straight, low)
    both_mate = swap_dp(both, 0)
    return [
        ((0, 0), first),
        ((2, 4), both),
        ((0, None), straight),
        ((6, 0), last),
        ((1, 0), swap_dp(first, 0)),
        ((3, 5), both_mate),
        ((1, None), swap_dp(straight, 0)),
        ((7, 0), swap_dp(last, 0)),
    ]


def fast_shards(
    block_input,
    conv_weight,
    slot_tap_table,
    conv_bias,
    conv_norm_gain,
    conv_norm_bias,
    w_in,
    b_in,
    w_out,
    b_out,
    ffn_norm_gain,
    ffn_norm_bias,
    species_id,
    species_count,
    out_grad,
):
    tap_count = lax.axis_size("tap")
    dp_bits = (lax.axis_size("dp") - 1).bit_length()
    rows_dev = block_input.shape[0] // tap_count
    chan = block_input.shape[1]
    hid = w_in.shape[1]
    windows = rows_dev // WINDOW_LENGTH
    slots = conv_weight.shape[0]
    vmem = pltpu.VMEM
    line = list(range(2, dp_bits))
    orders = (["t", 1] + line, [1, "t"] + line)
    over_x, over_y = 1, 4
    pad_shape = (windows, WINDOW_LENGTH + 2 * PAD, chan)
    rows_f = (rows_dev, chan)
    small_cost = claim(0)

    def row(vector):
        return vector.reshape(1, -1)

    shared, direct = cut_pieces(slot_tap_table, conv_weight)
    weight_shape = conv_weight.shape
    tiles = rows_dev // TILE
    dma = pltpu.SemaphoreType.DMA
    first = swap_tap(shared)
    x_pad, part, token = pl.pallas_call(
        own_conv_kernel,
        out_shape=[vmem(pad_shape, BF16), vmem(rows_f, F32), vmem((8, 128), F32)],
        in_specs=[SMEM] + [HBM] * 2 + [VMEM],
        out_specs=[VMEM] * 3,
        scratch_shapes=[vmem(weight_shape, BF16), dma((windows + slots,))],
        compiler_params=params(8),
        cost_estimate=claim(0),
        name="own_conv",
    )(slot_tap_table, far(block_input), far(conv_weight), near(first))
    pieces = fetch_pieces(first, direct, token)

    block_f = (hid + chan * hid // COLS) >> (dp_bits + 1)
    half_f = block_f << dp_bits
    main = pl.pallas_call(
        functools.partial(main_kernel, orders, dp_bits, [turn for turn, _ in pieces]),
        out_shape=[
            pltpu.HBM(rows_f, BF16),
            vmem(rows_f, F32),
            vmem(rows_f, F32),
            vmem((rows_dev, hid), BF16),
            vmem(conv_weight.shape, BF16),
            vmem((half_f, chan), F32),
            vmem((half_f, chan), BF16),
            vmem((8, chan), F32),
            vmem(rows_f, BF16),
            vmem(w_in.shape, BF16),
            jax.ShapeDtypeStruct((slots,), jnp.int32),
        ],
        in_specs=[SMEM] * 2 + [VMEM] * 2 + [HBM] * 3 + [VMEM] * (7 + len(pieces)),
        out_specs=[HBM] + [VMEM] * 9 + [SMEM],
        scratch_shapes=[
            vmem(w_out.shape, BF16),
            vmem(rows_f, F32),
            vmem(rows_f, BF16),
            vmem((rows_dev, hid), BF16),
            vmem((rows_dev, hid), F32),
            vmem(rows_f, BF16),
            vmem(rows_f, BF16),
            vmem((2, COLS, chan), F32),
            vmem((8, 8, chan), F32),
            dma,
            dma((12,)),
        ],
        compiler_params=params(34),
        cost_estimate=small_cost,
        name="main_rows",
    )(
        species_id,
        species_count,
        near(x_pad),
        near(part),
        far(out_grad),
        far(w_in),
        far(w_out),
        row(conv_bias),
        row(conv_norm_gain),
        row(conv_norm_bias),
        row(b_in),
        row(b_out),
        row(ffn_norm_gain),
        row(ffn_norm_bias),
        *[near(piece) for _, piece in pieces],
    )
    block_output, unit, slope, d_up, other_weight, keep_f, send_f, small_ffn = main[:8]
    grad_in, w_in_near, other_table = main[8:]
    got_f = swap_dp(send_f, 0)

    d_pad, d_hidden, small = pl.pallas_call(
        back_kernel,
        out_shape=[vmem(pad_shape, BF16), vmem(rows_f, F32), vmem((16, chan), F32)],
        in_specs=[SMEM] * 2 + [VMEM] * 7,
        out_specs=[VMEM] * 3,
        scratch_shapes=[vmem((8, 8, chan), F32)],
        compiler_params=params(8),
        cost_estimate=small_cost,
        name="back_rows",
    )(
        species_id,
        species_count,
        near(grad_in),
        near(w_in_near),
        near(d_up),
        near(unit),
        near(slope),
        row(conv_norm_gain),
        near(small_ffn),
    )
    keep_f, sends_f, _ = step([got_f], keep_f, False, small)
    gots_f = [swap(sends_f[0], over_x), swap(sends_f[1], over_y)]

    def terms(group, token, small, name):
        count = len(group) * chan
        extra = 0 if small is None else 2 * small.shape[0]
        outs = [vmem((count, chan), F32), vmem((count + extra, chan), BF16)]
        scratch = [vmem((2, chan, chan), F32)]
        if small is None:
            last, last_spec = far(conv_weight), HBM
            outs.append(vmem(weight_shape, BF16))
            scratch.append(dma((slots,)))
        else:
            last, last_spec = near(small), VMEM
        return pl.pallas_call(
            functools.partial(terms_kernel, group, orders, dp_bits, small is not None),
            out_shape=outs,
            in_specs=[SMEM] * 2 + [VMEM] * 2 + [last_spec, VMEM],
            out_specs=[VMEM] * len(outs),
            scratch_shapes=scratch,
            compiler_params=params(8),
            cost_estimate=small_cost,
            name=name,
        )(slot_tap_table, other_table, near(x_pad), near(d_pad), last, near(token))

    cut = (slots * 3 + 4) // 5
    keep_a, send_a = terms(range(0, cut), sends_f[0], small, "terms_a")
    got_a = swap_dp(send_a, 0)
    keep_b, send_b, own_weight = terms(range(cut, slots), keep_a, None, "terms_b")
    got_b = swap_dp(send_b, 0)
    def spaced(token, claimed=1):
        return after(mark, token, claimed)

    def turned(sends):
        return [swap(sends[0], over_y), swap(sends[1], over_x)]

    def along(sends, stage):
        return [swap(sends[0], 2 << line[stage])]

    mark = token
    keep_f, sends_f, _ = step(gots_f, keep_f, False, keep_b)
    gots_f = turned(sends_f)
    keep_a, sends_a, small = step([got_a], keep_a, False, spaced(keep_f, 100), small)
    gots_a = [swap(sends_a[0], over_x), swap(sends_a[1], over_y)]
    partial = pl.pallas_call(
        input_near_kernel,
        out_shape=vmem(rows_f, F32),
        in_specs=[SMEM] + [VMEM] * 4,
        out_specs=VMEM,
        compiler_params=params(8),
        cost_estimate=claim(0),
        name="input_near",
    )(slot_tap_table, near(d_pad), near(d_hidden), near(own_weight), near(keep_a))
    input_grad, mark = pl.pallas_call(
        input_far_kernel,
        out_shape=[pltpu.HBM(rows_f, F32), vmem((8, 128), F32)],
        in_specs=[SMEM] + [VMEM] * 4,
        out_specs=[HBM, VMEM],
        scratch_shapes=[vmem(rows_f, F32), pltpu.SemaphoreType.DMA((rows_dev // TILE,))],
        compiler_params=params(8),
        cost_estimate=small_cost,
        name="input_far",
    )(other_table, near(d_pad), near(partial), near(other_weight), near(keep_a))
    mark = spaced(mark)
    keep_f, sends_f, _ = step(gots_f, keep_f, True, mark)
    got_f = along(sends_f, 0)
    keep_b, sends_b, _ = step([got_b], keep_b, False, keep_f)
    gots_b = [swap(sends_b[0], over_x), swap(sends_b[1], over_y)]
    mark = spaced(keep_b)
    keep_a, sends_a, small = step(gots_a, keep_a, False, mark, small)
    gots_a = turned(sends_a)
    mark = spaced(keep_a)
    for stage in range(1, len(line)):
        keep_f, sends_f, _ = step(got_f, keep_f, True, mark)
        got_f = along(sends_f, stage)
        mark = spaced(keep_f)
    keep_b, sends_b, _ = step(gots_b, keep_b, False, mark)
    gots_b = turned(sends_b)
    mark = spaced(keep_b)
    keep_a, sends_a, small = step(gots_a, keep_a, True, mark, small)
    got_a = along(sends_a, 0)
    mark = spaced(keep_a)
    w_in_mine, w_out_mine = pl.pallas_call(
        functools.partial(last_ffn_kernel, 1),
        out_shape=[
            jax.ShapeDtypeStruct((chan >> (dp_bits + 1), hid), F32),
            jax.ShapeDtypeStruct((hid >> (dp_bits + 1), chan), F32),
        ],
        in_specs=[VMEM] * 3,
        out_specs=[VMEM] * 2,
        compiler_params=params(4),
        cost_estimate=claim(0),
        name="last_ffn",
    )(near(got_f[0]), near(keep_f), near(mark))
    keep_b, sends_b, _ = step(gots_b, keep_b, True, mark)
    got_b = along(sends_b, 0)
    mark = spaced(keep_b)
    for stage in range(1, len(line)):
        keep_a, sends_a, small = step(got_a, keep_a, True, mark, small)
        got_a = along(sends_a, stage)
        mark = spaced(keep_a)
        keep_b, sends_b, _ = step(got_b, keep_b, True, mark)
        got_b = along(sends_b, stage)
        mark = spaced(keep_b)
    part_a, small = pl.pallas_call(
        last_small_kernel,
        out_shape=[vmem(keep_a.shape, F32), vmem(small.shape, F32)],
        in_specs=[VMEM] * 4,
        out_specs=[VMEM] * 2,
        compiler_params=params(4),
        cost_estimate=claim(0),
        name="last_a",
    )(near(got_a[0]), near(keep_a), near(small), near(mark))
    conv_weight_grad = pl.pallas_call(
        last_conv_kernel,
        out_shape=jax.ShapeDtypeStruct((slots, chan >> dp_bits, chan), F32),
        in_specs=[VMEM] * 3,
        out_specs=VMEM,
        compiler_params=params(4),
        cost_estimate=claim(0),
        name="last_conv",
    )(near(got_b[0]), near(keep_b), near(part_a))
    chunks = hid // COLS

    owner = lax.axis_index("dp") * tap_count + lax.axis_index("tap")
    width = chan >> (dp_bits + 1)
    lanes = lax.dynamic_slice(small, (0, owner * width), (small.shape[0], width))
    wide = hid >> (dp_bits + 1)
    d_b_in = lax.dynamic_slice(small[3 : 3 + chunks].reshape(-1), (owner * wide,), (wide,))
    return (
        block_output,
        input_grad,
        conv_weight_grad,
        lanes[8],
        lanes[9],
        lanes[10],
        w_in_mine,
        d_b_in,
        w_out_mine,
        lanes[0],
        lanes[1],
        lanes[2],
    )


def narrow_enough(mesh):
    return mesh.shape["tap"] == 2 and mesh.shape["dp"] == 16


def solution(mesh):
    chosen = fast_shards if narrow_enough(mesh) else plain_shards
    return jax.shard_map(
        chosen,
        mesh=mesh,
        in_specs=(
            P("dp", None),
            P("tap", None, None),
            P("tap"),
            P(),
            P(),
            P(),
            P(),
            P(),
            P(),
            P(),
            P(),
            P(),
            P("dp"),
            P(),
            P(("dp", "tap"), None),
        ),
        out_specs=(
            P(("dp", "tap"), None),
            P(("dp", "tap"), None),
            P("tap", "dp", None),
            P(("dp", "tap")),
            P(("dp", "tap")),
            P(("dp", "tap")),
            P(("dp", "tap"), None),
            P(("dp", "tap")),
            P(("dp", "tap"), None),
            P(("dp", "tap")),
            P(("dp", "tap")),
            P(("dp", "tap")),
        ),
        check_vma=False,
    )
```

profile of v0, /device:TPU:0, one launch (start us, length us, event | category | flops | bytes accessed | tf_op | source)
XLA Modules:
  0.0 122.0 jit_solution(1692979062282137274)
XLA Ops:
  1.3 1.7 %cut_pieces.1 = (bf16[5,48,512]{2,1,0:T(8,128)(2,1)S(1)}, bf16[336,512]{1,0:T(8,128)(2,1)S(1)}) custom-call(s32[5]{0:T(128)S(1)} %copy-done, bf16[5,512,512]{2,1,0:T(8,128)(2,1)} %refs_0_.3), custom_call_target="tpu_custom_call" | custom-call | bytes 1 | tf_op jit(solution)/shard_map/cut_pieces/pallas_call | solution.py:807
  3.0 3.0 %collective-permute-start = (bf16[5,48,512]{2,1,0:T(8,128)(2,1)S(1)}, bf16[5,48,512]{2,1,0:T(8,128)(2,1)S(1)}, u32[]{:S(2)}, u32[]{:S(2)}) collective-permute-start(bf16[5,48,512]{2,1,0:T(8,128)(2,1)S(1)} %get-tuple-element.79), channel_id=1, source_target_pairs={{0,1},{1,0},{2,3},{3,2},{4,5},{5,4},{6,7},{7,6},{8,9},{9,8},{10,11... | collective-permute-start | bytes 737288 | tf_op jit(solution)/shard_map/ppermute | solution.py:68
  6.0 6.0 %collective-permute-done._.token.refs_14_ = bf16[5,48,512]{2,1,0:T(8,128)(2,1)S(1)} collective-permute-done((bf16[5,48,512]{2,1,0:T(8,128)(2,1)S(1)}, bf16[5,48,512]{2,1,0:T(8,128)(2,1)S(1)}, u32[]{:S(2)}, u32[]{:S(2)}) %collective-permute-start) | collective-permute-done | bytes 245792 | tf_op jit(solution)/shard_map/ppermute | solution.py:68
  12.0 1.8 %collective-permute-start.1 = (bf16[5,48,512]{2,1,0:T(8,128)(2,1)S(1)}, bf16[5,48,512]{2,1,0:T(8,128)(2,1)S(1)}, u32[]{:S(2)}, u32[]{:S(2)}) collective-permute-start(bf16[5,48,512]{2,1,0:T(8,128)(2,1)S(1)} %collective-permute-done._.token.refs_14_), channel_id=1, source_target_pairs={{0,4},{2,6},{4,0},{6,2},{8,12},{10,14},{12,8},{14,10},{16,20},{18,... | collective-permute-start | bytes 737288 | tf_op jit(solution)/shard_map/ppermute | solution.py:64
  13.8 1.6 %collective-permute-start.2 = (bf16[5,48,512]{2,1,0:T(8,128)(2,1)S(1)}, bf16[5,48,512]{2,1,0:T(8,128)(2,1)S(1)}, u32[]{:S(2)}, u32[]{:S(2)}) collective-permute-start(bf16[5,48,512]{2,1,0:T(8,128)(2,1)S(1)} %collective-permute-done._.token.refs_14_), channel_id=1, source_target_pairs={{0,8},{2,10},{4,12},{6,14},{8,0},{10,2},{12,4},{14,6},{16,24},{18,... | collective-permute-start | bytes 737288 | tf_op jit(solution)/shard_map/ppermute | solution.py:64
  15.3 1.5 %collective-permute-start.3 = (bf16[336,512]{1,0:T(8,128)(2,1)S(1)}, bf16[336,512]{1,0:T(8,128)(2,1)S(1)}, u32[]{:S(2)}, u32[]{:S(2)}) collective-permute-start(bf16[336,512]{1,0:T(8,128)(2,1)S(1)} %after.12), channel_id=1, source_target_pairs={{0,1},{1,0},{2,3},{3,2},{4,5},{5,4},{6,7},{7,6},{8,9},{9,8},{10,11... | collective-permute-start | bytes 1032200 | tf_op jit(solution)/shard_map/ppermute | solution.py:68
  16.8 5.6 %own_conv.1 = (bf16[2,640,512]{2,1,0:T(8,128)(2,1)S(1)}, f32[1024,512]{1,0:T(8,128)S(1)}, f32[8,128]{1,0:T(8,128)S(1)}) custom-call(s32[5]{0:T(128)S(1)} %copy-done.1, bf16[2048,512]{1,0:T(8,128)(2,1)} %x_hbm.1, bf16[5,512,512]{2,1,0:T(8,128)(2,1)} %refs_0_.3, bf16[5,48,512]{2,1,0:T(8,128)(2,1)S(1)} %collective-permute-done._.token.refs_14_), custom_call_target="tpu_custom_call" | custom-call | bytes 1 | tf_op jit(solution)/shard_map/own_conv/pallas_call | solution.py:913
  24.2 3.8 %collective-permute-done.5.high = bf16[2,48,512]{2,1,0:T(8,128)(2,1)S(1)} collective-permute-done((bf16[2,48,512]{2,1,0:T(8,128)(2,1)S(1)}, bf16[2,48,512]{2,1,0:T(8,128)(2,1)S(1)}, u32[]{:S(2)}, u32[]{:S(2)}) %collective-permute-start.5) | collective-permute-done | bytes 98336 | tf_op jit(solution)/shard_map/ppermute | solution.py:64
  29.0 1.5 %collective-permute-done.9.refs_21_ = bf16[5,48,512]{2,1,0:T(8,128)(2,1)S(1)} collective-permute-done((bf16[5,48,512]{2,1,0:T(8,128)(2,1)S(1)}, bf16[5,48,512]{2,1,0:T(8,128)(2,1)S(1)}, u32[]{:S(2)}, u32[]{:S(2)}) %collective-permute-start.9) | collective-permute-done | bytes 245792 | tf_op jit(solution)/shard_map/ppermute | solution.py:64
  30.5 23.4 %main_rows.1 = (bf16[1024,512]{1,0:T(8,128)(2,1)}, f32[1024,512]{1,0:T(8,128)S(1)}, f32[1024,512]{1,0:T(8,128)S(1)}, bf16[1024,2048]{1,0:T(8,128)(2,1)S(1)}, bf1...) custom-call(s32[4]{0:T(128)} %species.1, ...), custom_call_target="tpu_custom_call" | custom-call | bytes 1 | tf_op jit(solution)/shard_map/main_rows/pallas_call | solution.py:927
  54.2 4.3 %back_rows.1 = (bf16[2,640,512]{2,1,0:T(8,128)(2,1)S(1)}, f32[1024,512]{1,0:T(8,128)S(1)}, f32[16,512]{1,0:T(8,128)S(1)}) custom-call(s32[4]{0:T(128)S(1)} %copy-done.4, s32[16]{0:T(128)S(1)} %copy-done.5, bf16[1024,512]{1,0:T(8,128)(2,1)S(1)} %get-tuple-element.89.grad_in, bf16[512,2048]{1,0:T(8,128)(2,1)S(1)} %get-tuple-element.90.w_in, ...), custom_call_target="tpu_custom_call" | custom-call | bytes 1 | tf_op jit(solution)/shard_map/back_rows/pallas_call | solution.py:981
  60.2 5.1 %terms_a.1 = (f32[1536,512]{1,0:T(8,128)S(1)}, bf16[1568,512]{1,0:T(8,128)(2,1)S(1)}) custom-call(s32[5]{0:T(128)S(1)} %copy-done.1, s32[5]{0:T(128)S(1)} %copy-done.3, bf16[2,640,512]{2,1,0:T(8,128)(2,1)S(1)} %get-tuple-element.80.refs_2_.x_pad, bf16[2,640,512]{2,1,0:T(8,128)(2,1)S(1)} %get-tuple-element.95.d_pad, ...), custom_call_target="tpu_custom_call" | custom-call | bytes 1 | tf_op jit(solution)/shard_map/terms_a/pallas_call | solution.py:1015
  65.3 3.7 %terms_b.1 = (f32[1024,512]{1,0:T(8,128)S(1)}, bf16[1024,512]{1,0:T(8,128)(2,1)S(1)}, bf16[5,512,512]{2,1,0:T(8,128)(2,1)S(1)}) custom-call(s32[5]{0:T(128)S(1)} %copy-done.1, s32[5]{0:T(128)S(1)} %copy-done.3, bf16[2,640,512]{2,1,0:T(8,128)(2,1)S(1)} %get-tuple-element.80.refs_2_.x_pad, bf16[2,640,512]{2,1,0:T(8,128)(2,1)S(1)} %get-tuple-element.95.d_pad, ...), custom_call_target="tpu_custom_call" | custom-call | bytes 1 | tf_op jit(solution)/shard_map/terms_b/pallas_call | solution.py:1015
  69.6 3.6 %collective-permute-done.12.refs_0_ = bf16[512,512]{1,0:T(8,128)(2,1)S(1)} collective-permute-done((bf16[512,512]{1,0:T(8,128)(2,1)S(1)}, bf16[512,512]{1,0:T(8,128)(2,1)S(1)}, u32[]{:S(2)}, u32[]{:S(2)}) %collective-permute-start.12) | collective-permute-done | bytes 524320 | tf_op jit(solution)/shard_map/ppermute | solution.py:773
  74.0 1.6 %collective-permute-start.19 = (bf16[416,512]{1,0:T(8,128)(2,1)S(1)}, bf16[416,512]{1,0:T(8,128)(2,1)S(1)}, u32[]{:S(2)}, u32[]{:S(2)}) collective-permute-start(bf16[416,512]{1,0:T(8,128)(2,1)S(1)} %get-tuple-element.119), channel_id=1, source_target_pairs={{0,1},{1,0},{2,3},{3,2},{4,5},{5,4},{6,7},{7,6},{8,9},{9,8},{10,11... | collective-permute-start | bytes 1277960 | tf_op jit(solution)/shard_map/ppermute | solution.py:773
  76.8 1.3 %collective-permute-start.20 = (bf16[384,512]{1,0:T(8,128)(2,1)S(1)}, bf16[384,512]{1,0:T(8,128)(2,1)S(1)}, u32[]{:S(2)}, u32[]{:S(2)}) collective-permute-start(bf16[384,512]{1,0:T(8,128)(2,1)S(1)} %get-tuple-element.120), channel_id=1, source_target_pairs={{0,4},{1,5},{2,6},{3,7},{4,0},{5,1},{6,2},{7,3},{8,12},{9,13},{10,... | collective-permute-start | bytes 1179656 | tf_op jit(solution)/shard_map/ppermute | solution.py:773
  78.1 3.7 %input_near.1.base = f32[1024,512]{1,0:T(8,128)S(1)} custom-call(s32[5]{0:T(128)S(1)} %copy-done.1, bf16[2,640,512]{2,1,0:T(8,128)(2,1)S(1)} %get-tuple-element.95.d_pad, f32[1024,512]{1,0:T(8,128)S(1)} %get-tuple-element.96.base, bf16[5,512,512]{2,1,0:T(8,128)(2,1)S(1)} %get-tuple-element.102.weight, f32[768,512]{1,0:T(8,128)S(1)} %get-tuple-element.108._.refs_2_), custom_call_target="tpu_custom_call" | custom-call | bytes 1 | tf_op jit(solution)/shard_map/input_near/pallas_call | solution.py:1045
  81.8 4.5 %input_far.1 = (f32[1024,512]{1,0:T(8,128)}, f32[8,128]{1,0:T(8,128)S(1)}) custom-call(s32[5]{0:T(128)S(1)} %copy-done.3, bf16[2,640,512]{2,1,0:T(8,128)(2,1)S(1)} %get-tuple-element.95.d_pad, f32[1024,512]{1,0:T(8,128)S(1)} %input_near.1.base, bf16[5,512,512]{2,1,0:T(8,128)(2,1)S(1)} %get-tuple-element.109.weight, f32[768,512]{1,0:T(8,128)S(1)} %get-tuple-element.108._.refs_2_), custom_call_target="tpu_custom_call" | custom-call | bytes 1 | tf_op jit(solution)/shard_map/input_far/pallas_call | solution.py:1054
  86.4 4.4 %collective-permute-done.16.refs_1_ = bf16[256,512]{1,0:T(8,128)(2,1)S(1)} collective-permute-done((bf16[256,512]{1,0:T(8,128)(2,1)S(1)}, bf16[256,512]{1,0:T(8,128)(2,1)S(1)}, u32[]{:S(2)}, u32[]{:S(2)}) %collective-permute-start.16) | collective-permute-done | bytes 262176 | tf_op jit(solution)/shard_map/ppermute | solution.py:773
  91.6 1.5 %collective-permute-start.17 = (bf16[256,512]{1,0:T(8,128)(2,1)S(1)}, bf16[256,512]{1,0:T(8,128)(2,1)S(1)}, u32[]{:S(2)}, u32[]{:S(2)}) collective-permute-start(bf16[256,512]{1,0:T(8,128)(2,1)S(1)} %get-tuple-element.116), channel_id=1, source_target_pairs={{0,1},{1,0},{2,3},{3,2},{4,5},{5,4},{6,7},{7,6},{8,9},{9,8},{10,11... | collective-permute-start | bytes 786440 | tf_op jit(solution)/shard_map/ppermute | solution.py:773
  93.1 1.1 collective-permute-start.18
  95.9 1.6 %collective-permute-done.21.refs_0_ = bf16[256,512]{1,0:T(8,128)(2,1)S(1)} collective-permute-done((bf16[256,512]{1,0:T(8,128)(2,1)S(1)}, bf16[256,512]{1,0:T(8,128)(2,1)S(1)}, u32[]{:S(2)}, u32[]{:S(2)}) %collective-permute-start.21) | collective-permute-done | bytes 262176 | tf_op jit(solution)/shard_map/ppermute | solution.py:773
  97.5 3.7 %collective-permute-start.30 = (bf16[128,512]{1,0:T(8,128)(2,1)S(1)}, bf16[128,512]{1,0:T(8,128)(2,1)S(1)}, u32[]{:S(2)}, u32[]{:S(2)}) collective-permute-start(bf16[128,512]{1,0:T(8,128)(2,1)S(1)} %get-tuple-element.143), channel_id=1, source_target_pairs={{0,16},{1,17},{2,18},{3,19},{4,20},{5,21},{6,22},{7,23},{8,24},{9,... | collective-permute-start | bytes 393224 | tf_op jit(solution)/shard_map/ppermute | solution.py:773
  102.4 1.2 collective-permute-start.22
  103.9 1.4 %collective-permute-done.24.refs_0_ = bf16[224,512]{1,0:T(8,128)(2,1)S(1)} collective-permute-done((bf16[224,512]{1,0:T(8,128)(2,1)S(1)}, bf16[224,512]{1,0:T(8,128)(2,1)S(1)}, u32[]{:S(2)}, u32[]{:S(2)}) %collective-permute-start.24) | collective-permute-done | bytes 229408 | tf_op jit(solution)/shard_map/ppermute | solution.py:773
  105.4 1.6 %collective-permute-start.27 = (bf16[224,512]{1,0:T(8,128)(2,1)S(1)}, bf16[224,512]{1,0:T(8,128)(2,1)S(1)}, u32[]{:S(2)}, u32[]{:S(2)}) collective-permute-start(bf16[224,512]{1,0:T(8,128)(2,1)S(1)} %get-tuple-element.134), channel_id=1, source_target_pairs={{0,8},{1,9},{2,10},{3,11},{4,12},{5,13},{6,14},{7,15},{8,0},{9,1},... | collective-permute-start | bytes 688136 | tf_op jit(solution)/shard_map/ppermute | solution.py:773
  107.5 1.1 collective-permute-done.23.refs_1_
  108.6 1.6 %collective-permute-start.26 = (bf16[128,512]{1,0:T(8,128)(2,1)S(1)}, bf16[128,512]{1,0:T(8,128)(2,1)S(1)}, u32[]{:S(2)}, u32[]{:S(2)}) collective-permute-start(bf16[128,512]{1,0:T(8,128)(2,1)S(1)} %get-tuple-element.132), channel_id=1, source_target_pairs={{0,8},{1,9},{2,10},{3,11},{4,12},{5,13},{6,14},{7,15},{8,0},{9,1},... | collective-permute-start | bytes 393224 | tf_op jit(solution)/shard_map/ppermute | solution.py:773
  111.0 2.0 %collective-permute-done.27.refs_0_ = bf16[224,512]{1,0:T(8,128)(2,1)S(1)} collective-permute-done((bf16[224,512]{1,0:T(8,128)(2,1)S(1)}, bf16[224,512]{1,0:T(8,128)(2,1)S(1)}, u32[]{:S(2)}, u32[]{:S(2)}) %collective-permute-start.27) | collective-permute-done | bytes 229408 | tf_op jit(solution)/shard_map/ppermute | solution.py:773
  113.0 3.0 %collective-permute-start.29 = (bf16[128,512]{1,0:T(8,128)(2,1)S(1)}, bf16[128,512]{1,0:T(8,128)(2,1)S(1)}, u32[]{:S(2)}, u32[]{:S(2)}) collective-permute-start(bf16[128,512]{1,0:T(8,128)(2,1)S(1)} %get-tuple-element.139), channel_id=1, source_target_pairs={{0,16},{1,17},{2,18},{3,19},{4,20},{5,21},{6,22},{7,23},{8,24},{9,... | collective-permute-start | bytes 393224 | tf_op jit(solution)/shard_map/ppermute | solution.py:773
  116.0 1.7 %collective-permute-start.28 = (bf16[64,512]{1,0:T(8,128)(2,1)S(1)}, bf16[64,512]{1,0:T(8,128)(2,1)S(1)}, u32[]{:S(2)}, u32[]{:S(2)}) collective-permute-start(bf16[64,512]{1,0:T(8,128)(2,1)S(1)} %get-tuple-element.137), channel_id=1, source_target_pairs={{0,16},{1,17},{2,18},{3,19},{4,20},{5,21},{6,22},{7,23},{8,24},{9,... | collective-permute-start | bytes 196616 | tf_op jit(solution)/shard_map/ppermute | solution.py:773
  117.7 1.2 %collective-permute-done.29.got = bf16[128,512]{1,0:T(8,128)(2,1)S(1)} collective-permute-done((bf16[128,512]{1,0:T(8,128)(2,1)S(1)}, bf16[128,512]{1,0:T(8,128)(2,1)S(1)}, u32[]{:S(2)}, u32[]{:S(2)}) %collective-permute-start.29) | collective-permute-done | bytes 131104 | tf_op jit(solution)/shard_map/ppermute | solution.py:773
  (84 shorter events, 16.4 us)
Async XLA Ops:
  3.0 9.0 %collective-permute-start = (bf16[5,48,512]{2,1,0:T(8,128)(2,1)S(1)}, bf16[5,48,512]{2,1,0:T(8,128)(2,1)S(1)}, u32[]{:S(2)}, u32[]{:S(2)}) collective-permute-start(bf16[5,48,512]{2,1,0:T(8,128)(2,1)S(1)} %get-tuple-element.79), channel_id=1, source_target_pairs={{0,1},{1,0},{2,3},{3,2},{4,5},{5,4},{6,7},{7,6},{8,9},{9,8},{10,11... | collective-permute-start | bytes 737288 | tf_op jit(solution)/shard_map/ppermute | solution.py:68
  12.0 10.5 %collective-permute-start.1 = (bf16[5,48,512]{2,1,0:T(8,128)(2,1)S(1)}, bf16[5,48,512]{2,1,0:T(8,128)(2,1)S(1)}, u32[]{:S(2)}, u32[]{:S(2)}) collective-permute-start(bf16[5,48,512]{2,1,0:T(8,128)(2,1)S(1)} %collective-permute-done._.token.refs_14_), channel_id=1, source_target_pairs={{0,4},{2,6},{4,0},{6,2},{8,12},{10,14},{12,8},{14,10},{16,20},{18,... | collective-permute-start | bytes 737288 | tf_op jit(solution)/shard_map/ppermute | solution.py:64
  13.8 8.7 %collective-permute-start.2 = (bf16[5,48,512]{2,1,0:T(8,128)(2,1)S(1)}, bf16[5,48,512]{2,1,0:T(8,128)(2,1)S(1)}, u32[]{:S(2)}, u32[]{:S(2)}) collective-permute-start(bf16[5,48,512]{2,1,0:T(8,128)(2,1)S(1)} %collective-permute-done._.token.refs_14_), channel_id=1, source_target_pairs={{0,8},{2,10},{4,12},{6,14},{8,0},{10,2},{12,4},{14,6},{16,24},{18,... | collective-permute-start | bytes 737288 | tf_op jit(solution)/shard_map/ppermute | solution.py:64
  15.3 8.4 %collective-permute-start.3 = (bf16[336,512]{1,0:T(8,128)(2,1)S(1)}, bf16[336,512]{1,0:T(8,128)(2,1)S(1)}, u32[]{:S(2)}, u32[]{:S(2)}) collective-permute-start(bf16[336,512]{1,0:T(8,128)(2,1)S(1)} %after.12), channel_id=1, source_target_pairs={{0,1},{1,0},{2,3},{3,2},{4,5},{5,4},{6,7},{7,6},{8,9},{9,8},{10,11... | collective-permute-start | bytes 1032200 | tf_op jit(solution)/shard_map/ppermute | solution.py:68
  22.6 7.9 %collective-permute-start.7 = (bf16[10,48,512]{2,1,0:T(8,128)(2,1)S(1)}, bf16[10,48,512]{2,1,0:T(8,128)(2,1)S(1)}, u32[]{:S(2)}, u32[]{:S(2)}) collective-permute-start(bf16[10,48,512]{2,1,0:T(8,128)(2,1)S(1)} %get-tuple-element.83.refs_15_), channel_id=1, source_target_pairs={{0,2},{2,0},{4,6},{6,4},{8,10},{10,8},{12,14},{14,12},{16,18},{18,... | collective-permute-start | bytes 1474568 | tf_op jit(solution)/shard_map/ppermute | solution.py:64
  22.6 6.3 %collective-permute-start.4 = (bf16[3,48,512]{2,1,0:T(8,128)(2,1)S(1)}, bf16[3,48,512]{2,1,0:T(8,128)(2,1)S(1)}, u32[]{:S(2)}, u32[]{:S(2)}) collective-permute-start(bf16[3,48,512]{2,1,0:T(8,128)(2,1)S(1)} %get-tuple-element.85.token), channel_id=1, source_target_pairs={{0,4},{2,6},{4,0},{6,2},{8,12},{10,14},{12,8},{14,10},{16,20},{18,... | collective-permute-start | bytes 442376 | tf_op jit(solution)/shard_map/ppermute | solution.py:64
  23.2 4.9 %collective-permute-start.5 = (bf16[2,48,512]{2,1,0:T(8,128)(2,1)S(1)}, bf16[2,48,512]{2,1,0:T(8,128)(2,1)S(1)}, u32[]{:S(2)}, u32[]{:S(2)}) collective-permute-start(bf16[2,48,512]{2,1,0:T(8,128)(2,1)S(1)} %get-tuple-element.86), channel_id=1, source_target_pairs={{0,8},{2,10},{4,12},{6,14},{8,0},{10,2},{12,4},{14,6},{16,24},{18,... | collective-permute-start | bytes 294920 | tf_op jit(solution)/shard_map/ppermute | solution.py:64
  23.7 6.8 %collective-permute-start.8 = (bf16[336,512]{1,0:T(8,128)(2,1)S(1)}, bf16[336,512]{1,0:T(8,128)(2,1)S(1)}, u32[]{:S(2)}, u32[]{:S(2)}) collective-permute-start(bf16[336,512]{1,0:T(8,128)(2,1)S(1)} %after.13.refs_16_), channel_id=1, source_target_pairs={{0,2},{2,0},{4,6},{6,4},{8,10},{10,8},{12,14},{14,12},{16,18},{18,... | collective-permute-start | bytes 1032200 | tf_op jit(solution)/shard_map/ppermute | solution.py:64
  23.7 5.3 %collective-permute-start.6 = (bf16[5,48,512]{2,1,0:T(8,128)(2,1)S(1)}, bf16[5,48,512]{2,1,0:T(8,128)(2,1)S(1)}, u32[]{:S(2)}, u32[]{:S(2)}) collective-permute-start(bf16[5,48,512]{2,1,0:T(8,128)(2,1)S(1)} %collective-permute-done._.token.refs_14_), channel_id=1, source_target_pairs={{0,2},{2,0},{4,6},{6,4},{8,10},{10,8},{12,14},{14,12},{16,18},{18,... | collective-permute-start | bytes 737288 | tf_op jit(solution)/shard_map/ppermute | solution.py:64
  28.9 1.6 %collective-permute-start.9 = (bf16[5,48,512]{2,1,0:T(8,128)(2,1)S(1)}, bf16[5,48,512]{2,1,0:T(8,128)(2,1)S(1)}, u32[]{:S(2)}, u32[]{:S(2)}) collective-permute-start(bf16[5,48,512]{2,1,0:T(8,128)(2,1)S(1)} %pair_up.1.refs_17_), channel_id=1, source_target_pairs={{0,2},{2,0},{4,6},{6,4},{8,10},{10,8},{12,14},{14,12},{16,18},{18,... | collective-permute-start | bytes 737288 | tf_op jit(solution)/shard_map/ppermute | solution.py:64
  30.5 23.6 %copy-start.2 = (f32[512]{0:T(512)S(1)}, f32[512]{0:T(512)}, u32[]{:S(2)}) copy-start(f32[512]{0:T(512)} %param.19) | copy-start | bytes 6148
  53.9 4.5 %collective-permute-start.10 = (bf16[2048,512]{1,0:T(8,128)(2,1)S(1)}, bf16[2048,512]{1,0:T(8,128)(2,1)S(1)}, u32[]{:S(2)}, u32[]{:S(2)}) collective-permute-start(bf16[2048,512]{1,0:T(8,128)(2,1)S(1)} %get-tuple-element.98), channel_id=1, source_target_pairs={{0,2},{2,0},{4,6},{6,4},{8,10},{10,8},{12,14},{14,12},{16,18},{18,... | collective-permute-start | bytes 6291464 | tf_op jit(solution)/shard_map/ppermute | solution.py:64
  58.9 14.2 %collective-permute-start.12 = (bf16[512,512]{1,0:T(8,128)(2,1)S(1)}, bf16[512,512]{1,0:T(8,128)(2,1)S(1)}, u32[]{:S(2)}, u32[]{:S(2)}) collective-permute-start(bf16[512,512]{1,0:T(8,128)(2,1)S(1)} %get-tuple-element.100.refs_1_), channel_id=1, source_target_pairs={{0,1},{1,0},{2,3},{3,2},{4,5},{5,4},{6,7},{7,6},{8,9},{9,8},{10,11... | collective-permute-start | bytes 1572872 | tf_op jit(solution)/shard_map/ppermute | solution.py:773
  59.5 13.9 %collective-permute-start.13 = (bf16[512,512]{1,0:T(8,128)(2,1)S(1)}, bf16[512,512]{1,0:T(8,128)(2,1)S(1)}, u32[]{:S(2)}, u32[]{:S(2)}) collective-permute-start(bf16[512,512]{1,0:T(8,128)(2,1)S(1)} %get-tuple-element.104), channel_id=1, source_target_pairs={{0,4},{1,5},{2,6},{3,7},{4,0},{5,1},{6,2},{7,3},{8,12},{9,13},{10,... | collective-permute-start | bytes 1572872 | tf_op jit(solution)/shard_map/ppermute | solution.py:773
  69.0 4.6 %collective-permute-start.11 = (bf16[1568,512]{1,0:T(8,128)(2,1)S(1)}, bf16[1568,512]{1,0:T(8,128)(2,1)S(1)}, u32[]{:S(2)}, u32[]{:S(2)}) collective-permute-start(bf16[1568,512]{1,0:T(8,128)(2,1)S(1)} %get-tuple-element.103), channel_id=1, source_target_pairs={{0,2},{2,0},{4,6},{6,4},{8,10},{10,8},{12,14},{14,12},{16,18},{18,... | collective-permute-start | bytes 4816904 | tf_op jit(solution)/shard_map/ppermute | solution.py:64
  69.1 22.3 %collective-permute-start.14 = (bf16[1024,512]{1,0:T(8,128)(2,1)S(1)}, bf16[1024,512]{1,0:T(8,128)(2,1)S(1)}, u32[]{:S(2)}, u32[]{:S(2)}) collective-permute-start(bf16[1024,512]{1,0:T(8,128)(2,1)S(1)} %get-tuple-element.111), channel_id=1, source_target_pairs={{0,2},{2,0},{4,6},{6,4},{8,10},{10,8},{12,14},{14,12},{16,18},{18,... | collective-permute-start | bytes 3145736 | tf_op jit(solution)/shard_map/ppermute | solution.py:64
  74.0 20.2 %collective-permute-start.19 = (bf16[416,512]{1,0:T(8,128)(2,1)S(1)}, bf16[416,512]{1,0:T(8,128)(2,1)S(1)}, u32[]{:S(2)}, u32[]{:S(2)}) collective-permute-start(bf16[416,512]{1,0:T(8,128)(2,1)S(1)} %get-tuple-element.119), channel_id=1, source_target_pairs={{0,1},{1,0},{2,3},{3,2},{4,5},{5,4},{6,7},{7,6},{8,9},{9,8},{10,11... | collective-permute-start | bytes 1277960 | tf_op jit(solution)/shard_map/ppermute | solution.py:773
  75.6 10.8 %collective-permute-start.15 = (bf16[256,512]{1,0:T(8,128)(2,1)S(1)}, bf16[256,512]{1,0:T(8,128)(2,1)S(1)}, u32[]{:S(2)}, u32[]{:S(2)}) collective-permute-start(bf16[256,512]{1,0:T(8,128)(2,1)S(1)} %get-tuple-element.112), channel_id=1, source_target_pairs={{0,4},{1,5},{2,6},{3,7},{4,0},{5,1},{6,2},{7,3},{8,12},{9,13},{10,... | collective-permute-start | bytes 786440 | tf_op jit(solution)/shard_map/ppermute | solution.py:773
  76.3 14.5 %collective-permute-start.16 = (bf16[256,512]{1,0:T(8,128)(2,1)S(1)}, bf16[256,512]{1,0:T(8,128)(2,1)S(1)}, u32[]{:S(2)}, u32[]{:S(2)}) collective-permute-start(bf16[256,512]{1,0:T(8,128)(2,1)S(1)} %get-tuple-element.113), channel_id=1, source_target_pairs={{0,1},{1,0},{2,3},{3,2},{4,5},{5,4},{6,7},{7,6},{8,9},{9,8},{10,11... | collective-permute-start | bytes 786440 | tf_op jit(solution)/shard_map/ppermute | solution.py:773
  76.8 17.4 %collective-permute-start.20 = (bf16[384,512]{1,0:T(8,128)(2,1)S(1)}, bf16[384,512]{1,0:T(8,128)(2,1)S(1)}, u32[]{:S(2)}, u32[]{:S(2)}) collective-permute-start(bf16[384,512]{1,0:T(8,128)(2,1)S(1)} %get-tuple-element.120), channel_id=1, source_target_pairs={{0,4},{1,5},{2,6},{3,7},{4,0},{5,1},{6,2},{7,3},{8,12},{9,13},{10,... | collective-permute-start | bytes 1179656 | tf_op jit(solution)/shard_map/ppermute | solution.py:773
  90.8 6.6 %collective-permute-start.21 = (bf16[256,512]{1,0:T(8,128)(2,1)S(1)}, bf16[256,512]{1,0:T(8,128)(2,1)S(1)}, u32[]{:S(2)}, u32[]{:S(2)}) collective-permute-start(bf16[256,512]{1,0:T(8,128)(2,1)S(1)} %get-tuple-element.123), channel_id=1, source_target_pairs={{0,8},{1,9},{2,10},{3,11},{4,12},{5,13},{6,14},{7,15},{8,0},{9,1},... | collective-permute-start | bytes 786440 | tf_op jit(solution)/shard_map/ppermute | solution.py:773
  91.6 9.6 %collective-permute-start.17 = (bf16[256,512]{1,0:T(8,128)(2,1)S(1)}, bf16[256,512]{1,0:T(8,128)(2,1)S(1)}, u32[]{:S(2)}, u32[]{:S(2)}) collective-permute-start(bf16[256,512]{1,0:T(8,128)(2,1)S(1)} %get-tuple-element.116), channel_id=1, source_target_pairs={{0,1},{1,0},{2,3},{3,2},{4,5},{5,4},{6,7},{7,6},{8,9},{9,8},{10,11... | collective-permute-start | bytes 786440 | tf_op jit(solution)/shard_map/ppermute | solution.py:773
  93.1 9.2 %collective-permute-start.18 = (bf16[256,512]{1,0:T(8,128)(2,1)S(1)}, bf16[256,512]{1,0:T(8,128)(2,1)S(1)}, u32[]{:S(2)}, u32[]{:S(2)}) collective-permute-start(bf16[256,512]{1,0:T(8,128)(2,1)S(1)} %get-tuple-element.117), channel_id=1, source_target_pairs={{0,4},{1,5},{2,6},{3,7},{4,0},{5,1},{6,2},{7,3},{8,12},{9,13},{10,... | collective-permute-start | bytes 786440 | tf_op jit(solution)/shard_map/ppermute | solution.py:773
  94.4 11.0 %collective-permute-start.24 = (bf16[224,512]{1,0:T(8,128)(2,1)S(1)}, bf16[224,512]{1,0:T(8,128)(2,1)S(1)}, u32[]{:S(2)}, u32[]{:S(2)}) collective-permute-start(bf16[224,512]{1,0:T(8,128)(2,1)S(1)} %get-tuple-element.128), channel_id=1, source_target_pairs={{0,4},{1,5},{2,6},{3,7},{4,0},{5,1},{6,2},{7,3},{8,12},{9,13},{10,... | collective-permute-start | bytes 688136 | tf_op jit(solution)/shard_map/ppermute | solution.py:773
  95.3 8.6 %collective-permute-start.25 = (bf16[192,512]{1,0:T(8,128)(2,1)S(1)}, bf16[192,512]{1,0:T(8,128)(2,1)S(1)}, u32[]{:S(2)}, u32[]{:S(2)}) collective-permute-start(bf16[192,512]{1,0:T(8,128)(2,1)S(1)} %get-tuple-element.129), channel_id=1, source_target_pairs={{0,1},{1,0},{2,3},{3,2},{4,5},{5,4},{6,7},{7,6},{8,9},{9,8},{10,11... | collective-permute-start | bytes 589832 | tf_op jit(solution)/shard_map/ppermute | solution.py:773
  97.5 12.7 %collective-permute-start.30 = (bf16[128,512]{1,0:T(8,128)(2,1)S(1)}, bf16[128,512]{1,0:T(8,128)(2,1)S(1)}, u32[]{:S(2)}, u32[]{:S(2)}) collective-permute-start(bf16[128,512]{1,0:T(8,128)(2,1)S(1)} %get-tuple-element.143), channel_id=1, source_target_pairs={{0,16},{1,17},{2,18},{3,19},{4,20},{5,21},{6,22},{7,23},{8,24},{9,... | collective-permute-start | bytes 393224 | tf_op jit(solution)/shard_map/ppermute | solution.py:773
  102.4 5.0 %collective-permute-start.22 = (bf16[128,512]{1,0:T(8,128)(2,1)S(1)}, bf16[128,512]{1,0:T(8,128)(2,1)S(1)}, u32[]{:S(2)}, u32[]{:S(2)}) collective-permute-start(bf16[128,512]{1,0:T(8,128)(2,1)S(1)} %get-tuple-element.125), channel_id=1, source_target_pairs={{0,4},{1,5},{2,6},{3,7},{4,0},{5,1},{6,2},{7,3},{8,12},{9,13},{10,... | collective-permute-start | bytes 393224 | tf_op jit(solution)/shard_map/ppermute | solution.py:773
  103.6 5.0 %collective-permute-start.23 = (bf16[128,512]{1,0:T(8,128)(2,1)S(1)}, bf16[128,512]{1,0:T(8,128)(2,1)S(1)}, u32[]{:S(2)}, u32[]{:S(2)}) collective-permute-start(bf16[128,512]{1,0:T(8,128)(2,1)S(1)} %get-tuple-element.126), channel_id=1, source_target_pairs={{0,1},{1,0},{2,3},{3,2},{4,5},{5,4},{6,7},{7,6},{8,9},{9,8},{10,11... | collective-permute-start | bytes 393224 | tf_op jit(solution)/shard_map/ppermute | solution.py:773
  105.4 7.5 %collective-permute-start.27 = (bf16[224,512]{1,0:T(8,128)(2,1)S(1)}, bf16[224,512]{1,0:T(8,128)(2,1)S(1)}, u32[]{:S(2)}, u32[]{:S(2)}) collective-permute-start(bf16[224,512]{1,0:T(8,128)(2,1)S(1)} %get-tuple-element.134), channel_id=1, source_target_pairs={{0,8},{1,9},{2,10},{3,11},{4,12},{5,13},{6,14},{7,15},{8,0},{9,1},... | collective-permute-start | bytes 688136 | tf_op jit(solution)/shard_map/ppermute | solution.py:773
  108.6 7.4 %collective-permute-start.26 = (bf16[128,512]{1,0:T(8,128)(2,1)S(1)}, bf16[128,512]{1,0:T(8,128)(2,1)S(1)}, u32[]{:S(2)}, u32[]{:S(2)}) collective-permute-start(bf16[128,512]{1,0:T(8,128)(2,1)S(1)} %get-tuple-element.132), channel_id=1, source_target_pairs={{0,8},{1,9},{2,10},{3,11},{4,12},{5,13},{6,14},{7,15},{8,0},{9,1},... | collective-permute-start | bytes 393224 | tf_op jit(solution)/shard_map/ppermute | solution.py:773
  113.0 6.0 %collective-permute-start.29 = (bf16[128,512]{1,0:T(8,128)(2,1)S(1)}, bf16[128,512]{1,0:T(8,128)(2,1)S(1)}, u32[]{:S(2)}, u32[]{:S(2)}) collective-permute-start(bf16[128,512]{1,0:T(8,128)(2,1)S(1)} %get-tuple-element.139), channel_id=1, source_target_pairs={{0,16},{1,17},{2,18},{3,19},{4,20},{5,21},{6,22},{7,23},{8,24},{9,... | collective-permute-start | bytes 393224 | tf_op jit(solution)/shard_map/ppermute | solution.py:773
  116.0 5.3 %collective-permute-start.28 = (bf16[64,512]{1,0:T(8,128)(2,1)S(1)}, bf16[64,512]{1,0:T(8,128)(2,1)S(1)}, u32[]{:S(2)}, u32[]{:S(2)}) collective-permute-start(bf16[64,512]{1,0:T(8,128)(2,1)S(1)} %get-tuple-element.137), channel_id=1, source_target_pairs={{0,16},{1,17},{2,18},{3,19},{4,20},{5,21},{6,22},{7,23},{8,24},{9,... | collective-permute-start | bytes 196616 | tf_op jit(solution)/shard_map/ppermute | solution.py:773
  (5 other events, 65.3 us)
where the time goes:
time: 122 us
  Pallas kernels  55.4 us (45%)
  starting transfers between devices  33.6 us (28%)
  waiting for transfers between devices  30.2 us (25%)
  local copies, waits for them, and re-layouts  1.88 us (2%)
    pallas_call x1, Pallas kernels, fast_shards(): pl.pallas_call(functools.partial(main_kernel, orders, dp_bits, [turn for...  23.4 us
    ppermute x18, starting transfers between devices, swap(): lax.ppermute(value, ('dp', 'tap'), [(i, i ^ mask) for i in range(count)])  23.3 us
    ppermute x18, waiting for transfers between devices, swap(): lax.ppermute(value, ('dp', 'tap'), [(i, i ^ mask) for i in range(count)])  18 us
    pallas_call x2, Pallas kernels, terms(): pl.pallas_call(functools.partial(terms_kernel, group, orders, dp_bits, sm...  8.8 us
    ppermute x11, waiting for transfers between devices, swap_dp(): return lax.ppermute(value, 'dp', [(i, i ^ 1 << bit) for i in range(count)])  6.18 us
    ppermute x2, waiting for transfers between devices, swap_tap(): return lax.ppermute(value, 'tap', [(0, 1), (1, 0)])  6.01 us
    ppermute x11, starting transfers between devices, swap_dp(): return lax.ppermute(value, 'dp', [(i, i ^ 1 << bit) for i in range(count)])  5.81 us
    pallas_call x1, Pallas kernels, fast_shards(): pl.pallas_call(own_conv_kernel, out_shape=[vmem(pad_shape, BF16), vmem(ro...  5.63 us
  transfers between devices with their start and end apart: 31, of which 16 were waited for; matrix products, arithmetic and copies ran while one was open for 1% of the time, Pallas kernels for 24%

commit v1 on v0

--- a/solution.py
+++ b/solution.py
@@ -238,7 +238,7 @@
     )
 
 
-TILE = 256
+TILE = 512
 COLS = 512
 PAD = KERNEL_TAPS // 2 * DILATION_STEP
 MIB = 2**20
@@ -256,8 +256,8 @@
 
 def gelu_and_slope(value):
     cdf = 0.5 + 0.5 * lax.erf(value * 0.7071067811865476)
-    density = 0.3989422804014327 * jnp.exp(value * value * -0.5)
-    return value * cdf, cdf + value * density
+    density = jnp.exp2(value * value * -0.7213475204444817)
+    return value * cdf, cdf + (value * 0.3989422804014327) * density
 
 
 def norm_parts(value):
@@ -339,11 +339,18 @@
     return (4.0 / count)[0:1, :]
 
 
-def own_conv_kernel(table, x_hbm, weight_hbm, _, x_pad, part, token, weight, sems):
+def load_kernel(
+    table, x_hbm, weight_hbm, w_in_hbm, x_pad, weight, w_in, straight, sems
+):
     windows = x_pad.shape[0]
     slots = weight.shape[0]
+    rows = weight.shape[1] // 8
     base = lax.axis_index("tap") * windows * WINDOW_LENGTH
+    start = ((lax.axis_index("dp") & 7) ^ 6) * rows
     copies = []
+    for slot in range(slots):
+        source = weight_hbm.at[slot, rows_at(start, rows), :]
+        copies.append((source, straight.at[slot * rows : (slot + 1) * rows, :]))
     for win in range(windows):
         source = x_hbm.at[rows_at(base + win * WINDOW_LENGTH, WINDOW_LENGTH), :]
         copies.append((source, x_pad.at[win, PAD : PAD + WINDOW_LENGTH, :]))
@@ -352,16 +359,24 @@
         pltpu.make_async_copy(source, target, sems.at[at])
         for at, (source, target) in enumerate(copies)
     ]
+    copies += split_copy(w_in_hbm, w_in, sems, len(copies))
     for copy in copies:
         copy.start()
+    at = lax.broadcasted_iota(jnp.int32, (TABLE_ROWS, straight.shape[1]), 0)
+    taps = jnp.zeros(at.shape, jnp.int32)
+    for slot in range(slots):
+        taps = jnp.where(at == slot, table[slot], taps)
+    straight[slots * rows :, :] = taps.astype(F32).astype(BF16)
     clear_pads(x_pad)
+    wait_all(copies)
+
+
+def own_conv_kernel(table, x_pad, weight, _, part, token):
     token[...] = jnp.zeros(token.shape, token.dtype)
-    for copy in copies:
-        copy.wait()
 
     def convolve(rows, win, begin):
         total = None
-        for slot in range(slots):
+        for slot in range(weight.shape[0]):
             shifted = rows_at(table[slot] * DILATION_STEP + begin, TILE)
             term = dot_plain(x_pad[win, shifted, :], weight[slot])
             total = term if total is None else total + term
@@ -370,38 +385,31 @@
     each_tile(part.shape[0], convolve, 2)
 
 
-def fetch_plan(rows):
-    direct = rows // 8
-    return direct, (rows - 2 * direct) // 8
-
-
 def join_pieces(plan, pieces, weight):
-    direct, shared = fetch_plan(weight.shape[1])
-    place = lax.axis_index("dp")
-    for (turn, first), piece in zip(plan, pieces):
-        if first is None:
-            at = ((place & 1) ^ turn) * direct
-            for slot in range(weight.shape[0]):
-                part = piece[slot * direct : (slot + 1) * direct, :]
-                weight[slot, rows_at(at, direct), :] = part
-            continue
-        slots = weight.shape[0]
-        for begin, place_turn in ((0, turn), (slots, first)):
-            if begin < piece.shape[0]:
-                at = 2 * direct + ((place & 7) ^ place_turn) * shared
-                weight[:, rows_at(at, shared), :] = piece[begin : begin + slots]
+    slots = weight.shape[0]
+    rows = weight.shape[1] // 8
+    place = lax.axis_index("dp") & 7
+    for turns, piece in zip(plan, pieces):
+        flat = len(piece.shape) == 2
+        for number, turn in enumerate(turns):
+            there = rows_at((place ^ turn) * rows, rows)
+            if flat:
+                for slot in range(slots):
+                    weight[slot, there, :] = piece[slot * rows : (slot + 1) * rows, :]
+            else:
+                weight[:, there, :] = piece[number * slots : (number + 1) * slots]
 
 
 def main_kernel(orders, dp_bits, turns, *refs):
     species, counts = refs[:2]
-    x_pad, part, grad_hbm, w_in_hbm, w_out_hbm = refs[2:7]
+    x_pad, part, grad_hbm, w_in, w_out_hbm = refs[2:7]
     conv_bias, gain_one, bias_one, b_in, b_out, gain_two, bias_two = refs[7:14]
     pieces = refs[14 : 14 + len(turns)]
-    y_hbm, unit, slope, d_up, weight, keep, send, small, grad_in, w_in, table = refs[
-        14 + len(turns) : 25 + len(turns)
+    y_hbm, unit, slope, d_up, weight, keep, send, small, grad_in, table = refs[
+        14 + len(turns) : 24 + len(turns)
     ]
-    w_out, hidden, low, act, hid_slope, d_out, y_low, result, sums, sem, sems = refs[25 + len(turns) :]
-    told = pieces[turns.index((0, None))]
+    w_out, hidden, low, act, hid_slope, d_out, y_low, result, sums, sem, sems = refs[24 + len(turns) :]
+    told = pieces[turns.index((6,))]
     told_at = told.shape[0] - TABLE_ROWS
     taps = []
     for slot in range(weight.shape[0]):
@@ -413,10 +421,9 @@
     rows_dev, chan = hidden.shape
     hid_width = w_in.shape[1]
     windows = x_pad.shape[0]
-    in_copies = split_copy(w_in_hbm, w_in, sems, 0)
     out_copies = split_copy(w_out_hbm, w_out, sems, 4)
     grad_copies = split_copy(grad_hbm, grad_in, sems, 8)
-    for copy in in_copies + out_copies + grad_copies:
+    for copy in out_copies + grad_copies:
         copy.start()
     join_pieces(turns, pieces, weight)
     sums[...] = jnp.zeros(sums.shape, F32)
@@ -436,7 +443,6 @@
         low[rows, :] = summed.astype(BF16)
 
     each_tile(rows_dev, first_norm, 2)
-    wait_all(in_copies)
 
     def go_up(rows, win, begin):
         for at in range(0, hid_width, COLS):
@@ -571,13 +577,7 @@
         small, _, keep, send, result = refs
         store_small(small[...], send, keep.shape[0])
     else:
-        weight_hbm, _, keep, send, weight, result, sem = refs
-        copies = [
-            pltpu.make_async_copy(weight_hbm.at[slot], weight.at[slot], sem.at[slot])
-            for slot in range(weight.shape[0])
-        ]
-        for copy in copies:
-            copy.start()
+        _, keep, send, result = refs
     mine = my_bits(dp_bits)
     rows = x_pad.shape[2] >> dp_bits
     core = mine[0]
@@ -608,9 +608,6 @@
                     keep[place, :] = result[near_tap, mine_at, :]
                     send[place, :] = result[near_tap, other_at, :].astype(BF16)
 
-    if not with_small:
-        wait_all(copies)
-
 
 def input_sum(table, d_pad, base, weight, rows, win, begin):
     total = base[rows, :]
@@ -641,28 +638,39 @@
     pltpu.make_async_copy(out, out_hbm, sems.at[0]).wait()
 
 
-def step_kernel(joined_in, joined_out, with_small, *refs):
-    gots = refs[: 2 - joined_in]
-    keep = refs[2 - joined_in]
-    outs = refs[4 - joined_in + with_small :]
-    rows = keep.shape[0] // 2
-    half = rows // 2
-    for part in range(2):
-        got = gots[0 if joined_in else part]
-        base = part * rows if joined_in else 0
-        start = part * rows
-        sent = keep[start + half : start + rows, :] + got[base + half : base + rows, :].astype(F32)
-        if joined_out:
-            outs[1][part * half : (part + 1) * half, :] = sent.astype(BF16)
-        else:
-            outs[1 + part][0:half, :] = sent.astype(BF16)
-        kept = keep[start : start + half, :] + got[base : base + half, :].astype(F32)
-        outs[0][part * half : (part + 1) * half, :] = kept
-    if with_small:
-        small = refs[3 - joined_in]
-        total = small[...] + load_small(gots[0], rows * (1 + joined_in), small.shape[0])
-        outs[3 - joined_out][...] = total
-        store_small(total, outs[1], half * (1 + joined_out))
+def fused_kernel(got_count, plans, *refs):
+    gots = refs[:got_count]
+    at = got_count
+    inputs = []
+    for plan in plans:
+        inputs.append(refs[at : at + 1 + plan["with_small"]])
+        at += 1 + plan["with_small"]
+    at += 1
+    kept = []
+    for plan in plans:
+        kept.append(refs[at : at + 1 + plan["with_small"]])
+        at += 1 + plan["with_small"]
+    sent = refs[at:]
+    for plan, source, target in zip(plans, inputs, kept):
+        keep = source[0]
+        rows = keep.shape[0] // 2
+        half = rows // 2
+        for part in range(2):
+            which, base = plan["ins"][part]
+            out, spot = plan["outs"][part]
+            start = part * rows
+            theirs = gots[which][base + half : base + rows, :].astype(F32)
+            total = keep[start + half : start + rows, :] + theirs
+            sent[out][spot : spot + half, :] = total.astype(BF16)
+            ours = gots[which][base : base + half, :].astype(F32)
+            target[0][part * half : (part + 1) * half, :] = keep[start : start + half, :] + ours
+        if plan["with_small"]:
+            which, base = plan["small_in"]
+            count = source[1].shape[0]
+            total = source[1][...] + load_small(gots[which], base, count)
+            target[1][...] = total
+            out, spot = plan["small_out"]
+            store_small(total, sent[out], spot)
 
 
 def sum_of(gots, keep, rows):
@@ -674,7 +682,8 @@
 
 def last_ffn_kernel(members, *refs):
     gots = refs[:members]
-    keep, _, w_in_out, w_out_out = refs[members:]
+    keep, _, w_in_out, w_out_out, token = refs[members:]
+    token[...] = jnp.zeros(token.shape, token.dtype)
     out_rows, chan = w_out_out.shape
     in_rows = w_in_out.shape[0]
     half = keep.shape[0] // 2
@@ -689,25 +698,54 @@
             w_in_out[:, cols] = sum_of(gots, keep, slice(at, at + in_rows))
 
 
-def last_small_kernel(got, keep, small, _, out, next_small):
-    rows = out.shape[0]
-    out[...] = keep[...] + got[0:rows, :].astype(F32)
-    next_small[...] = small[...] + load_small(got, rows, small.shape[0])
-
-
-def last_conv_kernel(got, keep, done, out):
+def last_conv_kernel(
+    got,
+    keep_a,
+    small,
+    keep_b,
+    out,
+    total,
+    conv_bias,
+    gain_one,
+    bias_one,
+    b_out,
+    gain_two,
+    bias_two,
+    b_in,
+):
     size = out.shape[1] // 2
-    first = done.shape[0] // out.shape[1]
+    first = keep_a.shape[0] // out.shape[1]
     rest = out.shape[0] - first
+    shift = keep_a.shape[0]
     for slot in range(out.shape[0]):
         for part in range(2):
-            place = slice(part * size, (part + 1) * size)
             if slot < first:
                 at = (part * first + slot) * size
-                out[slot, place, :] = done[at : at + size, :]
+                kept, base = keep_a, 0
             else:
                 at = (part * rest + slot - first) * size
-                out[slot, place, :] = keep[at : at + size, :] + got[at : at + size, :].astype(F32)
+                kept, base = keep_b, shift
+            theirs = got[base + at : base + at + size, :].astype(F32)
+            out[slot, part * size : (part + 1) * size, :] = kept[at : at + size, :] + theirs
+    total[...] = small[...] + load_small(got, shift + keep_b.shape[0], small.shape[0])
+    lanes = small.shape[1]
+    owner = lax.axis_index("dp") * lax.axis_size("tap") + lax.axis_index("tap")
+    width = b_out.shape[1]
+    turned = pltpu.roll(total[...], (lanes - owner * width) % lanes, 1)
+    for at, target in (
+        (0, b_out),
+        (1, gain_two),
+        (2, bias_two),
+        (8, conv_bias),
+        (9, gain_one),
+        (10, bias_one),
+    ):
+        target[...] = turned[at : at + 1, 0:width]
+    width = b_in.shape[1]
+    start = owner * width
+    line = total[pl.ds(3 + start // lanes, 1), :]
+    line = pltpu.roll(jnp.broadcast_to(line, (8, lanes)), (lanes - start % lanes) % lanes, 1)
+    b_in[...] = line[0:1, 0:width]
 
 
 def params(mib):
@@ -743,29 +781,37 @@
     return pltpu.with_memory_space_constraint(value, pltpu.VMEM)
 
 
-def step(gots, keep, joined_out, token, small=None):
-    lanes = keep.shape[1]
-    half = keep.shape[0] // 4
-    extra = 0 if small is None else 2 * small.shape[0]
-    sent = [2 * half + extra] if joined_out else [half + extra, half]
-    outs = [pltpu.VMEM((2 * half, lanes), F32)]
-    outs += [pltpu.VMEM((rows, lanes), BF16) for rows in sent]
-    operands = [near(got) for got in gots] + [near(keep)]
-    if small is not None:
-        outs.append(pltpu.VMEM(small.shape, F32))
-        operands.append(near(small))
+def fused_step(gots, flows, plans, sizes, token):
+    lanes = flows[0]["keep"].shape[1]
+    operands = [near(got) for got in gots]
+    outs = []
+    for flow, plan in zip(flows, plans):
+        plan["with_small"] = "small_in" in plan
+        operands.append(near(flow["keep"]))
+        outs.append(pltpu.VMEM((flow["keep"].shape[0] // 2, lanes), F32))
+        if plan["with_small"]:
+            operands.append(near(flow["small"]))
+            outs.append(pltpu.VMEM(flow["small"].shape, F32))
+    operands.append(near(token))
+    kept = len(outs)
+    outs += [pltpu.VMEM((rows, lanes), BF16) for rows in sizes]
     out = pl.pallas_call(
-        functools.partial(step_kernel, len(gots) == 1, joined_out, small is not None),
+        functools.partial(fused_kernel, len(gots), plans),
         out_shape=outs,
-        in_specs=[VMEM] * (len(operands) + 1),
+        in_specs=[VMEM] * len(operands),
         out_specs=[VMEM] * len(outs),
         compiler_params=params(4),
         cost_estimate=claim(0),
         name="step",
-    )(*operands, near(token))
-    if small is None:
-        return out[0], out[1:], None
-    return out[0], out[1:-1], out[-1]
+    )(*operands)
+    at = 0
+    for flow, plan in zip(flows, plans):
+        flow["keep"] = out[at]
+        at += 1
+        if plan["with_small"]:
+            flow["small"] = out[at]
+            at += 1
+    return out[kept:]
 
 
 def swap(value, mask):
@@ -773,100 +819,61 @@
     return lax.ppermute(value, ("dp", "tap"), [(i, i ^ mask) for i in range(count)])
 
 
-def cut_kernel(table, weight_hbm, shared, direct, sems):
-    slots = shared.shape[0]
-    rows = (direct.shape[0] - TABLE_ROWS) // slots
-    place = lax.axis_index("dp")
-    start = 2 * rows + (place & 7) * shared.shape[1]
-    near_start = (place & 1) * rows
-    copies = []
-    for slot in range(slots):
-        pair = (
-            (weight_hbm.at[slot, rows_at(start, shared.shape[1]), :], shared.at[slot]),
-            (
-                weight_hbm.at[slot, rows_at(near_start, rows), :],
-                direct.at[slot * rows : (slot + 1) * rows, :],
-            ),
+def cut_kernel(weight_hbm, piece, sems):
+    rows = piece.shape[1]
+    start = (lax.axis_index("dp") & 7) * rows
+    copies = [
+        pltpu.make_async_copy(
+            weight_hbm.at[slot, rows_at(start, rows), :], piece.at[slot], sems.at[slot]
         )
-        for source, target in pair:
-            copies.append(pltpu.make_async_copy(source, target, sems.at[len(copies)]))
+        for slot in range(piece.shape[0])
+    ]
     for copy in copies:
         copy.start()
-    at = lax.broadcasted_iota(jnp.int32, (TABLE_ROWS, direct.shape[1]), 0)
-    taps = jnp.zeros(at.shape, jnp.int32)
-    for slot in range(slots):
-        taps = jnp.where(at == slot, table[slot], taps)
-    direct[slots * rows :, :] = taps.astype(F32).astype(BF16)
-    for copy in copies:
-        copy.wait()
-
-
-def cut_pieces(table, conv_weight):
+    wait_all(copies)
+
+
+def cut_piece(conv_weight):
     slots, chan, width = conv_weight.shape
-    direct, shared = fetch_plan(chan)
     return pl.pallas_call(
         cut_kernel,
-        out_shape=[
-            pltpu.VMEM((slots, shared, width), BF16),
-            pltpu.VMEM((slots * direct + TABLE_ROWS, width), BF16),
-        ],
-        in_specs=[SMEM, HBM],
-        out_specs=[VMEM] * 2,
-        scratch_shapes=[pltpu.SemaphoreType.DMA((2 * slots,))],
+        out_shape=pltpu.VMEM((slots, chan // 8, width), BF16),
+        in_specs=[HBM],
+        out_specs=VMEM,
+        scratch_shapes=[pltpu.SemaphoreType.DMA((slots,))],
         compiler_params=params(4),
         cost_estimate=claim(0),
-        name="cut_pieces",
-    )(table, far(conv_weight))
-
-
-def pick_kernel(over_one, over_two, _, low, high, both):
+        name="cut_piece",
+    )(far(conv_weight))
+
+
+def both_kernel(over_one, over_two, _, both):
     slots = over_one.shape[0]
-    low[...] = over_two[0 : low.shape[0]]
-    high[...] = over_one[low.shape[0] :]
     both[0:slots] = over_one[...]
     both[slots:] = over_two[...]
 
 
-def pair_up_kernel(low, high, both):
-    both[0 : low.shape[0]] = low[...]
-    both[low.shape[0] :] = high[...]
-
-
-def vmem_call(kernel, shapes, operands, name):
-    return pl.pallas_call(
-        kernel,
-        out_shape=[pltpu.VMEM(shape, BF16) for shape in shapes],
-        in_specs=[VMEM] * len(operands),
-        out_specs=[VMEM] * len(shapes),
+def fetch_pieces(first, straight, token):
+    over_one = swap_dp(first, 1)
+    over_two = swap_dp(first, 2)
+    straight = swap_tap(after(straight, first))
+    slots = first.shape[0]
+    both = pl.pallas_call(
+        both_kernel,
+        out_shape=pltpu.VMEM((2 * slots,) + first.shape[1:], BF16),
+        in_specs=[VMEM] * 3,
+        out_specs=VMEM,
         compiler_params=params(4),
         cost_estimate=claim(0),
-        name=name,
-    )(*[near(operand) for operand in operands])
-
-
-def fetch_pieces(first, direct, token):
-    over_one = swap_dp(first, 1)
-    over_two = swap_dp(first, 2)
-    straight = swap_tap(after(direct, first))
-    slots = first.shape[0]
-    cut = (slots + 1) // 2
-    rest = first.shape[1:]
-    shapes = [(count,) + rest for count in (cut, slots - cut, 2 * slots)]
-    low, high, both = vmem_call(pick_kernel, shapes, [over_one, over_two, token], "pick")
-    (last,) = vmem_call(
-        pair_up_kernel, [first.shape], [swap_dp(low, 1), swap_dp(high, 2)], "pair_up"
-    )
-    straight = after(straight, low)
-    both_mate = swap_dp(both, 0)
+        name="both",
+    )(near(over_one), near(over_two), near(token))
     return [
-        ((0, 0), first),
+        ((0,), first),
         ((2, 4), both),
-        ((0, None), straight),
-        ((6, 0), last),
-        ((1, 0), swap_dp(first, 0)),
-        ((3, 5), both_mate),
-        ((1, None), swap_dp(straight, 0)),
-        ((7, 0), swap_dp(last, 0)),
+        ((6,), straight),
+        ((1,), swap_dp(first, 0)),
+        ((3, 5), swap_dp(both, 0)),
+        ((7,), swap_dp(straight, 0)),
     ]
 
 
@@ -897,6 +904,7 @@
     vmem = pltpu.VMEM
     line = list(range(2, dp_bits))
     orders = (["t", 1] + line, [1, "t"] + line)
+    orders_b = ([2, "t", 1] + line[1:], [2, 1, "t"] + line[1:])
     over_x, over_y = 1, 4
     pad_shape = (windows, WINDOW_LENGTH + 2 * PAD, chan)
     rows_f = (rows_dev, chan)
@@ -905,22 +913,37 @@
     def row(vector):
         return vector.reshape(1, -1)
 
-    shared, direct = cut_pieces(slot_tap_table, conv_weight)
+    piece = cut_piece(conv_weight)
     weight_shape = conv_weight.shape
     tiles = rows_dev // TILE
     dma = pltpu.SemaphoreType.DMA
-    first = swap_tap(shared)
-    x_pad, part, token = pl.pallas_call(
+    first = swap_tap(piece)
+    x_pad, own_weight, w_in_near, straight = pl.pallas_call(
+        load_kernel,
+        out_shape=[
+            vmem(pad_shape, BF16),
+            vmem(weight_shape, BF16),
+            vmem(w_in.shape, BF16),
+            vmem((slots * chan // 8 + TABLE_ROWS, chan), BF16),
+        ],
+        in_specs=[SMEM] + [HBM] * 3,
+        out_specs=[VMEM] * 4,
+        scratch_shapes=[dma((windows + 2 * slots + 4,))],
+        compiler_params=params(8),
+        cost_estimate=claim(0),
+        name="load",
+    )(slot_tap_table, far(block_input), far(conv_weight), far(w_in))
+    first = after(first, x_pad)
+    part, token = pl.pallas_call(
         own_conv_kernel,
-        out_shape=[vmem(pad_shape, BF16), vmem(rows_f, F32), vmem((8, 128), F32)],
-        in_specs=[SMEM] + [HBM] * 2 + [VMEM],
-        out_specs=[VMEM] * 3,
-        scratch_shapes=[vmem(weight_shape, BF16), dma((windows + slots,))],
+        out_shape=[vmem(rows_f, F32), vmem((8, 128), F32)],
+        in_specs=[SMEM] + [VMEM] * 3,
+        out_specs=[VMEM] * 2,
         compiler_params=params(8),
         cost_estimate=claim(0),
         name="own_conv",
-    )(slot_tap_table, far(block_input), far(conv_weight), near(first))
-    pieces = fetch_pieces(first, direct, token)
+    )(slot_tap_table, near(x_pad), near(own_weight), near(first))
+    pieces = fetch_pieces(first, straight, token)
 
     block_f = (hid + chan * hid // COLS) >> (dp_bits + 1)
     half_f = block_f << dp_bits
@@ -936,11 +959,10 @@
             vmem((half_f, chan), BF16),
             vmem((8, chan), F32),
             vmem(rows_f, BF16),
-            vmem(w_in.shape, BF16),
             jax.ShapeDtypeStruct((slots,), jnp.int32),
         ],
-        in_specs=[SMEM] * 2 + [VMEM] * 2 + [HBM] * 3 + [VMEM] * (7 + len(pieces)),
-        out_specs=[HBM] + [VMEM] * 9 + [SMEM],
+        in_specs=[SMEM] * 2 + [VMEM] * 2 + [HBM, VMEM, HBM] + [VMEM] * (7 + len(pieces)),
+        out_specs=[HBM] + [VMEM] * 8 + [SMEM],
         scratch_shapes=[
             vmem(w_out.shape, BF16),
             vmem(rows_f, F32),
@@ -963,7 +985,7 @@
         near(x_pad),
         near(part),
         far(out_grad),
-        far(w_in),
+        near(w_in_near),
         far(w_out),
         row(conv_bias),
         row(conv_norm_gain),
@@ -975,7 +997,7 @@
         *[near(piece) for _, piece in pieces],
     )
     block_output, unit, slope, d_up, other_weight, keep_f, send_f, small_ffn = main[:8]
-    grad_in, w_in_near, other_table = main[8:]
+    grad_in, other_table = main[8:]
     got_f = swap_dp(send_f, 0)
 
     d_pad, d_hidden, small = pl.pallas_call(
@@ -998,50 +1020,63 @@
         row(conv_norm_gain),
         near(small_ffn),
     )
-    keep_f, sends_f, _ = step([got_f], keep_f, False, small)
+    flow_f = dict(keep=keep_f)
+    rows = keep_f.shape[0] // 2
+    plan = dict(ins=[(0, 0), (0, rows)], outs=[(0, 0), (1, 0)])
+    sends_f = fused_step([got_f], [flow_f], [plan], [rows // 2] * 2, small)
     gots_f = [swap(sends_f[0], over_x), swap(sends_f[1], over_y)]
 
-    def terms(group, token, small, name):
+    def terms(group, orders, token, small, name):
         count = len(group) * chan
         extra = 0 if small is None else 2 * small.shape[0]
         outs = [vmem((count, chan), F32), vmem((count + extra, chan), BF16)]
         scratch = [vmem((2, chan, chan), F32)]
-        if small is None:
-            last, last_spec = far(conv_weight), HBM
-            outs.append(vmem(weight_shape, BF16))
-            scratch.append(dma((slots,)))
-        else:
-            last, last_spec = near(small), VMEM
+        more = [] if small is None else [near(small)]
         return pl.pallas_call(
             functools.partial(terms_kernel, group, orders, dp_bits, small is not None),
             out_shape=outs,
-            in_specs=[SMEM] * 2 + [VMEM] * 2 + [last_spec, VMEM],
+            in_specs=[SMEM] * 2 + [VMEM] * (3 + len(more)),
             out_specs=[VMEM] * len(outs),
             scratch_shapes=scratch,
             compiler_params=params(8),
             cost_estimate=small_cost,
             name=name,
-        )(slot_tap_table, other_table, near(x_pad), near(d_pad), last, near(token))
+        )(slot_tap_table, other_table, near(x_pad), near(d_pad), *more, near(token))
 
     cut = (slots * 3 + 4) // 5
-    keep_a, send_a = terms(range(0, cut), sends_f[0], small, "terms_a")
+    keep_a, send_a = terms(range(0, cut), orders, sends_f[0], None, "terms_a")
     got_a = swap_dp(send_a, 0)
-    keep_b, send_b, own_weight = terms(range(cut, slots), keep_a, None, "terms_b")
+    keep_b, send_b = terms(range(cut, slots), orders_b, keep_a, small, "terms_b")
     got_b = swap_dp(send_b, 0)
     def spaced(token, claimed=1):
         return after(mark, token, claimed)
 
-    def turned(sends):
-        return [swap(sends[0], over_y), swap(sends[1], over_x)]
-
-    def along(sends, stage):
-        return [swap(sends[0], 2 << line[stage])]
-
     mark = token
-    keep_f, sends_f, _ = step(gots_f, keep_f, False, keep_b)
-    gots_f = turned(sends_f)
-    keep_a, sends_a, small = step([got_a], keep_a, False, spaced(keep_f, 100), small)
-    gots_a = [swap(sends_a[0], over_x), swap(sends_a[1], over_y)]
+    flow_a = dict(keep=keep_a)
+    flow_b = dict(keep=keep_b, small=small)
+    extra = 2 * small.shape[0]
+    over_z, over_zz = 2 << line[0], 2 << line[1]
+
+    def half_of(flow):
+        return flow["keep"].shape[0] // 4
+
+    def joined(base, flow):
+        return [(0, base), (0, base + 2 * half_of(flow))]
+
+    size = half_of(flow_f)
+    plan = dict(ins=[(0, 0), (1, 0)], outs=[(0, 0), (1, 0)])
+    sends = fused_step(gots_f, [flow_f], [plan], [size] * 2, keep_b)
+    gots_f = [swap(sends[0], over_y), swap(sends[1], over_x)]
+    mark = spaced(flow_f["keep"], 100)
+    size = half_of(flow_b)
+    plan = dict(
+        ins=joined(0, flow_b),
+        small_in=(0, 4 * size),
+        outs=[(0, 0), (0, size)],
+        small_out=(0, 2 * size),
+    )
+    sends = fused_step([got_b], [flow_b], [plan], [2 * size + extra], mark)
+    got_b = swap(sends[0], over_z)
     partial = pl.pallas_call(
         input_near_kernel,
         out_shape=vmem(rows_f, F32),
@@ -1050,7 +1085,16 @@
         compiler_params=params(8),
         cost_estimate=claim(0),
         name="input_near",
-    )(slot_tap_table, near(d_pad), near(d_hidden), near(own_weight), near(keep_a))
+    )(slot_tap_table, near(d_pad), near(d_hidden), near(own_weight), near(flow_b["keep"]))
+    size = half_of(flow_f)
+    plan = dict(ins=[(0, 0), (1, 0)], outs=[(0, 0), (0, size)])
+    sends = fused_step(gots_f, [flow_f], [plan], [2 * size], partial)
+    got_f = swap(sends[0], over_z)
+    mark = spaced(flow_f["keep"])
+    size = half_of(flow_a)
+    plan = dict(ins=joined(0, flow_a), outs=[(0, 0), (1, 0)])
+    sends = fused_step([got_a], [flow_a], [plan], [size] * 2, mark)
+    gots_a = [swap(sends[0], over_x), swap(sends[1], over_y)]
     input_grad, mark = pl.pallas_call(
         input_far_kernel,
         out_shape=[pltpu.HBM(rows_f, F32), vmem((8, 128), F32)],
@@ -1060,86 +1104,105 @@
         compiler_params=params(8),
         cost_estimate=small_cost,
         name="input_far",
-    )(other_table, near(d_pad), near(partial), near(other_weight), near(keep_a))
+    )(other_table, near(d_pad), near(partial), near(other_weight), near(flow_a["keep"]))
     mark = spaced(mark)
-    keep_f, sends_f, _ = step(gots_f, keep_f, True, mark)
-    got_f = along(sends_f, 0)
-    keep_b, sends_b, _ = step([got_b], keep_b, False, keep_f)
-    gots_b = [swap(sends_b[0], over_x), swap(sends_b[1], over_y)]
-    mark = spaced(keep_b)
-    keep_a, sends_a, small = step(gots_a, keep_a, False, mark, small)
-    gots_a = turned(sends_a)
-    mark = spaced(keep_a)
-    for stage in range(1, len(line)):
-        keep_f, sends_f, _ = step(got_f, keep_f, True, mark)
-        got_f = along(sends_f, stage)
-        mark = spaced(keep_f)
-    keep_b, sends_b, _ = step(gots_b, keep_b, False, mark)
-    gots_b = turned(sends_b)
-    mark = spaced(keep_b)
-    keep_a, sends_a, small = step(gots_a, keep_a, True, mark, small)
-    got_a = along(sends_a, 0)
-    mark = spaced(keep_a)
-    w_in_mine, w_out_mine = pl.pallas_call(
+    size = half_of(flow_f)
+    plan = dict(ins=joined(0, flow_f), outs=[(0, 0), (0, size)])
+    sends = fused_step([got_f], [flow_f], [plan], [2 * size], mark)
+    got_f = swap(sends[0], over_zz)
+    mark = spaced(flow_f["keep"])
+    size, size_b = half_of(flow_a), half_of(flow_b)
+    plan = dict(ins=[(0, 0), (1, 0)], outs=[(0, 0), (1, 0)])
+    plan_b = dict(
+        ins=[(2, 0), (2, 2 * size_b)],
+        small_in=(2, 4 * size_b),
+        outs=[(1, size), (0, size)],
+        small_out=(1, size + size_b),
+    )
+    sends = fused_step(
+        gots_a + [got_b],
+        [flow_a, flow_b],
+        [plan, plan_b],
+        [size + size_b, size + size_b + extra],
+        mark,
+    )
+    gots = [swap(sends[0], over_y), swap(sends[1], over_x)]
+    mark = spaced(flow_a["keep"])
+    shift = size
+    size = half_of(flow_a)
+    plan = dict(ins=[(0, 0), (1, 0)], outs=[(0, 0), (0, size)])
+    sends = fused_step(gots, [flow_a], [plan], [2 * size], mark)
+    got_a = swap(sends[0], over_z)
+    size = half_of(flow_b)
+    plan = dict(
+        ins=[(1, shift), (0, shift)],
+        small_in=(1, shift + 2 * size),
+        outs=[(0, 0), (1, 0)],
+        small_out=(0, size),
+    )
+    sends = fused_step(gots, [flow_b], [plan], [size + extra, size], flow_a["keep"])
+    gots_b = [swap(sends[0], over_y), swap(sends[1], over_x)]
+    mark = spaced(flow_b["keep"])
+    w_in_mine, w_out_mine, mark = pl.pallas_call(
         functools.partial(last_ffn_kernel, 1),
         out_shape=[
             jax.ShapeDtypeStruct((chan >> (dp_bits + 1), hid), F32),
             jax.ShapeDtypeStruct((hid >> (dp_bits + 1), chan), F32),
+            vmem((8, 128), F32),
         ],
         in_specs=[VMEM] * 3,
-        out_specs=[VMEM] * 2,
+        out_specs=[VMEM] * 3,
         compiler_params=params(4),
         cost_estimate=claim(0),
         name="last_ffn",
-    )(near(got_f[0]), near(keep_f), near(mark))
-    keep_b, sends_b, _ = step(gots_b, keep_b, True, mark)
-    got_b = along(sends_b, 0)
-    mark = spaced(keep_b)
-    for stage in range(1, len(line)):
-        keep_a, sends_a, small = step(got_a, keep_a, True, mark, small)
-        got_a = along(sends_a, stage)
-        mark = spaced(keep_a)
-        keep_b, sends_b, _ = step(got_b, keep_b, True, mark)
-        got_b = along(sends_b, stage)
-        mark = spaced(keep_b)
-    part_a, small = pl.pallas_call(
-        last_small_kernel,
-        out_shape=[vmem(keep_a.shape, F32), vmem(small.shape, F32)],
+    )(near(got_f), near(flow_f["keep"]), near(mark))
+    mark = spaced(mark)
+    size, size_b = half_of(flow_a), half_of(flow_b)
+    plan = dict(ins=joined(0, flow_a), outs=[(0, 0), (0, size)])
+    shift = 2 * size
+    plan_b = dict(
+        ins=[(1, 0), (2, 0)],
+        small_in=(1, 2 * size_b),
+        outs=[(0, shift), (0, shift + size_b)],
+        small_out=(0, shift + 2 * size_b),
+    )
+    sends = fused_step(
+        [got_a] + gots_b, [flow_a, flow_b], [plan, plan_b], [shift + 2 * size_b + extra], mark
+    )
+    got = swap(sends[0], over_zz)
+    width = chan >> (dp_bits + 1)
+    wide = hid >> (dp_bits + 1)
+    small = flow_b["small"]
+    conv_weight_grad, _, *vectors = pl.pallas_call(
+        last_conv_kernel,
+        out_shape=[
+            jax.ShapeDtypeStruct((slots, chan >> dp_bits, chan), F32),
+            vmem(small.shape, F32),
+        ]
+        + [jax.ShapeDtypeStruct((1, width), F32)] * 6
+        + [jax.ShapeDtypeStruct((1, wide), F32)],
         in_specs=[VMEM] * 4,
-        out_specs=[VMEM] * 2,
-        compiler_params=params(4),
-        cost_estimate=claim(0),
-        name="last_a",
-    )(near(got_a[0]), near(keep_a), near(small), near(mark))
-    conv_weight_grad = pl.pallas_call(
-        last_conv_kernel,
-        out_shape=jax.ShapeDtypeStruct((slots, chan >> dp_bits, chan), F32),
-        in_specs=[VMEM] * 3,
-        out_specs=VMEM,
+        out_specs=[VMEM] * 9,
         compiler_params=params(4),
         cost_estimate=claim(0),
         name="last_conv",
-    )(near(got_b[0]), near(keep_b), near(part_a))
-    chunks = hid // COLS
-
-    owner = lax.axis_index("dp") * tap_count + lax.axis_index("tap")
-    width = chan >> (dp_bits + 1)
-    lanes = lax.dynamic_slice(small, (0, owner * width), (small.shape[0], width))
-    wide = hid >> (dp_bits + 1)
-    d_b_in = lax.dynamic_slice(small[3 : 3 + chunks].reshape(-1), (owner * wide,), (wide,))
+    )(near(got), near(flow_a["keep"]), near(small), near(flow_b["keep"]))
+    conv_bias_grad, gain_one_grad, bias_one_grad, b_out_grad, gain_two_grad, bias_two_grad, b_in_grad = [
+        vector.reshape(-1) for vector in vectors
+    ]
     return (
         block_output,
         input_grad,
         conv_weight_grad,
-        lanes[8],
-        lanes[9],
-        lanes[10],
+        conv_bias_grad,
+        gain_one_grad,
+        bias_one_grad,
         w_in_mine,
-        d_b_in,
+        b_in_grad,
         w_out_mine,
-        lanes[0],
-        lanes[1],
-        lanes[2],
+        b_out_grad,
+        gain_two_grad,
+        bias_two_grad,
     )
 
 

time: 122 us -> 116 us (0.951)
  starting transfers between devices: 33.6 us -> 27.8 us
  waiting for transfers between devices: 30.2 us -> 32.7 us
  local copies, waits for them, and re-layouts: 1.88 us -> 0.03 us
    ppermute x18 -> x15, waiting for transfers between devices: 18 us -> 23.5 us  [swap(): lax.ppermute(value, ('dp', 'tap'), [(i, i ^ mask) for i in range(count)])]
    ppermute x18 -> x15, starting transfers between devices: 23.3 us -> 18.5 us  [swap(): lax.ppermute(value, ('dp', 'tap'), [(i, i ^ mask) for i in range(count)])]
    ppermute x11 -> x8, waiting for transfers between devices: 6.18 us -> 3.57 us  [swap_dp(): return lax.ppermute(value, 'dp', [(i, i ^ 1 << bit) for i in range(count)])]
    ppermute x11 -> x8, starting transfers between devices: 5.81 us -> 4.78 us  [swap_dp(): return lax.ppermute(value, 'dp', [(i, i ^ 1 << bit) for i in range(count)])]
    pallas_call x18 -> x15, Pallas kernels: 10.1 us -> 10.4 us  [the longest x1 3.49 us: fast_shards(): pl.pallas_call(load_kernel, out_shape=[vmem(pad_shape, BF16), vmem(weight...]
  transfers between devices with their start and end apart: 31 -> 25, of which waited for: 16 -> 17; matrix products, arithmetic and copies ran while one was open for 1% -> 0% of each run, Pallas kernels for 24% -> 25%
where the time goes in v1:
time: 116 us
  Pallas kernels  54.6 us (47%)
  waiting for transfers between devices  32.7 us (28%)
  starting transfers between devices  27.8 us (24%)
    ppermute x15, waiting for transfers between devices, swap(): lax.ppermute(value, ('dp', 'tap'), [(i, i ^ mask) for i in range(count)])  23.5 us
    pallas_call x1, Pallas kernels, fast_shards(): pl.pallas_call(functools.partial(main_kernel, orders, dp_bits, [turn for...  22.7 us
    ppermute x15, starting transfers between devices, swap(): lax.ppermute(value, ('dp', 'tap'), [(i, i ^ mask) for i in range(count)])  18.5 us
    pallas_call x2, Pallas kernels, terms(): pl.pallas_call(functools.partial(terms_kernel, group, orders, dp_bits, sm...  8.92 us
    ppermute x2, waiting for transfers between devices, swap_tap(): return lax.ppermute(value, 'tap', [(0, 1), (1, 0)])  5.68 us
    ppermute x8, starting transfers between devices, swap_dp(): return lax.ppermute(value, 'dp', [(i, i ^ 1 << bit) for i in range(count)])  4.78 us
    ppermute x2, starting transfers between devices, swap_tap(): return lax.ppermute(value, 'tap', [(0, 1), (1, 0)])  4.49 us
    pallas_call x1, Pallas kernels, fast_shards(): pl.pallas_call(input_far_kernel, out_shape=[pltpu.HBM(rows_f, F32), vmem(...  4.44 us
  transfers between devices with their start and end apart: 25, of which 17 were waited for; matrix products, arithmetic and copies ran while one was open for 0% of the time, Pallas kernels for 25%

profile of v1, /device:TPU:0, one launch (start us, length us, event | category | flops | bytes accessed | tf_op | source)
XLA Modules:
  0.0 116.1 jit_solution(18020561140650808684)
XLA Ops:
  0.7 1.0 cut_piece.1
  1.7 3.0 %collective-permute-start = (bf16[5,64,512]{2,1,0:T(8,128)(2,1)S(1)}, bf16[5,64,512]{2,1,0:T(8,128)(2,1)S(1)}, u32[]{:S(2)}, u32[]{:S(2)}) collective-permute-start(bf16[5,64,512]{2,1,0:T(8,128)(2,1)S(1)} %cut_piece.1), channel_id=1, source_target_pairs={{0,1},{1,0},{2,3},{3,2},{4,5},{5,4},{6,7},{7,6},{8,9},{9,8},{10,11... | collective-permute-start | bytes 983048 | tf_op jit(solution)/shard_map/ppermute | solution.py:68
  4.7 3.5 %load.1 = (bf16[2,640,512]{2,1,0:T(8,128)(2,1)S(1)}, bf16[5,512,512]{2,1,0:T(8,128)(2,1)S(1)}, bf16[512,2048]{1,0:T(8,128)(2,1)S(1)}, bf16[336,512]{1,0:T(8,128)(2,1)S(1)}) custom-call(s32[5]{0:T(128)S(1)} %copy-done, bf16[2048,512]{1,0:T(8,128)(2,1)} %x_hbm.1, bf16[5,512,512]{2,1,0:T(8,128)(2,1)} %weight_hbm.3, bf16[512,2048]{1,0:T(8,128)(2,1)} %w_in_hbm.1), custom_call_target="tpu_custom_call" | custom-call | bytes 1 | tf_op jit(solution)/shard_map/load/pallas_call | solution.py:921
  8.2 4.2 %collective-permute-done._ = bf16[5,64,512]{2,1,0:T(8,128)(2,1)S(1)} collective-permute-done((bf16[5,64,512]{2,1,0:T(8,128)(2,1)S(1)}, bf16[5,64,512]{2,1,0:T(8,128)(2,1)S(1)}, u32[]{:S(2)}, u32[]{:S(2)}) %collective-permute-start) | collective-permute-done | bytes 327712 | tf_op jit(solution)/shard_map/ppermute | solution.py:68
  12.4 1.8 %collective-permute-start.2 = (bf16[5,64,512]{2,1,0:T(8,128)(2,1)S(1)}, bf16[5,64,512]{2,1,0:T(8,128)(2,1)S(1)}, u32[]{:S(2)}, u32[]{:S(2)}) collective-permute-start(bf16[5,64,512]{2,1,0:T(8,128)(2,1)S(1)} %after.9._.token.refs_14_), channel_id=1, source_target_pairs={{0,8},{2,10},{4,12},{6,14},{8,0},{10,2},{12,4},{14,6},{16,24},{18,... | collective-permute-start | bytes 983048 | tf_op jit(solution)/shard_map/ppermute | solution.py:64
  14.2 1.5 %collective-permute-start.1 = (bf16[5,64,512]{2,1,0:T(8,128)(2,1)S(1)}, bf16[5,64,512]{2,1,0:T(8,128)(2,1)S(1)}, u32[]{:S(2)}, u32[]{:S(2)}) collective-permute-start(bf16[5,64,512]{2,1,0:T(8,128)(2,1)S(1)} %after.9._.token.refs_14_), channel_id=1, source_target_pairs={{0,4},{2,6},{4,0},{6,2},{8,12},{10,14},{12,8},{14,10},{16,20},{18,... | collective-permute-start | bytes 983048 | tf_op jit(solution)/shard_map/ppermute | solution.py:64
  15.7 1.5 %collective-permute-start.3 = (bf16[336,512]{1,0:T(8,128)(2,1)S(1)}, bf16[336,512]{1,0:T(8,128)(2,1)S(1)}, u32[]{:S(2)}, u32[]{:S(2)}) collective-permute-start(bf16[336,512]{1,0:T(8,128)(2,1)S(1)} %after.10), channel_id=1, source_target_pairs={{0,1},{1,0},{2,3},{3,2},{4,5},{5,4},{6,7},{7,6},{8,9},{9,8},{10,11... | collective-permute-start | bytes 1032200 | tf_op jit(solution)/shard_map/ppermute | solution.py:68
  17.2 3.4 %own_conv.1 = (f32[1024,512]{1,0:T(8,128)S(1)}, f32[8,128]{1,0:T(8,128)S(1)}) custom-call(s32[5]{0:T(128)S(1)} %copy-done, bf16[2,640,512]{2,1,0:T(8,128)(2,1)S(1)} %get-tuple-element.79.token.x_pad.refs_2_, bf16[5,512,512]{2,1,0:T(8,128)(2,1)S(1)} %get-tuple-element.80.weight, bf16[5,64,512]{2,1,0:T(8,128)(2,1)S(1)} %after.9._.token.refs_14_), custom_call_target="tpu_custom_call" | custom-call | bytes 1 | tf_op jit(solution)/shard_map/own_conv/pallas_call | solution.py:937
  21.3 1.2 %collective-permute-done.1.over_one = bf16[5,64,512]{2,1,0:T(8,128)(2,1)S(1)} collective-permute-done((bf16[5,64,512]{2,1,0:T(8,128)(2,1)S(1)}, bf16[5,64,512]{2,1,0:T(8,128)(2,1)S(1)}, u32[]{:S(2)}, u32[]{:S(2)}) %collective-permute-start.1) | collective-permute-done | bytes 327712 | tf_op jit(solution)/shard_map/ppermute | solution.py:64
  22.6 1.5 %collective-permute-done.3.refs_16_ = bf16[336,512]{1,0:T(8,128)(2,1)S(1)} collective-permute-done((bf16[336,512]{1,0:T(8,128)(2,1)S(1)}, bf16[336,512]{1,0:T(8,128)(2,1)S(1)}, u32[]{:S(2)}, u32[]{:S(2)}) %collective-permute-start.3) | collective-permute-done | bytes 344096 | tf_op jit(solution)/shard_map/ppermute | solution.py:68
  24.6 1.6 %collective-permute-done.4.refs_17_ = bf16[5,64,512]{2,1,0:T(8,128)(2,1)S(1)} collective-permute-done((bf16[5,64,512]{2,1,0:T(8,128)(2,1)S(1)}, bf16[5,64,512]{2,1,0:T(8,128)(2,1)S(1)}, u32[]{:S(2)}, u32[]{:S(2)}) %collective-permute-start.4) | collective-permute-done | bytes 327712 | tf_op jit(solution)/shard_map/ppermute | solution.py:64
  26.3 22.7 %main_rows.1 = (bf16[1024,512]{1,0:T(8,128)(2,1)}, f32[1024,512]{1,0:T(8,128)S(1)}, f32[1024,512]{1,0:T(8,128)S(1)}, bf16[1024,2048]{1,0:T(8,128)(2,1)S(1)}, bf1...) custom-call(s32[4]{0:T(128)} %species.1, ...), custom_call_target="tpu_custom_call" | custom-call | bytes 1 | tf_op jit(solution)/shard_map/main_rows/pallas_call | solution.py:950
  49.2 3.9 %back_rows.1 = (bf16[2,640,512]{2,1,0:T(8,128)(2,1)S(1)}, f32[1024,512]{1,0:T(8,128)S(1)}, f32[16,512]{1,0:T(8,128)S(1)}) custom-call(s32[4]{0:T(128)S(1)} %copy-done.3, s32[16]{0:T(128)S(1)} %copy-done.4, bf16[1024,512]{1,0:T(8,128)(2,1)S(1)} %get-tuple-element.87.grad_in, bf16[512,2048]{1,0:T(8,128)(2,1)S(1)} %get-tuple-element.82.refs_5_.w_in, ...), custom_call_target="tpu_custom_call" | custom-call | bytes 1 | tf_op jit(solution)/shard_map/back_rows/pallas_call | solution.py:1003
  53.7 1.0 collective-permute-start.10
  54.8 1.5 %collective-permute-start.9 = (bf16[512,512]{1,0:T(8,128)(2,1)S(1)}, bf16[512,512]{1,0:T(8,128)(2,1)S(1)}, u32[]{:S(2)}, u32[]{:S(2)}) collective-permute-start(bf16[512,512]{1,0:T(8,128)(2,1)S(1)} %get-tuple-element.97.refs_0_), channel_id=1, source_target_pairs={{0,1},{1,0},{2,3},{3,2},{4,5},{5,4},{6,7},{7,6},{8,9},{9,8},{10,11... | collective-permute-start | bytes 1572872 | tf_op jit(solution)/shard_map/ppermute | solution.py:819
  56.3 5.1 %terms_a.1 = (f32[1536,512]{1,0:T(8,128)S(1)}, bf16[1536,512]{1,0:T(8,128)(2,1)S(1)}) custom-call(s32[5]{0:T(128)S(1)} %copy-done, s32[5]{0:T(128)S(1)} %copy-done.2, bf16[2,640,512]{2,1,0:T(8,128)(2,1)S(1)} %get-tuple-element.79.token.x_pad.refs_2_, bf16[2,640,512]{2,1,0:T(8,128)(2,1)S(1)} %get-tuple-element.92.d_pad, ...), custom_call_target="tpu_custom_call" | custom-call | bytes 1 | tf_op jit(solution)/shard_map/terms_a/pallas_call | solution.py:1035
  61.5 3.8 %terms_b.1 = (f32[1024,512]{1,0:T(8,128)S(1)}, bf16[1056,512]{1,0:T(8,128)(2,1)S(1)}) custom-call(s32[5]{0:T(128)S(1)} %copy-done, s32[5]{0:T(128)S(1)} %copy-done.2, bf16[2,640,512]{2,1,0:T(8,128)(2,1)S(1)} %get-tuple-element.79.token.x_pad.refs_2_, bf16[2,640,512]{2,1,0:T(8,128)(2,1)S(1)} %get-tuple-element.92.d_pad, ...), custom_call_target="tpu_custom_call" | custom-call | bytes 1 | tf_op jit(solution)/shard_map/terms_b/pallas_call | solution.py:1035
  65.8 2.1 %collective-permute-done.10.refs_1_ = bf16[512,512]{1,0:T(8,128)(2,1)S(1)} collective-permute-done((bf16[512,512]{1,0:T(8,128)(2,1)S(1)}, bf16[512,512]{1,0:T(8,128)(2,1)S(1)}, u32[]{:S(2)}, u32[]{:S(2)}) %collective-permute-start.10) | collective-permute-done | bytes 524320 | tf_op jit(solution)/shard_map/ppermute | solution.py:819
  68.8 1.1 collective-permute-start.12
  69.9 1.5 %collective-permute-start.13 = (bf16[256,512]{1,0:T(8,128)(2,1)S(1)}, bf16[256,512]{1,0:T(8,128)(2,1)S(1)}, u32[]{:S(2)}, u32[]{:S(2)}) collective-permute-start(bf16[256,512]{1,0:T(8,128)(2,1)S(1)} %get-tuple-element.108), channel_id=1, source_target_pairs={{0,1},{1,0},{2,3},{3,2},{4,5},{5,4},{6,7},{7,6},{8,9},{9,8},{10,11... | collective-permute-start | bytes 786440 | tf_op jit(solution)/shard_map/ppermute | solution.py:819
  72.2 3.4 %input_near.1.refs_3_.base = f32[1024,512]{1,0:T(8,128)S(1)} custom-call(s32[5]{0:T(128)S(1)} %copy-done, bf16[2,640,512]{2,1,0:T(8,128)(2,1)S(1)} %get-tuple-element.92.d_pad, f32[1024,512]{1,0:T(8,128)S(1)} %get-tuple-element.93.base, bf16[5,512,512]{2,1,0:T(8,128)(2,1)S(1)} %get-tuple-element.80.weight, f32[512,512]{1,0:T(8,128)S(1)} %get-tuple-element.104._.refs_4_), custom_call_target="tpu_custom_call" | custom-call | bytes 1 | tf_op jit(solution)/shard_map/input_near/pallas_call | solution.py:1080
  77.4 1.6 %collective-permute-start.14 = (bf16[384,512]{1,0:T(8,128)(2,1)S(1)}, bf16[384,512]{1,0:T(8,128)(2,1)S(1)}, u32[]{:S(2)}, u32[]{:S(2)}) collective-permute-start(bf16[384,512]{1,0:T(8,128)(2,1)S(1)} %get-tuple-element.112), channel_id=1, source_target_pairs={{0,1},{1,0},{2,3},{3,2},{4,5},{5,4},{6,7},{7,6},{8,9},{9,8},{10,11... | collective-permute-start | bytes 1179656 | tf_op jit(solution)/shard_map/ppermute | solution.py:819
  80.4 4.4 %input_far.1 = (f32[1024,512]{1,0:T(8,128)}, f32[8,128]{1,0:T(8,128)S(1)}) custom-call(s32[5]{0:T(128)S(1)} %copy-done.2, bf16[2,640,512]{2,1,0:T(8,128)(2,1)S(1)} %get-tuple-element.92.d_pad, f32[1024,512]{1,0:T(8,128)S(1)} %input_near.1.refs_3_.base, bf16[5,512,512]{2,1,0:T(8,128)(2,1)S(1)} %get-tuple-element.105.weight, ...), custom_call_target="tpu_custom_call" | custom-call | bytes 1 | tf_op jit(solution)/shard_map/input_far/pallas_call | solution.py:1098
  84.9 5.7 %collective-permute-done.17.refs_0_ = bf16[256,512]{1,0:T(8,128)(2,1)S(1)} collective-permute-done((bf16[256,512]{1,0:T(8,128)(2,1)S(1)}, bf16[256,512]{1,0:T(8,128)(2,1)S(1)}, u32[]{:S(2)}, u32[]{:S(2)}) %collective-permute-start.17) | collective-permute-done | bytes 262176 | tf_op jit(solution)/shard_map/ppermute | solution.py:819
  92.4 2.6 %collective-permute-start.23 = (bf16[128,512]{1,0:T(8,128)(2,1)S(1)}, bf16[128,512]{1,0:T(8,128)(2,1)S(1)}, u32[]{:S(2)}, u32[]{:S(2)}) collective-permute-start(bf16[128,512]{1,0:T(8,128)(2,1)S(1)} %get-tuple-element.130), channel_id=1, source_target_pairs={{0,16},{1,17},{2,18},{3,19},{4,20},{5,21},{6,22},{7,23},{8,24},{9,... | collective-permute-start | bytes 393224 | tf_op jit(solution)/shard_map/ppermute | solution.py:819
  95.0 3.5 %collective-permute-done.18.refs_0_ = bf16[320,512]{1,0:T(8,128)(2,1)S(1)} collective-permute-done((bf16[320,512]{1,0:T(8,128)(2,1)S(1)}, bf16[320,512]{1,0:T(8,128)(2,1)S(1)}, u32[]{:S(2)}, u32[]{:S(2)}) %collective-permute-start.18) | collective-permute-done | bytes 327712 | tf_op jit(solution)/shard_map/ppermute | solution.py:819
  100.4 1.5 %collective-permute-start.22 = (bf16[64,512]{1,0:T(8,128)(2,1)S(1)}, bf16[64,512]{1,0:T(8,128)(2,1)S(1)}, u32[]{:S(2)}, u32[]{:S(2)}) collective-permute-start(bf16[64,512]{1,0:T(8,128)(2,1)S(1)} %get-tuple-element.127), channel_id=1, source_target_pairs={{0,1},{1,0},{2,3},{3,2},{4,5},{5,4},{6,7},{7,6},{8,9},{9,8},{10,11... | collective-permute-start | bytes 196616 | tf_op jit(solution)/shard_map/ppermute | solution.py:819
  101.9 1.0 collective-permute-start.21
  102.9 1.7 %collective-permute-done.22.refs_2_ = bf16[64,512]{1,0:T(8,128)(2,1)S(1)} collective-permute-done((bf16[64,512]{1,0:T(8,128)(2,1)S(1)}, bf16[64,512]{1,0:T(8,128)(2,1)S(1)}, u32[]{:S(2)}, u32[]{:S(2)}) %collective-permute-start.22) | collective-permute-done | bytes 65568 | tf_op jit(solution)/shard_map/ppermute | solution.py:819
  104.7 1.8 %collective-permute-done.21.refs_1_ = bf16[96,512]{1,0:T(8,128)(2,1)S(1)} collective-permute-done((bf16[96,512]{1,0:T(8,128)(2,1)S(1)}, bf16[96,512]{1,0:T(8,128)(2,1)S(1)}, u32[]{:S(2)}, u32[]{:S(2)}) %collective-permute-start.21) | collective-permute-done | bytes 98336 | tf_op jit(solution)/shard_map/ppermute | solution.py:819
  106.6 2.7 %collective-permute-start.24 = (bf16[192,512]{1,0:T(8,128)(2,1)S(1)}, bf16[192,512]{1,0:T(8,128)(2,1)S(1)}, u32[]{:S(2)}, u32[]{:S(2)}) collective-permute-start(bf16[192,512]{1,0:T(8,128)(2,1)S(1)} %get-tuple-element.132), channel_id=1, source_target_pairs={{0,16},{1,17},{2,18},{3,19},{4,20},{5,21},{6,22},{7,23},{8,24},{9,... | collective-permute-start | bytes 589832 | tf_op jit(solution)/shard_map/ppermute | solution.py:819
  109.2 6.1 %collective-permute-done.24.got = bf16[192,512]{1,0:T(8,128)(2,1)S(1)} collective-permute-done((bf16[192,512]{1,0:T(8,128)(2,1)S(1)}, bf16[192,512]{1,0:T(8,128)(2,1)S(1)}, u32[]{:S(2)}, u32[]{:S(2)}) %collective-permute-start.24) | collective-permute-done | bytes 196640 | tf_op jit(solution)/shard_map/ppermute | solution.py:819
  (61 shorter events, 12.1 us)
Async XLA Ops:
  0.6 4.0 %copy-start = (s32[5]{0:T(128)S(1)}, s32[5]{0:T(128)}, u32[]{:S(2)}) copy-start(s32[5]{0:T(128)} %table.5) | copy-start | bytes 64
  1.7 10.7 %collective-permute-start = (bf16[5,64,512]{2,1,0:T(8,128)(2,1)S(1)}, bf16[5,64,512]{2,1,0:T(8,128)(2,1)S(1)}, u32[]{:S(2)}, u32[]{:S(2)}) collective-permute-start(bf16[5,64,512]{2,1,0:T(8,128)(2,1)S(1)} %cut_piece.1), channel_id=1, source_target_pairs={{0,1},{1,0},{2,3},{3,2},{4,5},{5,4},{6,7},{7,6},{8,9},{9,8},{10,11... | collective-permute-start | bytes 983048 | tf_op jit(solution)/shard_map/ppermute | solution.py:68
  12.4 8.9 %collective-permute-start.2 = (bf16[5,64,512]{2,1,0:T(8,128)(2,1)S(1)}, bf16[5,64,512]{2,1,0:T(8,128)(2,1)S(1)}, u32[]{:S(2)}, u32[]{:S(2)}) collective-permute-start(bf16[5,64,512]{2,1,0:T(8,128)(2,1)S(1)} %after.9._.token.refs_14_), channel_id=1, source_target_pairs={{0,8},{2,10},{4,12},{6,14},{8,0},{10,2},{12,4},{14,6},{16,24},{18,... | collective-permute-start | bytes 983048 | tf_op jit(solution)/shard_map/ppermute | solution.py:64
  14.2 8.3 %collective-permute-start.1 = (bf16[5,64,512]{2,1,0:T(8,128)(2,1)S(1)}, bf16[5,64,512]{2,1,0:T(8,128)(2,1)S(1)}, u32[]{:S(2)}, u32[]{:S(2)}) collective-permute-start(bf16[5,64,512]{2,1,0:T(8,128)(2,1)S(1)} %after.9._.token.refs_14_), channel_id=1, source_target_pairs={{0,4},{2,6},{4,0},{6,2},{8,12},{10,14},{12,8},{14,10},{16,20},{18,... | collective-permute-start | bytes 983048 | tf_op jit(solution)/shard_map/ppermute | solution.py:64
  15.7 8.4 %collective-permute-start.3 = (bf16[336,512]{1,0:T(8,128)(2,1)S(1)}, bf16[336,512]{1,0:T(8,128)(2,1)S(1)}, u32[]{:S(2)}, u32[]{:S(2)}) collective-permute-start(bf16[336,512]{1,0:T(8,128)(2,1)S(1)} %after.10), channel_id=1, source_target_pairs={{0,1},{1,0},{2,3},{3,2},{4,5},{5,4},{6,7},{7,6},{8,9},{9,8},{10,11... | collective-permute-start | bytes 1032200 | tf_op jit(solution)/shard_map/ppermute | solution.py:68
  22.6 3.7 %collective-permute-start.5 = (bf16[10,64,512]{2,1,0:T(8,128)(2,1)S(1)}, bf16[10,64,512]{2,1,0:T(8,128)(2,1)S(1)}, u32[]{:S(2)}, u32[]{:S(2)}) collective-permute-start(bf16[10,64,512]{2,1,0:T(8,128)(2,1)S(1)} %both.1.refs_15_), channel_id=1, source_target_pairs={{0,2},{2,0},{4,6},{6,4},{8,10},{10,8},{12,14},{14,12},{16,18},{18,... | collective-permute-start | bytes 1966088 | tf_op jit(solution)/shard_map/ppermute | solution.py:64
  24.1 2.1 %collective-permute-start.6 = (bf16[336,512]{1,0:T(8,128)(2,1)S(1)}, bf16[336,512]{1,0:T(8,128)(2,1)S(1)}, u32[]{:S(2)}, u32[]{:S(2)}) collective-permute-start(bf16[336,512]{1,0:T(8,128)(2,1)S(1)} %collective-permute-done.3.refs_16_), channel_id=1, source_target_pairs={{0,2},{2,0},{4,6},{6,4},{8,10},{10,8},{12,14},{14,12},{16,18},{18,... | collective-permute-start | bytes 1032200 | tf_op jit(solution)/shard_map/ppermute | solution.py:64
  24.1 2.1 %collective-permute-start.4 = (bf16[5,64,512]{2,1,0:T(8,128)(2,1)S(1)}, bf16[5,64,512]{2,1,0:T(8,128)(2,1)S(1)}, u32[]{:S(2)}, u32[]{:S(2)}) collective-permute-start(bf16[5,64,512]{2,1,0:T(8,128)(2,1)S(1)} %after.9._.token.refs_14_), channel_id=1, source_target_pairs={{0,2},{2,0},{4,6},{6,4},{8,10},{10,8},{12,14},{14,12},{16,18},{18,... | collective-permute-start | bytes 983048 | tf_op jit(solution)/shard_map/ppermute | solution.py:64
  26.2 23.0 %copy-start.1 = (f32[512]{0:T(512)S(1)}, f32[512]{0:T(512)}, u32[]{:S(2)}) copy-start(f32[512]{0:T(512)} %param.19) | copy-start | bytes 6148
  26.2 23.0 %copy-start.3 = (s32[4]{0:T(128)S(1)}, s32[4]{0:T(128)}, u32[]{:S(2)}) copy-start(s32[4]{0:T(128)} %species.1) | copy-start | bytes 52
  26.3 23.0 %copy-start.4 = (s32[16]{0:T(128)S(1)}, s32[16]{0:T(128)}, u32[]{:S(2)}) copy-start(s32[16]{0:T(128)} %counts.1) | copy-start | bytes 196
  49.0 4.2 %collective-permute-start.7 = (bf16[2048,512]{1,0:T(8,128)(2,1)S(1)}, bf16[2048,512]{1,0:T(8,128)(2,1)S(1)}, u32[]{:S(2)}, u32[]{:S(2)}) collective-permute-start(bf16[2048,512]{1,0:T(8,128)(2,1)S(1)} %get-tuple-element.95), channel_id=1, source_target_pairs={{0,2},{2,0},{4,6},{6,4},{8,10},{10,8},{12,14},{14,12},{16,18},{18,... | collective-permute-start | bytes 6291464 | tf_op jit(solution)/shard_map/ppermute | solution.py:64
  53.2 3.0 %copy-start.2 = (s32[5]{0:T(128)S(1)}, s32[5]{0:T(128)}, u32[]{:S(2)}) copy-start(s32[5]{0:T(128)} %get-tuple-element.86.other_table.table) | copy-start | bytes 64
  53.7 14.2 %collective-permute-start.10 = (bf16[512,512]{1,0:T(8,128)(2,1)S(1)}, bf16[512,512]{1,0:T(8,128)(2,1)S(1)}, u32[]{:S(2)}, u32[]{:S(2)}) collective-permute-start(bf16[512,512]{1,0:T(8,128)(2,1)S(1)} %get-tuple-element.101), channel_id=1, source_target_pairs={{0,4},{1,5},{2,6},{3,7},{4,0},{5,1},{6,2},{7,3},{8,12},{9,13},{10,... | collective-permute-start | bytes 1572872 | tf_op jit(solution)/shard_map/ppermute | solution.py:819
  54.8 13.9 %collective-permute-start.9 = (bf16[512,512]{1,0:T(8,128)(2,1)S(1)}, bf16[512,512]{1,0:T(8,128)(2,1)S(1)}, u32[]{:S(2)}, u32[]{:S(2)}) collective-permute-start(bf16[512,512]{1,0:T(8,128)(2,1)S(1)} %get-tuple-element.97.refs_0_), channel_id=1, source_target_pairs={{0,1},{1,0},{2,3},{3,2},{4,5},{5,4},{6,7},{7,6},{8,9},{9,8},{10,11... | collective-permute-start | bytes 1572872 | tf_op jit(solution)/shard_map/ppermute | solution.py:819
  61.4 15.8 %collective-permute-start.11 = (bf16[1536,512]{1,0:T(8,128)(2,1)S(1)}, bf16[1536,512]{1,0:T(8,128)(2,1)S(1)}, u32[]{:S(2)}, u32[]{:S(2)}) collective-permute-start(bf16[1536,512]{1,0:T(8,128)(2,1)S(1)} %get-tuple-element.106), channel_id=1, source_target_pairs={{0,2},{2,0},{4,6},{6,4},{8,10},{10,8},{12,14},{14,12},{16,18},{18,... | collective-permute-start | bytes 4718600 | tf_op jit(solution)/shard_map/ppermute | solution.py:64
  65.3 6.1 %collective-permute-start.8 = (bf16[1056,512]{1,0:T(8,128)(2,1)S(1)}, bf16[1056,512]{1,0:T(8,128)(2,1)S(1)}, u32[]{:S(2)}, u32[]{:S(2)}) collective-permute-start(bf16[1056,512]{1,0:T(8,128)(2,1)S(1)} %get-tuple-element.99), channel_id=1, source_target_pairs={{0,2},{2,0},{4,6},{6,4},{8,10},{10,8},{12,14},{14,12},{16,18},{18,... | collective-permute-start | bytes 3244040 | tf_op jit(solution)/shard_map/ppermute | solution.py:64
  68.8 7.5 %collective-permute-start.12 = (bf16[256,512]{1,0:T(8,128)(2,1)S(1)}, bf16[256,512]{1,0:T(8,128)(2,1)S(1)}, u32[]{:S(2)}, u32[]{:S(2)}) collective-permute-start(bf16[256,512]{1,0:T(8,128)(2,1)S(1)} %get-tuple-element.107), channel_id=1, source_target_pairs={{0,4},{1,5},{2,6},{3,7},{4,0},{5,1},{6,2},{7,3},{8,12},{9,13},{10,... | collective-permute-start | bytes 786440 | tf_op jit(solution)/shard_map/ppermute | solution.py:819
  69.9 7.1 %collective-permute-start.13 = (bf16[256,512]{1,0:T(8,128)(2,1)S(1)}, bf16[256,512]{1,0:T(8,128)(2,1)S(1)}, u32[]{:S(2)}, u32[]{:S(2)}) collective-permute-start(bf16[256,512]{1,0:T(8,128)(2,1)S(1)} %get-tuple-element.108), channel_id=1, source_target_pairs={{0,1},{1,0},{2,3},{3,2},{4,5},{5,4},{6,7},{7,6},{8,9},{9,8},{10,11... | collective-permute-start | bytes 786440 | tf_op jit(solution)/shard_map/ppermute | solution.py:819
  71.7 18.9 %collective-permute-start.16 = (bf16[544,512]{1,0:T(8,128)(2,1)S(1)}, bf16[544,512]{1,0:T(8,128)(2,1)S(1)}, u32[]{:S(2)}, u32[]{:S(2)}) collective-permute-start(bf16[544,512]{1,0:T(8,128)(2,1)S(1)} %get-tuple-element.114), channel_id=1, source_target_pairs={{0,8},{1,9},{2,10},{3,11},{4,12},{5,13},{6,14},{7,15},{8,0},{9,1},... | collective-permute-start | bytes 1671176 | tf_op jit(solution)/shard_map/ppermute | solution.py:819
  77.4 13.2 %collective-permute-start.14 = (bf16[384,512]{1,0:T(8,128)(2,1)S(1)}, bf16[384,512]{1,0:T(8,128)(2,1)S(1)}, u32[]{:S(2)}, u32[]{:S(2)}) collective-permute-start(bf16[384,512]{1,0:T(8,128)(2,1)S(1)} %get-tuple-element.112), channel_id=1, source_target_pairs={{0,1},{1,0},{2,3},{3,2},{4,5},{5,4},{6,7},{7,6},{8,9},{9,8},{10,11... | collective-permute-start | bytes 1179656 | tf_op jit(solution)/shard_map/ppermute | solution.py:819
  79.0 11.6 %collective-permute-start.15 = (bf16[384,512]{1,0:T(8,128)(2,1)S(1)}, bf16[384,512]{1,0:T(8,128)(2,1)S(1)}, u32[]{:S(2)}, u32[]{:S(2)}) collective-permute-start(bf16[384,512]{1,0:T(8,128)(2,1)S(1)} %get-tuple-element.113), channel_id=1, source_target_pairs={{0,4},{1,5},{2,6},{3,7},{4,0},{5,1},{6,2},{7,3},{8,12},{9,13},{10,... | collective-permute-start | bytes 1179656 | tf_op jit(solution)/shard_map/ppermute | solution.py:819
  79.9 10.6 %collective-permute-start.17 = (bf16[256,512]{1,0:T(8,128)(2,1)S(1)}, bf16[256,512]{1,0:T(8,128)(2,1)S(1)}, u32[]{:S(2)}, u32[]{:S(2)}) collective-permute-start(bf16[256,512]{1,0:T(8,128)(2,1)S(1)} %get-tuple-element.117), channel_id=1, source_target_pairs={{0,8},{1,9},{2,10},{3,11},{4,12},{5,13},{6,14},{7,15},{8,0},{9,1},... | collective-permute-start | bytes 786440 | tf_op jit(solution)/shard_map/ppermute | solution.py:819
  90.8 8.1 %collective-permute-start.19 = (bf16[352,512]{1,0:T(8,128)(2,1)S(1)}, bf16[352,512]{1,0:T(8,128)(2,1)S(1)}, u32[]{:S(2)}, u32[]{:S(2)}) collective-permute-start(bf16[352,512]{1,0:T(8,128)(2,1)S(1)} %get-tuple-element.120), channel_id=1, source_target_pairs={{0,1},{1,0},{2,3},{3,2},{4,5},{5,4},{6,7},{7,6},{8,9},{9,8},{10,11... | collective-permute-start | bytes 1081352 | tf_op jit(solution)/shard_map/ppermute | solution.py:819
  91.4 7.1 %collective-permute-start.18 = (bf16[320,512]{1,0:T(8,128)(2,1)S(1)}, bf16[320,512]{1,0:T(8,128)(2,1)S(1)}, u32[]{:S(2)}, u32[]{:S(2)}) collective-permute-start(bf16[320,512]{1,0:T(8,128)(2,1)S(1)} %get-tuple-element.119), channel_id=1, source_target_pairs={{0,4},{1,5},{2,6},{3,7},{4,0},{5,1},{6,2},{7,3},{8,12},{9,13},{10,... | collective-permute-start | bytes 983048 | tf_op jit(solution)/shard_map/ppermute | solution.py:819
  92.4 7.3 %collective-permute-start.23 = (bf16[128,512]{1,0:T(8,128)(2,1)S(1)}, bf16[128,512]{1,0:T(8,128)(2,1)S(1)}, u32[]{:S(2)}, u32[]{:S(2)}) collective-permute-start(bf16[128,512]{1,0:T(8,128)(2,1)S(1)} %get-tuple-element.130), channel_id=1, source_target_pairs={{0,16},{1,17},{2,18},{3,19},{4,20},{5,21},{6,22},{7,23},{8,24},{9,... | collective-permute-start | bytes 393224 | tf_op jit(solution)/shard_map/ppermute | solution.py:819
  99.0 7.5 %collective-permute-start.20 = (bf16[192,512]{1,0:T(8,128)(2,1)S(1)}, bf16[192,512]{1,0:T(8,128)(2,1)S(1)}, u32[]{:S(2)}, u32[]{:S(2)}) collective-permute-start(bf16[192,512]{1,0:T(8,128)(2,1)S(1)} %get-tuple-element.122), channel_id=1, source_target_pairs={{0,8},{1,9},{2,10},{3,11},{4,12},{5,13},{6,14},{7,15},{8,0},{9,1},... | collective-permute-start | bytes 589832 | tf_op jit(solution)/shard_map/ppermute | solution.py:819
  100.4 4.3 %collective-permute-start.22 = (bf16[64,512]{1,0:T(8,128)(2,1)S(1)}, bf16[64,512]{1,0:T(8,128)(2,1)S(1)}, u32[]{:S(2)}, u32[]{:S(2)}) collective-permute-start(bf16[64,512]{1,0:T(8,128)(2,1)S(1)} %get-tuple-element.127), channel_id=1, source_target_pairs={{0,1},{1,0},{2,3},{3,2},{4,5},{5,4},{6,7},{7,6},{8,9},{9,8},{10,11... | collective-permute-start | bytes 196616 | tf_op jit(solution)/shard_map/ppermute | solution.py:819
  101.9 4.6 %collective-permute-start.21 = (bf16[96,512]{1,0:T(8,128)(2,1)S(1)}, bf16[96,512]{1,0:T(8,128)(2,1)S(1)}, u32[]{:S(2)}, u32[]{:S(2)}) collective-permute-start(bf16[96,512]{1,0:T(8,128)(2,1)S(1)} %get-tuple-element.126), channel_id=1, source_target_pairs={{0,4},{1,5},{2,6},{3,7},{4,0},{5,1},{6,2},{7,3},{8,12},{9,13},{10,... | collective-permute-start | bytes 294920 | tf_op jit(solution)/shard_map/ppermute | solution.py:819
  106.6 8.7 %collective-permute-start.24 = (bf16[192,512]{1,0:T(8,128)(2,1)S(1)}, bf16[192,512]{1,0:T(8,128)(2,1)S(1)}, u32[]{:S(2)}, u32[]{:S(2)}) collective-permute-start(bf16[192,512]{1,0:T(8,128)(2,1)S(1)} %get-tuple-element.132), channel_id=1, source_target_pairs={{0,16},{1,17},{2,18},{3,19},{4,20},{5,21},{6,22},{7,23},{8,24},{9,... | collective-permute-start | bytes 589832 | tf_op jit(solution)/shard_map/ppermute | solution.py:819

commit v2 on v1

--- a/solution.py
+++ b/solution.py
@@ -1106,11 +1106,6 @@
         name="input_far",
     )(other_table, near(d_pad), near(partial), near(other_weight), near(flow_a["keep"]))
     mark = spaced(mark)
-    size = half_of(flow_f)
-    plan = dict(ins=joined(0, flow_f), outs=[(0, 0), (0, size)])
-    sends = fused_step([got_f], [flow_f], [plan], [2 * size], mark)
-    got_f = swap(sends[0], over_zz)
-    mark = spaced(flow_f["keep"])
     size, size_b = half_of(flow_a), half_of(flow_b)
     plan = dict(ins=[(0, 0), (1, 0)], outs=[(0, 0), (1, 0)])
     plan_b = dict(
@@ -1127,8 +1122,13 @@
         mark,
     )
     gots = [swap(sends[0], over_y), swap(sends[1], over_x)]
+    shift = size
     mark = spaced(flow_a["keep"])
-    shift = size
+    size = half_of(flow_f)
+    plan = dict(ins=joined(0, flow_f), outs=[(0, 0), (0, size)])
+    sends = fused_step([got_f], [flow_f], [plan], [2 * size], mark)
+    got_f = swap(sends[0], over_zz)
+    mark = spaced(flow_f["keep"])
     size = half_of(flow_a)
     plan = dict(ins=[(0, 0), (1, 0)], outs=[(0, 0), (0, size)])
     sends = fused_step(gots, [flow_a], [plan], [2 * size], mark)
@@ -1142,7 +1142,7 @@
     )
     sends = fused_step(gots, [flow_b], [plan], [size + extra, size], flow_a["keep"])
     gots_b = [swap(sends[0], over_y), swap(sends[1], over_x)]
-    mark = spaced(flow_b["keep"])
+    mark = flow_b["keep"]
     w_in_mine, w_out_mine, mark = pl.pallas_call(
         functools.partial(last_ffn_kernel, 1),
         out_shape=[

time: 116 us -> 114 us (0.983)
  waiting for transfers between devices: 32.7 us -> 30.7 us
    ppermute x15, waiting for transfers between devices: 23.5 us -> 21.4 us  [swap(): lax.ppermute(value, ('dp', 'tap'), [(i, i ^ mask) for i in range(count)])]
  transfers between devices with their start and end apart: 25 -> 25, of which waited for: 17 -> 18; matrix products, arithmetic and copies ran while one was open for 0% -> 0% of each run, Pallas kernels for 25% -> 26%
where the time goes in v2:
time: 114 us; the launch traced here: 113 us
  Pallas kernels  54.7 us (48%)
  waiting for transfers between devices  30.7 us (27%)
  starting transfers between devices  27.1 us (24%)
    pallas_call x1, Pallas kernels, fast_shards(): pl.pallas_call(functools.partial(main_kernel, orders, dp_bits, [turn for...  22.7 us
    ppermute x15, waiting for transfers between devices, swap(): lax.ppermute(value, ('dp', 'tap'), [(i, i ^ mask) for i in range(count)])  21.4 us
    ppermute x15, starting transfers between devices, swap(): lax.ppermute(value, ('dp', 'tap'), [(i, i ^ mask) for i in range(count)])  17.8 us
    pallas_call x2, Pallas kernels, terms(): pl.pallas_call(functools.partial(terms_kernel, group, orders, dp_bits, sm...  8.92 us
    ppermute x2, waiting for transfers between devices, swap_tap(): return lax.ppermute(value, 'tap', [(0, 1), (1, 0)])  5.68 us
    ppermute x8, starting transfers between devices, swap_dp(): return lax.ppermute(value, 'dp', [(i, i ^ 1 << bit) for i in range(count)])  4.78 us
    ppermute x2, starting transfers between devices, swap_tap(): return lax.ppermute(value, 'tap', [(0, 1), (1, 0)])  4.49 us
    pallas_call x1, Pallas kernels, fast_shards(): pl.pallas_call(input_far_kernel, out_shape=[pltpu.HBM(rows_f, F32), vmem(...  4.44 us
  transfers between devices with their start and end apart: 25, of which 18 were waited for; matrix products, arithmetic and copies ran while one was open for 0% of the time, Pallas kernels for 26%

profile of v2, /device:TPU:0, one launch (start us, length us, event | category | flops | bytes accessed | tf_op | source)
XLA Modules:
  0.0 113.4 jit_solution(1992220813152778504)
XLA Ops:
  0.7 1.0 cut_piece.1
  1.7 3.0 %collective-permute-start = (bf16[5,64,512]{2,1,0:T(8,128)(2,1)S(1)}, bf16[5,64,512]{2,1,0:T(8,128)(2,1)S(1)}, u32[]{:S(2)}, u32[]{:S(2)}) collective-permute-start(bf16[5,64,512]{2,1,0:T(8,128)(2,1)S(1)} %cut_piece.1), channel_id=1, source_target_pairs={{0,1},{1,0},{2,3},{3,2},{4,5},{5,4},{6,7},{7,6},{8,9},{9,8},{10,11... | collective-permute-start | bytes 983048 | tf_op jit(solution)/shard_map/ppermute | solution.py:68
  4.7 3.5 %load.1 = (bf16[2,640,512]{2,1,0:T(8,128)(2,1)S(1)}, bf16[5,512,512]{2,1,0:T(8,128)(2,1)S(1)}, bf16[512,2048]{1,0:T(8,128)(2,1)S(1)}, bf16[336,512]{1,0:T(8,128)(2,1)S(1)}) custom-call(s32[5]{0:T(128)S(1)} %copy-done, bf16[2048,512]{1,0:T(8,128)(2,1)} %x_hbm.1, bf16[5,512,512]{2,1,0:T(8,128)(2,1)} %weight_hbm.3, bf16[512,2048]{1,0:T(8,128)(2,1)} %w_in_hbm.1), custom_call_target="tpu_custom_call" | custom-call | bytes 1 | tf_op jit(solution)/shard_map/load/pallas_call | solution.py:921
  8.2 4.2 %collective-permute-done._ = bf16[5,64,512]{2,1,0:T(8,128)(2,1)S(1)} collective-permute-done((bf16[5,64,512]{2,1,0:T(8,128)(2,1)S(1)}, bf16[5,64,512]{2,1,0:T(8,128)(2,1)S(1)}, u32[]{:S(2)}, u32[]{:S(2)}) %collective-permute-start) | collective-permute-done | bytes 327712 | tf_op jit(solution)/shard_map/ppermute | solution.py:68
  12.4 1.8 %collective-permute-start.2 = (bf16[5,64,512]{2,1,0:T(8,128)(2,1)S(1)}, bf16[5,64,512]{2,1,0:T(8,128)(2,1)S(1)}, u32[]{:S(2)}, u32[]{:S(2)}) collective-permute-start(bf16[5,64,512]{2,1,0:T(8,128)(2,1)S(1)} %after.8._.token.refs_14_), channel_id=1, source_target_pairs={{0,8},{2,10},{4,12},{6,14},{8,0},{10,2},{12,4},{14,6},{16,24},{18,... | collective-permute-start | bytes 983048 | tf_op jit(solution)/shard_map/ppermute | solution.py:64
  14.2 1.5 %collective-permute-start.1 = (bf16[5,64,512]{2,1,0:T(8,128)(2,1)S(1)}, bf16[5,64,512]{2,1,0:T(8,128)(2,1)S(1)}, u32[]{:S(2)}, u32[]{:S(2)}) collective-permute-start(bf16[5,64,512]{2,1,0:T(8,128)(2,1)S(1)} %after.8._.token.refs_14_), channel_id=1, source_target_pairs={{0,4},{2,6},{4,0},{6,2},{8,12},{10,14},{12,8},{14,10},{16,20},{18,... | collective-permute-start | bytes 983048 | tf_op jit(solution)/shard_map/ppermute | solution.py:64
  15.7 1.5 %collective-permute-start.3 = (bf16[336,512]{1,0:T(8,128)(2,1)S(1)}, bf16[336,512]{1,0:T(8,128)(2,1)S(1)}, u32[]{:S(2)}, u32[]{:S(2)}) collective-permute-start(bf16[336,512]{1,0:T(8,128)(2,1)S(1)} %after.9), channel_id=1, source_target_pairs={{0,1},{1,0},{2,3},{3,2},{4,5},{5,4},{6,7},{7,6},{8,9},{9,8},{10,11... | collective-permute-start | bytes 1032200 | tf_op jit(solution)/shard_map/ppermute | solution.py:68
  17.2 3.4 %own_conv.1 = (f32[1024,512]{1,0:T(8,128)S(1)}, f32[8,128]{1,0:T(8,128)S(1)}) custom-call(s32[5]{0:T(128)S(1)} %copy-done, bf16[2,640,512]{2,1,0:T(8,128)(2,1)S(1)} %get-tuple-element.79.token.x_pad.refs_2_, bf16[5,512,512]{2,1,0:T(8,128)(2,1)S(1)} %get-tuple-element.80.weight, bf16[5,64,512]{2,1,0:T(8,128)(2,1)S(1)} %after.8._.token.refs_14_), custom_call_target="tpu_custom_call" | custom-call | bytes 1 | tf_op jit(solution)/shard_map/own_conv/pallas_call | solution.py:937
  21.3 1.2 %collective-permute-done.1.over_one = bf16[5,64,512]{2,1,0:T(8,128)(2,1)S(1)} collective-permute-done((bf16[5,64,512]{2,1,0:T(8,128)(2,1)S(1)}, bf16[5,64,512]{2,1,0:T(8,128)(2,1)S(1)}, u32[]{:S(2)}, u32[]{:S(2)}) %collective-permute-start.1) | collective-permute-done | bytes 327712 | tf_op jit(solution)/shard_map/ppermute | solution.py:64
  22.6 1.5 %collective-permute-done.3.refs_16_ = bf16[336,512]{1,0:T(8,128)(2,1)S(1)} collective-permute-done((bf16[336,512]{1,0:T(8,128)(2,1)S(1)}, bf16[336,512]{1,0:T(8,128)(2,1)S(1)}, u32[]{:S(2)}, u32[]{:S(2)}) %collective-permute-start.3) | collective-permute-done | bytes 344096 | tf_op jit(solution)/shard_map/ppermute | solution.py:68
  24.6 1.6 %collective-permute-done.4.refs_17_ = bf16[5,64,512]{2,1,0:T(8,128)(2,1)S(1)} collective-permute-done((bf16[5,64,512]{2,1,0:T(8,128)(2,1)S(1)}, bf16[5,64,512]{2,1,0:T(8,128)(2,1)S(1)}, u32[]{:S(2)}, u32[]{:S(2)}) %collective-permute-start.4) | collective-permute-done | bytes 327712 | tf_op jit(solution)/shard_map/ppermute | solution.py:64
  26.3 22.7 %main_rows.1 = (bf16[1024,512]{1,0:T(8,128)(2,1)}, f32[1024,512]{1,0:T(8,128)S(1)}, f32[1024,512]{1,0:T(8,128)S(1)}, bf16[1024,2048]{1,0:T(8,128)(2,1)S(1)}, bf1...) custom-call(s32[4]{0:T(128)} %species.1, ...), custom_call_target="tpu_custom_call" | custom-call | bytes 1 | tf_op jit(solution)/shard_map/main_rows/pallas_call | solution.py:950
  49.2 3.9 %back_rows.1 = (bf16[2,640,512]{2,1,0:T(8,128)(2,1)S(1)}, f32[1024,512]{1,0:T(8,128)S(1)}, f32[16,512]{1,0:T(8,128)S(1)}) custom-call(s32[4]{0:T(128)S(1)} %copy-done.3, s32[16]{0:T(128)S(1)} %copy-done.4, bf16[1024,512]{1,0:T(8,128)(2,1)S(1)} %get-tuple-element.87.grad_in, bf16[512,2048]{1,0:T(8,128)(2,1)S(1)} %get-tuple-element.82.refs_5_.w_in, ...), custom_call_target="tpu_custom_call" | custom-call | bytes 1 | tf_op jit(solution)/shard_map/back_rows/pallas_call | solution.py:1003
  53.7 1.0 collective-permute-start.10
  54.8 1.5 %collective-permute-start.9 = (bf16[512,512]{1,0:T(8,128)(2,1)S(1)}, bf16[512,512]{1,0:T(8,128)(2,1)S(1)}, u32[]{:S(2)}, u32[]{:S(2)}) collective-permute-start(bf16[512,512]{1,0:T(8,128)(2,1)S(1)} %get-tuple-element.97.refs_0_), channel_id=1, source_target_pairs={{0,1},{1,0},{2,3},{3,2},{4,5},{5,4},{6,7},{7,6},{8,9},{9,8},{10,11... | collective-permute-start | bytes 1572872 | tf_op jit(solution)/shard_map/ppermute | solution.py:819
  56.3 5.1 %terms_a.1 = (f32[1536,512]{1,0:T(8,128)S(1)}, bf16[1536,512]{1,0:T(8,128)(2,1)S(1)}) custom-call(s32[5]{0:T(128)S(1)} %copy-done, s32[5]{0:T(128)S(1)} %copy-done.2, bf16[2,640,512]{2,1,0:T(8,128)(2,1)S(1)} %get-tuple-element.79.token.x_pad.refs_2_, bf16[2,640,512]{2,1,0:T(8,128)(2,1)S(1)} %get-tuple-element.92.d_pad, ...), custom_call_target="tpu_custom_call" | custom-call | bytes 1 | tf_op jit(solution)/shard_map/terms_a/pallas_call | solution.py:1035
  61.5 3.8 %terms_b.1 = (f32[1024,512]{1,0:T(8,128)S(1)}, bf16[1056,512]{1,0:T(8,128)(2,1)S(1)}) custom-call(s32[5]{0:T(128)S(1)} %copy-done, s32[5]{0:T(128)S(1)} %copy-done.2, bf16[2,640,512]{2,1,0:T(8,128)(2,1)S(1)} %get-tuple-element.79.token.x_pad.refs_2_, bf16[2,640,512]{2,1,0:T(8,128)(2,1)S(1)} %get-tuple-element.92.d_pad, ...), custom_call_target="tpu_custom_call" | custom-call | bytes 1 | tf_op jit(solution)/shard_map/terms_b/pallas_call | solution.py:1035
  65.8 2.1 %collective-permute-done.10.refs_1_ = bf16[512,512]{1,0:T(8,128)(2,1)S(1)} collective-permute-done((bf16[512,512]{1,0:T(8,128)(2,1)S(1)}, bf16[512,512]{1,0:T(8,128)(2,1)S(1)}, u32[]{:S(2)}, u32[]{:S(2)}) %collective-permute-start.10) | collective-permute-done | bytes 524320 | tf_op jit(solution)/shard_map/ppermute | solution.py:819
  68.8 1.1 collective-permute-start.12
  69.9 1.5 %collective-permute-start.13 = (bf16[256,512]{1,0:T(8,128)(2,1)S(1)}, bf16[256,512]{1,0:T(8,128)(2,1)S(1)}, u32[]{:S(2)}, u32[]{:S(2)}) collective-permute-start(bf16[256,512]{1,0:T(8,128)(2,1)S(1)} %get-tuple-element.108), channel_id=1, source_target_pairs={{0,1},{1,0},{2,3},{3,2},{4,5},{5,4},{6,7},{7,6},{8,9},{9,8},{10,11... | collective-permute-start | bytes 786440 | tf_op jit(solution)/shard_map/ppermute | solution.py:819
  72.2 3.4 %input_near.1.refs_3_.base = f32[1024,512]{1,0:T(8,128)S(1)} custom-call(s32[5]{0:T(128)S(1)} %copy-done, bf16[2,640,512]{2,1,0:T(8,128)(2,1)S(1)} %get-tuple-element.92.d_pad, f32[1024,512]{1,0:T(8,128)S(1)} %get-tuple-element.93.base, bf16[5,512,512]{2,1,0:T(8,128)(2,1)S(1)} %get-tuple-element.80.weight, f32[512,512]{1,0:T(8,128)S(1)} %get-tuple-element.104._.refs_4_), custom_call_target="tpu_custom_call" | custom-call | bytes 1 | tf_op jit(solution)/shard_map/input_near/pallas_call | solution.py:1080
  77.4 1.6 %collective-permute-start.14 = (bf16[384,512]{1,0:T(8,128)(2,1)S(1)}, bf16[384,512]{1,0:T(8,128)(2,1)S(1)}, u32[]{:S(2)}, u32[]{:S(2)}) collective-permute-start(bf16[384,512]{1,0:T(8,128)(2,1)S(1)} %get-tuple-element.112), channel_id=1, source_target_pairs={{0,1},{1,0},{2,3},{3,2},{4,5},{5,4},{6,7},{7,6},{8,9},{9,8},{10,11... | collective-permute-start | bytes 1179656 | tf_op jit(solution)/shard_map/ppermute | solution.py:819
  80.4 4.4 %input_far.1 = (f32[1024,512]{1,0:T(8,128)}, f32[8,128]{1,0:T(8,128)S(1)}) custom-call(s32[5]{0:T(128)S(1)} %copy-done.2, bf16[2,640,512]{2,1,0:T(8,128)(2,1)S(1)} %get-tuple-element.92.d_pad, f32[1024,512]{1,0:T(8,128)S(1)} %input_near.1.refs_3_.base, bf16[5,512,512]{2,1,0:T(8,128)(2,1)S(1)} %get-tuple-element.105.weight, ...), custom_call_target="tpu_custom_call" | custom-call | bytes 1 | tf_op jit(solution)/shard_map/input_far/pallas_call | solution.py:1098
  84.9 2.4 %collective-permute-done.16.refs_2_ = bf16[544,512]{1,0:T(8,128)(2,1)S(1)} collective-permute-done((bf16[544,512]{1,0:T(8,128)(2,1)S(1)}, bf16[544,512]{1,0:T(8,128)(2,1)S(1)}, u32[]{:S(2)}, u32[]{:S(2)}) %collective-permute-start.16) | collective-permute-done | bytes 557088 | tf_op jit(solution)/shard_map/ppermute | solution.py:819
  89.5 1.0 collective-permute-done.19.refs_0_
  90.6 3.4 %collective-permute-start.23 = (bf16[128,512]{1,0:T(8,128)(2,1)S(1)}, bf16[128,512]{1,0:T(8,128)(2,1)S(1)}, u32[]{:S(2)}, u32[]{:S(2)}) collective-permute-start(bf16[128,512]{1,0:T(8,128)(2,1)S(1)} %get-tuple-element.130), channel_id=1, source_target_pairs={{0,16},{1,17},{2,18},{3,19},{4,20},{5,21},{6,22},{7,23},{8,24},{9,... | collective-permute-start | bytes 393224 | tf_op jit(solution)/shard_map/ppermute | solution.py:819
  94.0 1.7 %collective-permute-done.17.refs_0_ = bf16[320,512]{1,0:T(8,128)(2,1)S(1)} collective-permute-done((bf16[320,512]{1,0:T(8,128)(2,1)S(1)}, bf16[320,512]{1,0:T(8,128)(2,1)S(1)}, u32[]{:S(2)}, u32[]{:S(2)}) %collective-permute-start.17) | collective-permute-done | bytes 327712 | tf_op jit(solution)/shard_map/ppermute | solution.py:819
  96.4 1.5 %collective-permute-done.23.refs_0_ = bf16[128,512]{1,0:T(8,128)(2,1)S(1)} collective-permute-done((bf16[128,512]{1,0:T(8,128)(2,1)S(1)}, bf16[128,512]{1,0:T(8,128)(2,1)S(1)}, u32[]{:S(2)}, u32[]{:S(2)}) %collective-permute-start.23) | collective-permute-done | bytes 131104 | tf_op jit(solution)/shard_map/ppermute | solution.py:819
  99.2 1.0 collective-permute-start.21
  100.2 2.7 %collective-permute-done.22.refs_2_ = bf16[64,512]{1,0:T(8,128)(2,1)S(1)} collective-permute-done((bf16[64,512]{1,0:T(8,128)(2,1)S(1)}, bf16[64,512]{1,0:T(8,128)(2,1)S(1)}, u32[]{:S(2)}, u32[]{:S(2)}) %collective-permute-start.22) | collective-permute-done | bytes 65568 | tf_op jit(solution)/shard_map/ppermute | solution.py:819
  103.8 2.0 %collective-permute-start.24 = (bf16[192,512]{1,0:T(8,128)(2,1)S(1)}, bf16[192,512]{1,0:T(8,128)(2,1)S(1)}, u32[]{:S(2)}, u32[]{:S(2)}) collective-permute-start(bf16[192,512]{1,0:T(8,128)(2,1)S(1)} %get-tuple-element.132), channel_id=1, source_target_pairs={{0,16},{1,17},{2,18},{3,19},{4,20},{5,21},{6,22},{7,23},{8,24},{9,... | collective-permute-start | bytes 589832 | tf_op jit(solution)/shard_map/ppermute | solution.py:819
  105.9 6.7 %collective-permute-done.24.got = bf16[192,512]{1,0:T(8,128)(2,1)S(1)} collective-permute-done((bf16[192,512]{1,0:T(8,128)(2,1)S(1)}, bf16[192,512]{1,0:T(8,128)(2,1)S(1)}, u32[]{:S(2)}, u32[]{:S(2)}) %collective-permute-start.24) | collective-permute-done | bytes 196640 | tf_op jit(solution)/shard_map/ppermute | solution.py:819
  (60 shorter events, 13.6 us)
Async XLA Ops:
  0.6 4.0 %copy-start = (s32[5]{0:T(128)S(1)}, s32[5]{0:T(128)}, u32[]{:S(2)}) copy-start(s32[5]{0:T(128)} %table.5) | copy-start | bytes 64
  1.7 10.7 %collective-permute-start = (bf16[5,64,512]{2,1,0:T(8,128)(2,1)S(1)}, bf16[5,64,512]{2,1,0:T(8,128)(2,1)S(1)}, u32[]{:S(2)}, u32[]{:S(2)}) collective-permute-start(bf16[5,64,512]{2,1,0:T(8,128)(2,1)S(1)} %cut_piece.1), channel_id=1, source_target_pairs={{0,1},{1,0},{2,3},{3,2},{4,5},{5,4},{6,7},{7,6},{8,9},{9,8},{10,11... | collective-permute-start | bytes 983048 | tf_op jit(solution)/shard_map/ppermute | solution.py:68
  12.4 8.9 %collective-permute-start.2 = (bf16[5,64,512]{2,1,0:T(8,128)(2,1)S(1)}, bf16[5,64,512]{2,1,0:T(8,128)(2,1)S(1)}, u32[]{:S(2)}, u32[]{:S(2)}) collective-permute-start(bf16[5,64,512]{2,1,0:T(8,128)(2,1)S(1)} %after.8._.token.refs_14_), channel_id=1, source_target_pairs={{0,8},{2,10},{4,12},{6,14},{8,0},{10,2},{12,4},{14,6},{16,24},{18,... | collective-permute-start | bytes 983048 | tf_op jit(solution)/shard_map/ppermute | solution.py:64
  14.2 8.3 %collective-permute-start.1 = (bf16[5,64,512]{2,1,0:T(8,128)(2,1)S(1)}, bf16[5,64,512]{2,1,0:T(8,128)(2,1)S(1)}, u32[]{:S(2)}, u32[]{:S(2)}) collective-permute-start(bf16[5,64,512]{2,1,0:T(8,128)(2,1)S(1)} %after.8._.token.refs_14_), channel_id=1, source_target_pairs={{0,4},{2,6},{4,0},{6,2},{8,12},{10,14},{12,8},{14,10},{16,20},{18,... | collective-permute-start | bytes 983048 | tf_op jit(solution)/shard_map/ppermute | solution.py:64
  15.7 8.4 %collective-permute-start.3 = (bf16[336,512]{1,0:T(8,128)(2,1)S(1)}, bf16[336,512]{1,0:T(8,128)(2,1)S(1)}, u32[]{:S(2)}, u32[]{:S(2)}) collective-permute-start(bf16[336,512]{1,0:T(8,128)(2,1)S(1)} %after.9), channel_id=1, source_target_pairs={{0,1},{1,0},{2,3},{3,2},{4,5},{5,4},{6,7},{7,6},{8,9},{9,8},{10,11... | collective-permute-start | bytes 1032200 | tf_op jit(solution)/shard_map/ppermute | solution.py:68
  22.6 3.7 %collective-permute-start.5 = (bf16[10,64,512]{2,1,0:T(8,128)(2,1)S(1)}, bf16[10,64,512]{2,1,0:T(8,128)(2,1)S(1)}, u32[]{:S(2)}, u32[]{:S(2)}) collective-permute-start(bf16[10,64,512]{2,1,0:T(8,128)(2,1)S(1)} %both.1.refs_15_), channel_id=1, source_target_pairs={{0,2},{2,0},{4,6},{6,4},{8,10},{10,8},{12,14},{14,12},{16,18},{18,... | collective-permute-start | bytes 1966088 | tf_op jit(solution)/shard_map/ppermute | solution.py:64
  24.1 2.1 %collective-permute-start.6 = (bf16[336,512]{1,0:T(8,128)(2,1)S(1)}, bf16[336,512]{1,0:T(8,128)(2,1)S(1)}, u32[]{:S(2)}, u32[]{:S(2)}) collective-permute-start(bf16[336,512]{1,0:T(8,128)(2,1)S(1)} %collective-permute-done.3.refs_16_), channel_id=1, source_target_pairs={{0,2},{2,0},{4,6},{6,4},{8,10},{10,8},{12,14},{14,12},{16,18},{18,... | collective-permute-start | bytes 1032200 | tf_op jit(solution)/shard_map/ppermute | solution.py:64
  24.1 2.1 %collective-permute-start.4 = (bf16[5,64,512]{2,1,0:T(8,128)(2,1)S(1)}, bf16[5,64,512]{2,1,0:T(8,128)(2,1)S(1)}, u32[]{:S(2)}, u32[]{:S(2)}) collective-permute-start(bf16[5,64,512]{2,1,0:T(8,128)(2,1)S(1)} %after.8._.token.refs_14_), channel_id=1, source_target_pairs={{0,2},{2,0},{4,6},{6,4},{8,10},{10,8},{12,14},{14,12},{16,18},{18,... | collective-permute-start | bytes 983048 | tf_op jit(solution)/shard_map/ppermute | solution.py:64
  26.2 23.0 %copy-start.1 = (f32[512]{0:T(512)S(1)}, f32[512]{0:T(512)}, u32[]{:S(2)}) copy-start(f32[512]{0:T(512)} %param.19) | copy-start | bytes 6148
  26.2 23.0 %copy-start.3 = (s32[4]{0:T(128)S(1)}, s32[4]{0:T(128)}, u32[]{:S(2)}) copy-start(s32[4]{0:T(128)} %species.1) | copy-start | bytes 52
  26.3 23.0 %copy-start.4 = (s32[16]{0:T(128)S(1)}, s32[16]{0:T(128)}, u32[]{:S(2)}) copy-start(s32[16]{0:T(128)} %counts.1) | copy-start | bytes 196
  49.0 4.2 %collective-permute-start.7 = (bf16[2048,512]{1,0:T(8,128)(2,1)S(1)}, bf16[2048,512]{1,0:T(8,128)(2,1)S(1)}, u32[]{:S(2)}, u32[]{:S(2)}) collective-permute-start(bf16[2048,512]{1,0:T(8,128)(2,1)S(1)} %get-tuple-element.95), channel_id=1, source_target_pairs={{0,2},{2,0},{4,6},{6,4},{8,10},{10,8},{12,14},{14,12},{16,18},{18,... | collective-permute-start | bytes 6291464 | tf_op jit(solution)/shard_map/ppermute | solution.py:64
  53.2 3.0 %copy-start.2 = (s32[5]{0:T(128)S(1)}, s32[5]{0:T(128)}, u32[]{:S(2)}) copy-start(s32[5]{0:T(128)} %get-tuple-element.86.other_table.table) | copy-start | bytes 64
  53.7 14.2 %collective-permute-start.10 = (bf16[512,512]{1,0:T(8,128)(2,1)S(1)}, bf16[512,512]{1,0:T(8,128)(2,1)S(1)}, u32[]{:S(2)}, u32[]{:S(2)}) collective-permute-start(bf16[512,512]{1,0:T(8,128)(2,1)S(1)} %get-tuple-element.101), channel_id=1, source_target_pairs={{0,4},{1,5},{2,6},{3,7},{4,0},{5,1},{6,2},{7,3},{8,12},{9,13},{10,... | collective-permute-start | bytes 1572872 | tf_op jit(solution)/shard_map/ppermute | solution.py:819
  54.8 13.9 %collective-permute-start.9 = (bf16[512,512]{1,0:T(8,128)(2,1)S(1)}, bf16[512,512]{1,0:T(8,128)(2,1)S(1)}, u32[]{:S(2)}, u32[]{:S(2)}) collective-permute-start(bf16[512,512]{1,0:T(8,128)(2,1)S(1)} %get-tuple-element.97.refs_0_), channel_id=1, source_target_pairs={{0,1},{1,0},{2,3},{3,2},{4,5},{5,4},{6,7},{7,6},{8,9},{9,8},{10,11... | collective-permute-start | bytes 1572872 | tf_op jit(solution)/shard_map/ppermute | solution.py:819
  61.4 15.8 %collective-permute-start.11 = (bf16[1536,512]{1,0:T(8,128)(2,1)S(1)}, bf16[1536,512]{1,0:T(8,128)(2,1)S(1)}, u32[]{:S(2)}, u32[]{:S(2)}) collective-permute-start(bf16[1536,512]{1,0:T(8,128)(2,1)S(1)} %get-tuple-element.106), channel_id=1, source_target_pairs={{0,2},{2,0},{4,6},{6,4},{8,10},{10,8},{12,14},{14,12},{16,18},{18,... | collective-permute-start | bytes 4718600 | tf_op jit(solution)/shard_map/ppermute | solution.py:64
  65.3 6.1 %collective-permute-start.8 = (bf16[1056,512]{1,0:T(8,128)(2,1)S(1)}, bf16[1056,512]{1,0:T(8,128)(2,1)S(1)}, u32[]{:S(2)}, u32[]{:S(2)}) collective-permute-start(bf16[1056,512]{1,0:T(8,128)(2,1)S(1)} %get-tuple-element.99), channel_id=1, source_target_pairs={{0,2},{2,0},{4,6},{6,4},{8,10},{10,8},{12,14},{14,12},{16,18},{18,... | collective-permute-start | bytes 3244040 | tf_op jit(solution)/shard_map/ppermute | solution.py:64
  68.8 7.5 %collective-permute-start.12 = (bf16[256,512]{1,0:T(8,128)(2,1)S(1)}, bf16[256,512]{1,0:T(8,128)(2,1)S(1)}, u32[]{:S(2)}, u32[]{:S(2)}) collective-permute-start(bf16[256,512]{1,0:T(8,128)(2,1)S(1)} %get-tuple-element.107), channel_id=1, source_target_pairs={{0,4},{1,5},{2,6},{3,7},{4,0},{5,1},{6,2},{7,3},{8,12},{9,13},{10,... | collective-permute-start | bytes 786440 | tf_op jit(solution)/shard_map/ppermute | solution.py:819
  69.9 7.1 %collective-permute-start.13 = (bf16[256,512]{1,0:T(8,128)(2,1)S(1)}, bf16[256,512]{1,0:T(8,128)(2,1)S(1)}, u32[]{:S(2)}, u32[]{:S(2)}) collective-permute-start(bf16[256,512]{1,0:T(8,128)(2,1)S(1)} %get-tuple-element.108), channel_id=1, source_target_pairs={{0,1},{1,0},{2,3},{3,2},{4,5},{5,4},{6,7},{7,6},{8,9},{9,8},{10,11... | collective-permute-start | bytes 786440 | tf_op jit(solution)/shard_map/ppermute | solution.py:819
  71.7 15.6 %collective-permute-start.16 = (bf16[544,512]{1,0:T(8,128)(2,1)S(1)}, bf16[544,512]{1,0:T(8,128)(2,1)S(1)}, u32[]{:S(2)}, u32[]{:S(2)}) collective-permute-start(bf16[544,512]{1,0:T(8,128)(2,1)S(1)} %get-tuple-element.114), channel_id=1, source_target_pairs={{0,8},{1,9},{2,10},{3,11},{4,12},{5,13},{6,14},{7,15},{8,0},{9,1},... | collective-permute-start | bytes 1671176 | tf_op jit(solution)/shard_map/ppermute | solution.py:819
  77.4 9.9 %collective-permute-start.14 = (bf16[384,512]{1,0:T(8,128)(2,1)S(1)}, bf16[384,512]{1,0:T(8,128)(2,1)S(1)}, u32[]{:S(2)}, u32[]{:S(2)}) collective-permute-start(bf16[384,512]{1,0:T(8,128)(2,1)S(1)} %get-tuple-element.112), channel_id=1, source_target_pairs={{0,1},{1,0},{2,3},{3,2},{4,5},{5,4},{6,7},{7,6},{8,9},{9,8},{10,11... | collective-permute-start | bytes 1179656 | tf_op jit(solution)/shard_map/ppermute | solution.py:819
  79.0 8.7 %collective-permute-start.15 = (bf16[384,512]{1,0:T(8,128)(2,1)S(1)}, bf16[384,512]{1,0:T(8,128)(2,1)S(1)}, u32[]{:S(2)}, u32[]{:S(2)}) collective-permute-start(bf16[384,512]{1,0:T(8,128)(2,1)S(1)} %get-tuple-element.113), channel_id=1, source_target_pairs={{0,4},{1,5},{2,6},{3,7},{4,0},{5,1},{6,2},{7,3},{8,12},{9,13},{10,... | collective-permute-start | bytes 1179656 | tf_op jit(solution)/shard_map/ppermute | solution.py:819
  79.9 10.6 %collective-permute-start.19 = (bf16[256,512]{1,0:T(8,128)(2,1)S(1)}, bf16[256,512]{1,0:T(8,128)(2,1)S(1)}, u32[]{:S(2)}, u32[]{:S(2)}) collective-permute-start(bf16[256,512]{1,0:T(8,128)(2,1)S(1)} %get-tuple-element.120), channel_id=1, source_target_pairs={{0,8},{1,9},{2,10},{3,11},{4,12},{5,13},{6,14},{7,15},{8,0},{9,1},... | collective-permute-start | bytes 786440 | tf_op jit(solution)/shard_map/ppermute | solution.py:819
  88.0 7.7 %collective-permute-start.18 = (bf16[352,512]{1,0:T(8,128)(2,1)S(1)}, bf16[352,512]{1,0:T(8,128)(2,1)S(1)}, u32[]{:S(2)}, u32[]{:S(2)}) collective-permute-start(bf16[352,512]{1,0:T(8,128)(2,1)S(1)} %get-tuple-element.118), channel_id=1, source_target_pairs={{0,1},{1,0},{2,3},{3,2},{4,5},{5,4},{6,7},{7,6},{8,9},{9,8},{10,11... | collective-permute-start | bytes 1081352 | tf_op jit(solution)/shard_map/ppermute | solution.py:819
  88.6 7.1 %collective-permute-start.17 = (bf16[320,512]{1,0:T(8,128)(2,1)S(1)}, bf16[320,512]{1,0:T(8,128)(2,1)S(1)}, u32[]{:S(2)}, u32[]{:S(2)}) collective-permute-start(bf16[320,512]{1,0:T(8,128)(2,1)S(1)} %get-tuple-element.117), channel_id=1, source_target_pairs={{0,4},{1,5},{2,6},{3,7},{4,0},{5,1},{6,2},{7,3},{8,12},{9,13},{10,... | collective-permute-start | bytes 983048 | tf_op jit(solution)/shard_map/ppermute | solution.py:819
  90.6 7.3 %collective-permute-start.23 = (bf16[128,512]{1,0:T(8,128)(2,1)S(1)}, bf16[128,512]{1,0:T(8,128)(2,1)S(1)}, u32[]{:S(2)}, u32[]{:S(2)}) collective-permute-start(bf16[128,512]{1,0:T(8,128)(2,1)S(1)} %get-tuple-element.130), channel_id=1, source_target_pairs={{0,16},{1,17},{2,18},{3,19},{4,20},{5,21},{6,22},{7,23},{8,24},{9,... | collective-permute-start | bytes 393224 | tf_op jit(solution)/shard_map/ppermute | solution.py:819
  95.7 8.1 %collective-permute-start.20 = (bf16[192,512]{1,0:T(8,128)(2,1)S(1)}, bf16[192,512]{1,0:T(8,128)(2,1)S(1)}, u32[]{:S(2)}, u32[]{:S(2)}) collective-permute-start(bf16[192,512]{1,0:T(8,128)(2,1)S(1)} %get-tuple-element.122), channel_id=1, source_target_pairs={{0,8},{1,9},{2,10},{3,11},{4,12},{5,13},{6,14},{7,15},{8,0},{9,1},... | collective-permute-start | bytes 589832 | tf_op jit(solution)/shard_map/ppermute | solution.py:819
  98.6 4.3 %collective-permute-start.22 = (bf16[64,512]{1,0:T(8,128)(2,1)S(1)}, bf16[64,512]{1,0:T(8,128)(2,1)S(1)}, u32[]{:S(2)}, u32[]{:S(2)}) collective-permute-start(bf16[64,512]{1,0:T(8,128)(2,1)S(1)} %get-tuple-element.127), channel_id=1, source_target_pairs={{0,1},{1,0},{2,3},{3,2},{4,5},{5,4},{6,7},{7,6},{8,9},{9,8},{10,11... | collective-permute-start | bytes 196616 | tf_op jit(solution)/shard_map/ppermute | solution.py:819
  99.2 4.6 %collective-permute-start.21 = (bf16[96,512]{1,0:T(8,128)(2,1)S(1)}, bf16[96,512]{1,0:T(8,128)(2,1)S(1)}, u32[]{:S(2)}, u32[]{:S(2)}) collective-permute-start(bf16[96,512]{1,0:T(8,128)(2,1)S(1)} %get-tuple-element.126), channel_id=1, source_target_pairs={{0,4},{1,5},{2,6},{3,7},{4,0},{5,1},{6,2},{7,3},{8,12},{9,13},{10,... | collective-permute-start | bytes 294920 | tf_op jit(solution)/shard_map/ppermute | solution.py:819
  103.8 8.7 %collective-permute-start.24 = (bf16[192,512]{1,0:T(8,128)(2,1)S(1)}, bf16[192,512]{1,0:T(8,128)(2,1)S(1)}, u32[]{:S(2)}, u32[]{:S(2)}) collective-permute-start(bf16[192,512]{1,0:T(8,128)(2,1)S(1)} %get-tuple-element.132), channel_id=1, source_target_pairs={{0,16},{1,17},{2,18},{3,19},{4,20},{5,21},{6,22},{7,23},{8,24},{9,... | collective-permute-start | bytes 589832 | tf_op jit(solution)/shard_map/ppermute | solution.py:819

commit v3 on v2

--- a/solution.py
+++ b/solution.py
@@ -561,15 +561,11 @@
 
 
 def store_small(total, ref, first):
-    count = total.shape[0]
-    high = total.astype(BF16)
-    ref[first : first + count, :] = high
-    ref[first + count : first + 2 * count, :] = (total - high.astype(F32)).astype(BF16)
+    ref[first : first + total.shape[0], :] = total.astype(BF16)
 
 
 def load_small(ref, first, count):
-    high = ref[first : first + count, :].astype(F32)
-    return high + ref[first + count : first + 2 * count, :].astype(F32)
+    return ref[first : first + count, :].astype(F32)
 
 
 def terms_kernel(slots, orders, dp_bits, with_small, own_table, other_table, x_pad, d_pad, *refs):
@@ -680,10 +676,7 @@
     return total
 
 
-def last_ffn_kernel(members, *refs):
-    gots = refs[:members]
-    keep, _, w_in_out, w_out_out, token = refs[members:]
-    token[...] = jnp.zeros(token.shape, token.dtype)
+def finish_ffn(got, keep, w_in_out, w_out_out):
     out_rows, chan = w_out_out.shape
     in_rows = w_in_out.shape[0]
     half = keep.shape[0] // 2
@@ -691,11 +684,11 @@
     for part in range(2):
         base = part * half
         size = out_rows // 2
-        w_out_out[part * size : (part + 1) * size, :] = sum_of(gots, keep, slice(base, base + size))
+        w_out_out[part * size : (part + 1) * size, :] = sum_of([got], keep, slice(base, base + size))
         for step in range(steps):
             at = base + size + step * in_rows
             cols = slice((part * steps + step) * chan, (part * steps + step + 1) * chan)
-            w_in_out[:, cols] = sum_of(gots, keep, slice(at, at + in_rows))
+            w_in_out[:, cols] = sum_of([got], keep, slice(at, at + in_rows))
 
 
 def last_conv_kernel(
@@ -703,6 +696,8 @@
     keep_a,
     small,
     keep_b,
+    got_f,
+    keep_f,
     out,
     total,
     conv_bias,
@@ -712,7 +707,10 @@
     gain_two,
     bias_two,
     b_in,
+    w_in_out,
+    w_out_out,
 ):
+    finish_ffn(got_f, keep_f, w_in_out, w_out_out)
     size = out.shape[1] // 2
     first = keep_a.shape[0] // out.shape[1]
     rest = out.shape[0] - first
@@ -1028,7 +1026,7 @@
 
     def terms(group, orders, token, small, name):
         count = len(group) * chan
-        extra = 0 if small is None else 2 * small.shape[0]
+        extra = 0 if small is None else small.shape[0]
         outs = [vmem((count, chan), F32), vmem((count + extra, chan), BF16)]
         scratch = [vmem((2, chan, chan), F32)]
         more = [] if small is None else [near(small)]
@@ -1054,7 +1052,7 @@
     mark = token
     flow_a = dict(keep=keep_a)
     flow_b = dict(keep=keep_b, small=small)
-    extra = 2 * small.shape[0]
+    extra = small.shape[0]
     over_z, over_zz = 2 << line[0], 2 << line[1]
 
     def half_of(flow):
@@ -1143,20 +1141,8 @@
     sends = fused_step(gots, [flow_b], [plan], [size + extra, size], flow_a["keep"])
     gots_b = [swap(sends[0], over_y), swap(sends[1], over_x)]
     mark = flow_b["keep"]
-    w_in_mine, w_out_mine, mark = pl.pallas_call(
-        functools.partial(last_ffn_kernel, 1),
-        out_shape=[
-            jax.ShapeDtypeStruct((chan >> (dp_bits + 1), hid), F32),
-            jax.ShapeDtypeStruct((hid >> (dp_bits + 1), chan), F32),
-            vmem((8, 128), F32),
-        ],
-        in_specs=[VMEM] * 3,
-        out_specs=[VMEM] * 3,
-        compiler_params=params(4),
-        cost_estimate=claim(0),
-        name="last_ffn",
-    )(near(got_f), near(flow_f["keep"]), near(mark))
-    mark = spaced(mark)
+    got_f = after(got_f, mark)
+    mark = spaced(got_f)
     size, size_b = half_of(flow_a), half_of(flow_b)
     plan = dict(ins=joined(0, flow_a), outs=[(0, 0), (0, size)])
     shift = 2 * size
@@ -1173,20 +1159,31 @@
     width = chan >> (dp_bits + 1)
     wide = hid >> (dp_bits + 1)
     small = flow_b["small"]
-    conv_weight_grad, _, *vectors = pl.pallas_call(
+    conv_weight_grad, _, *vectors, w_in_mine, w_out_mine = pl.pallas_call(
         last_conv_kernel,
         out_shape=[
             jax.ShapeDtypeStruct((slots, chan >> dp_bits, chan), F32),
             vmem(small.shape, F32),
         ]
         + [jax.ShapeDtypeStruct((1, width), F32)] * 6
-        + [jax.ShapeDtypeStruct((1, wide), F32)],
-        in_specs=[VMEM] * 4,
-        out_specs=[VMEM] * 9,
+        + [
+            jax.ShapeDtypeStruct((1, wide), F32),
+            jax.ShapeDtypeStruct((chan >> (dp_bits + 1), hid), F32),
+            jax.ShapeDtypeStruct((hid >> (dp_bits + 1), chan), F32),
+        ],
+        in_specs=[VMEM] * 6,
+        out_specs=[VMEM] * 11,
         compiler_params=params(4),
         cost_estimate=claim(0),
         name="last_conv",
-    )(near(got), near(flow_a["keep"]), near(small), near(flow_b["keep"]))
+    )(
+        near(got),
+        near(flow_a["keep"]),
+        near(small),
+        near(flow_b["keep"]),
+        near(got_f),
+        near(flow_f["keep"]),
+    )
     conv_bias_grad, gain_one_grad, bias_one_grad, b_out_grad, gain_two_grad, bias_two_grad, b_in_grad = [
         vector.reshape(-1) for vector in vectors
     ]

time: 114 us -> 112 us (0.982)
  waiting for transfers between devices: 30.7 us -> 28.1 us
  starting transfers between devices: 27.1 us -> 29 us
    ppermute x15, waiting for transfers between devices: 21.4 us -> 18.8 us  [swap(): lax.ppermute(value, ('dp', 'tap'), [(i, i ^ mask) for i in range(count)])]
    ppermute x15, starting transfers between devices: 17.8 us -> 19.7 us  [swap(): lax.ppermute(value, ('dp', 'tap'), [(i, i ^ mask) for i in range(count)])]
where the time goes in v3:
time: 112 us
  Pallas kernels  54 us (48%)
  starting transfers between devices  29 us (26%)
  waiting for transfers between devices  28.1 us (25%)
    pallas_call x1, Pallas kernels, fast_shards(): pl.pallas_call(functools.partial(main_kernel, orders, dp_bits, [turn for...  22.7 us
    ppermute x15, starting transfers between devices, swap(): lax.ppermute(value, ('dp', 'tap'), [(i, i ^ mask) for i in range(count)])  19.7 us
    ppermute x15, waiting for transfers between devices, swap(): lax.ppermute(value, ('dp', 'tap'), [(i, i ^ mask) for i in range(count)])  18.8 us
    pallas_call x2, Pallas kernels, terms(): pl.pallas_call(functools.partial(terms_kernel, group, orders, dp_bits, sm...  8.92 us
    ppermute x2, waiting for transfers between devices, swap_tap(): return lax.ppermute(value, 'tap', [(0, 1), (1, 0)])  5.68 us
    ppermute x8, starting transfers between devices, swap_dp(): return lax.ppermute(value, 'dp', [(i, i ^ 1 << bit) for i in range(count)])  4.78 us
    ppermute x2, starting transfers between devices, swap_tap(): return lax.ppermute(value, 'tap', [(0, 1), (1, 0)])  4.49 us
    pallas_call x1, Pallas kernels, fast_shards(): pl.pallas_call(input_far_kernel, out_shape=[pltpu.HBM(rows_f, F32), vmem(...  4.44 us
  transfers between devices with their start and end apart: 25, of which 18 were waited for; matrix products, arithmetic and copies ran while one was open for 0% of the time, Pallas kernels for 26%

profile of v3, /device:TPU:0, one launch (start us, length us, event | category | flops | bytes accessed | tf_op | source)
XLA Modules:
  0.0 112.0 jit_solution(2671052467888948818)
XLA Ops:
  0.7 1.0 cut_piece.1
  1.7 3.0 %collective-permute-start = (bf16[5,64,512]{2,1,0:T(8,128)(2,1)S(1)}, bf16[5,64,512]{2,1,0:T(8,128)(2,1)S(1)}, u32[]{:S(2)}, u32[]{:S(2)}) collective-permute-start(bf16[5,64,512]{2,1,0:T(8,128)(2,1)S(1)} %cut_piece.1), channel_id=1, source_target_pairs={{0,1},{1,0},{2,3},{3,2},{4,5},{5,4},{6,7},{7,6},{8,9},{9,8},{10,11... | collective-permute-start | bytes 983048 | tf_op jit(solution)/shard_map/ppermute | solution.py:68
  4.7 3.5 %load.1 = (bf16[2,640,512]{2,1,0:T(8,128)(2,1)S(1)}, bf16[5,512,512]{2,1,0:T(8,128)(2,1)S(1)}, bf16[512,2048]{1,0:T(8,128)(2,1)S(1)}, bf16[336,512]{1,0:T(8,128)(2,1)S(1)}) custom-call(s32[5]{0:T(128)S(1)} %copy-done, bf16[2048,512]{1,0:T(8,128)(2,1)} %x_hbm.1, bf16[5,512,512]{2,1,0:T(8,128)(2,1)} %weight_hbm.3, bf16[512,2048]{1,0:T(8,128)(2,1)} %w_in_hbm.1), custom_call_target="tpu_custom_call" | custom-call | bytes 1 | tf_op jit(solution)/shard_map/load/pallas_call | solution.py:919
  8.2 4.2 %collective-permute-done._ = bf16[5,64,512]{2,1,0:T(8,128)(2,1)S(1)} collective-permute-done((bf16[5,64,512]{2,1,0:T(8,128)(2,1)S(1)}, bf16[5,64,512]{2,1,0:T(8,128)(2,1)S(1)}, u32[]{:S(2)}, u32[]{:S(2)}) %collective-permute-start) | collective-permute-done | bytes 327712 | tf_op jit(solution)/shard_map/ppermute | solution.py:68
  12.4 1.8 %collective-permute-start.2 = (bf16[5,64,512]{2,1,0:T(8,128)(2,1)S(1)}, bf16[5,64,512]{2,1,0:T(8,128)(2,1)S(1)}, u32[]{:S(2)}, u32[]{:S(2)}) collective-permute-start(bf16[5,64,512]{2,1,0:T(8,128)(2,1)S(1)} %after.9._.token.refs_14_), channel_id=1, source_target_pairs={{0,8},{2,10},{4,12},{6,14},{8,0},{10,2},{12,4},{14,6},{16,24},{18,... | collective-permute-start | bytes 983048 | tf_op jit(solution)/shard_map/ppermute | solution.py:64
  14.2 1.5 %collective-permute-start.1 = (bf16[5,64,512]{2,1,0:T(8,128)(2,1)S(1)}, bf16[5,64,512]{2,1,0:T(8,128)(2,1)S(1)}, u32[]{:S(2)}, u32[]{:S(2)}) collective-permute-start(bf16[5,64,512]{2,1,0:T(8,128)(2,1)S(1)} %after.9._.token.refs_14_), channel_id=1, source_target_pairs={{0,4},{2,6},{4,0},{6,2},{8,12},{10,14},{12,8},{14,10},{16,20},{18,... | collective-permute-start | bytes 983048 | tf_op jit(solution)/shard_map/ppermute | solution.py:64
  15.7 1.5 %collective-permute-start.3 = (bf16[336,512]{1,0:T(8,128)(2,1)S(1)}, bf16[336,512]{1,0:T(8,128)(2,1)S(1)}, u32[]{:S(2)}, u32[]{:S(2)}) collective-permute-start(bf16[336,512]{1,0:T(8,128)(2,1)S(1)} %after.10), channel_id=1, source_target_pairs={{0,1},{1,0},{2,3},{3,2},{4,5},{5,4},{6,7},{7,6},{8,9},{9,8},{10,11... | collective-permute-start | bytes 1032200 | tf_op jit(solution)/shard_map/ppermute | solution.py:68
  17.2 3.4 %own_conv.1 = (f32[1024,512]{1,0:T(8,128)S(1)}, f32[8,128]{1,0:T(8,128)S(1)}) custom-call(s32[5]{0:T(128)S(1)} %copy-done, bf16[2,640,512]{2,1,0:T(8,128)(2,1)S(1)} %get-tuple-element.78.token.x_pad.refs_2_, bf16[5,512,512]{2,1,0:T(8,128)(2,1)S(1)} %get-tuple-element.79.weight, bf16[5,64,512]{2,1,0:T(8,128)(2,1)S(1)} %after.9._.token.refs_14_), custom_call_target="tpu_custom_call" | custom-call | bytes 1 | tf_op jit(solution)/shard_map/own_conv/pallas_call | solution.py:935
  21.3 1.2 %collective-permute-done.1.over_one = bf16[5,64,512]{2,1,0:T(8,128)(2,1)S(1)} collective-permute-done((bf16[5,64,512]{2,1,0:T(8,128)(2,1)S(1)}, bf16[5,64,512]{2,1,0:T(8,128)(2,1)S(1)}, u32[]{:S(2)}, u32[]{:S(2)}) %collective-permute-start.1) | collective-permute-done | bytes 327712 | tf_op jit(solution)/shard_map/ppermute | solution.py:64
  22.6 1.5 %collective-permute-done.3.refs_16_ = bf16[336,512]{1,0:T(8,128)(2,1)S(1)} collective-permute-done((bf16[336,512]{1,0:T(8,128)(2,1)S(1)}, bf16[336,512]{1,0:T(8,128)(2,1)S(1)}, u32[]{:S(2)}, u32[]{:S(2)}) %collective-permute-start.3) | collective-permute-done | bytes 344096 | tf_op jit(solution)/shard_map/ppermute | solution.py:68
  24.6 1.6 %collective-permute-done.4.refs_17_ = bf16[5,64,512]{2,1,0:T(8,128)(2,1)S(1)} collective-permute-done((bf16[5,64,512]{2,1,0:T(8,128)(2,1)S(1)}, bf16[5,64,512]{2,1,0:T(8,128)(2,1)S(1)}, u32[]{:S(2)}, u32[]{:S(2)}) %collective-permute-start.4) | collective-permute-done | bytes 327712 | tf_op jit(solution)/shard_map/ppermute | solution.py:64
  26.3 22.7 %main_rows.1 = (bf16[1024,512]{1,0:T(8,128)(2,1)}, f32[1024,512]{1,0:T(8,128)S(1)}, f32[1024,512]{1,0:T(8,128)S(1)}, bf16[1024,2048]{1,0:T(8,128)(2,1)S(1)}, bf1...) custom-call(s32[4]{0:T(128)} %species.1, ...), custom_call_target="tpu_custom_call" | custom-call | bytes 1 | tf_op jit(solution)/shard_map/main_rows/pallas_call | solution.py:948
  49.2 3.9 %back_rows.1 = (bf16[2,640,512]{2,1,0:T(8,128)(2,1)S(1)}, f32[1024,512]{1,0:T(8,128)S(1)}, f32[16,512]{1,0:T(8,128)S(1)}) custom-call(s32[4]{0:T(128)S(1)} %copy-done.3, s32[16]{0:T(128)S(1)} %copy-done.4, bf16[1024,512]{1,0:T(8,128)(2,1)S(1)} %get-tuple-element.86.grad_in, bf16[512,2048]{1,0:T(8,128)(2,1)S(1)} %get-tuple-element.81.refs_5_.w_in, ...), custom_call_target="tpu_custom_call" | custom-call | bytes 1 | tf_op jit(solution)/shard_map/back_rows/pallas_call | solution.py:1001
  53.7 1.0 collective-permute-start.10
  54.8 1.5 %collective-permute-start.9 = (bf16[512,512]{1,0:T(8,128)(2,1)S(1)}, bf16[512,512]{1,0:T(8,128)(2,1)S(1)}, u32[]{:S(2)}, u32[]{:S(2)}) collective-permute-start(bf16[512,512]{1,0:T(8,128)(2,1)S(1)} %get-tuple-element.96.refs_0_), channel_id=1, source_target_pairs={{0,1},{1,0},{2,3},{3,2},{4,5},{5,4},{6,7},{7,6},{8,9},{9,8},{10,11... | collective-permute-start | bytes 1572872 | tf_op jit(solution)/shard_map/ppermute | solution.py:817
  56.3 5.1 %terms_a.1 = (f32[1536,512]{1,0:T(8,128)S(1)}, bf16[1536,512]{1,0:T(8,128)(2,1)S(1)}) custom-call(s32[5]{0:T(128)S(1)} %copy-done, s32[5]{0:T(128)S(1)} %copy-done.2, bf16[2,640,512]{2,1,0:T(8,128)(2,1)S(1)} %get-tuple-element.78.token.x_pad.refs_2_, bf16[2,640,512]{2,1,0:T(8,128)(2,1)S(1)} %get-tuple-element.91.d_pad, ...), custom_call_target="tpu_custom_call" | custom-call | bytes 1 | tf_op jit(solution)/shard_map/terms_a/pallas_call | solution.py:1033
  61.5 3.8 %terms_b.1 = (f32[1024,512]{1,0:T(8,128)S(1)}, bf16[1040,512]{1,0:T(8,128)(2,1)S(1)}) custom-call(s32[5]{0:T(128)S(1)} %copy-done, s32[5]{0:T(128)S(1)} %copy-done.2, bf16[2,640,512]{2,1,0:T(8,128)(2,1)S(1)} %get-tuple-element.78.token.x_pad.refs_2_, bf16[2,640,512]{2,1,0:T(8,128)(2,1)S(1)} %get-tuple-element.91.d_pad, ...), custom_call_target="tpu_custom_call" | custom-call | bytes 1 | tf_op jit(solution)/shard_map/terms_b/pallas_call | solution.py:1033
  65.8 2.1 %collective-permute-done.10.refs_1_ = bf16[512,512]{1,0:T(8,128)(2,1)S(1)} collective-permute-done((bf16[512,512]{1,0:T(8,128)(2,1)S(1)}, bf16[512,512]{1,0:T(8,128)(2,1)S(1)}, u32[]{:S(2)}, u32[]{:S(2)}) %collective-permute-start.10) | collective-permute-done | bytes 524320 | tf_op jit(solution)/shard_map/ppermute | solution.py:817
  68.8 1.1 %collective-permute-start.12 = (bf16[256,512]{1,0:T(8,128)(2,1)S(1)}, bf16[256,512]{1,0:T(8,128)(2,1)S(1)}, u32[]{:S(2)}, u32[]{:S(2)}) collective-permute-start(bf16[256,512]{1,0:T(8,128)(2,1)S(1)} %get-tuple-element.106), channel_id=1, source_target_pairs={{0,4},{1,5},{2,6},{3,7},{4,0},{5,1},{6,2},{7,3},{8,12},{9,13},{10,... | collective-permute-start | bytes 786440 | tf_op jit(solution)/shard_map/ppermute | solution.py:817
  69.9 1.5 %collective-permute-start.13 = (bf16[256,512]{1,0:T(8,128)(2,1)S(1)}, bf16[256,512]{1,0:T(8,128)(2,1)S(1)}, u32[]{:S(2)}, u32[]{:S(2)}) collective-permute-start(bf16[256,512]{1,0:T(8,128)(2,1)S(1)} %get-tuple-element.107), channel_id=1, source_target_pairs={{0,1},{1,0},{2,3},{3,2},{4,5},{5,4},{6,7},{7,6},{8,9},{9,8},{10,11... | collective-permute-start | bytes 786440 | tf_op jit(solution)/shard_map/ppermute | solution.py:817
  72.2 3.4 %input_near.1.refs_3_.base = f32[1024,512]{1,0:T(8,128)S(1)} custom-call(s32[5]{0:T(128)S(1)} %copy-done, bf16[2,640,512]{2,1,0:T(8,128)(2,1)S(1)} %get-tuple-element.91.d_pad, f32[1024,512]{1,0:T(8,128)S(1)} %get-tuple-element.92.base, bf16[5,512,512]{2,1,0:T(8,128)(2,1)S(1)} %get-tuple-element.79.weight, f32[512,512]{1,0:T(8,128)S(1)} %get-tuple-element.103._.refs_4_), custom_call_target="tpu_custom_call" | custom-call | bytes 1 | tf_op jit(solution)/shard_map/input_near/pallas_call | solution.py:1078
  77.4 1.6 %collective-permute-start.14 = (bf16[384,512]{1,0:T(8,128)(2,1)S(1)}, bf16[384,512]{1,0:T(8,128)(2,1)S(1)}, u32[]{:S(2)}, u32[]{:S(2)}) collective-permute-start(bf16[384,512]{1,0:T(8,128)(2,1)S(1)} %get-tuple-element.111), channel_id=1, source_target_pairs={{0,1},{1,0},{2,3},{3,2},{4,5},{5,4},{6,7},{7,6},{8,9},{9,8},{10,11... | collective-permute-start | bytes 1179656 | tf_op jit(solution)/shard_map/ppermute | solution.py:817
  79.0 1.0 collective-permute-start.15
  80.4 4.4 %input_far.1 = (f32[1024,512]{1,0:T(8,128)}, f32[8,128]{1,0:T(8,128)S(1)}) custom-call(s32[5]{0:T(128)S(1)} %copy-done.2, bf16[2,640,512]{2,1,0:T(8,128)(2,1)S(1)} %get-tuple-element.91.d_pad, f32[1024,512]{1,0:T(8,128)S(1)} %input_near.1.refs_3_.base, bf16[5,512,512]{2,1,0:T(8,128)(2,1)S(1)} %get-tuple-element.104.weight, ...), custom_call_target="tpu_custom_call" | custom-call | bytes 1 | tf_op jit(solution)/shard_map/input_far/pallas_call | solution.py:1096
  84.9 2.1 %collective-permute-done.16.refs_2_ = bf16[528,512]{1,0:T(8,128)(2,1)S(1)} collective-permute-done((bf16[528,512]{1,0:T(8,128)(2,1)S(1)}, bf16[528,512]{1,0:T(8,128)(2,1)S(1)}, u32[]{:S(2)}, u32[]{:S(2)}) %collective-permute-start.16) | collective-permute-done | bytes 540704 | tf_op jit(solution)/shard_map/ppermute | solution.py:817
  90.2 3.4 %collective-permute-start.23 = (bf16[128,512]{1,0:T(8,128)(2,1)S(1)}, bf16[128,512]{1,0:T(8,128)(2,1)S(1)}, u32[]{:S(2)}, u32[]{:S(2)}) collective-permute-start(bf16[128,512]{1,0:T(8,128)(2,1)S(1)} %get-tuple-element.129), channel_id=1, source_target_pairs={{0,16},{1,17},{2,18},{3,19},{4,20},{5,21},{6,22},{7,23},{8,24},{9,... | collective-permute-start | bytes 393224 | tf_op jit(solution)/shard_map/ppermute | solution.py:817
  93.6 2.0 %collective-permute-done.17.refs_0_ = bf16[320,512]{1,0:T(8,128)(2,1)S(1)} collective-permute-done((bf16[320,512]{1,0:T(8,128)(2,1)S(1)}, bf16[320,512]{1,0:T(8,128)(2,1)S(1)}, u32[]{:S(2)}, u32[]{:S(2)}) %collective-permute-start.17) | collective-permute-done | bytes 327712 | tf_op jit(solution)/shard_map/ppermute | solution.py:817
  96.4 1.9 %collective-permute-start.22 = (bf16[64,512]{1,0:T(8,128)(2,1)S(1)}, bf16[64,512]{1,0:T(8,128)(2,1)S(1)}, u32[]{:S(2)}, u32[]{:S(2)}) collective-permute-start(bf16[64,512]{1,0:T(8,128)(2,1)S(1)} %get-tuple-element.126), channel_id=1, source_target_pairs={{0,1},{1,0},{2,3},{3,2},{4,5},{5,4},{6,7},{7,6},{8,9},{9,8},{10,11... | collective-permute-start | bytes 196616 | tf_op jit(solution)/shard_map/ppermute | solution.py:817
  99.3 1.4 %collective-permute-done.22.refs_2_ = bf16[64,512]{1,0:T(8,128)(2,1)S(1)} collective-permute-done((bf16[64,512]{1,0:T(8,128)(2,1)S(1)}, bf16[64,512]{1,0:T(8,128)(2,1)S(1)}, u32[]{:S(2)}, u32[]{:S(2)}) %collective-permute-start.22) | collective-permute-done | bytes 65568 | tf_op jit(solution)/shard_map/ppermute | solution.py:817
  100.7 2.0 %collective-permute-done.21.refs_1_ = bf16[80,512]{1,0:T(8,128)(2,1)S(1)} collective-permute-done((bf16[80,512]{1,0:T(8,128)(2,1)S(1)}, bf16[80,512]{1,0:T(8,128)(2,1)S(1)}, u32[]{:S(2)}, u32[]{:S(2)}) %collective-permute-start.21) | collective-permute-done | bytes 81952 | tf_op jit(solution)/shard_map/ppermute | solution.py:817
  102.8 3.0 %collective-permute-start.24 = (bf16[176,512]{1,0:T(8,128)(2,1)S(1)}, bf16[176,512]{1,0:T(8,128)(2,1)S(1)}, u32[]{:S(2)}, u32[]{:S(2)}) collective-permute-start(bf16[176,512]{1,0:T(8,128)(2,1)S(1)} %get-tuple-element.130), channel_id=1, source_target_pairs={{0,16},{1,17},{2,18},{3,19},{4,20},{5,21},{6,22},{7,23},{8,24},{9,... | collective-permute-start | bytes 540680 | tf_op jit(solution)/shard_map/ppermute | solution.py:817
  105.7 5.4 %collective-permute-done.24.got = bf16[176,512]{1,0:T(8,128)(2,1)S(1)} collective-permute-done((bf16[176,512]{1,0:T(8,128)(2,1)S(1)}, bf16[176,512]{1,0:T(8,128)(2,1)S(1)}, u32[]{:S(2)}, u32[]{:S(2)}) %collective-permute-start.24) | collective-permute-done | bytes 180256 | tf_op jit(solution)/shard_map/ppermute | solution.py:817
  (60 shorter events, 12.4 us)
Async XLA Ops:
  0.6 4.0 %copy-start = (s32[5]{0:T(128)S(1)}, s32[5]{0:T(128)}, u32[]{:S(2)}) copy-start(s32[5]{0:T(128)} %table.5) | copy-start | bytes 64
  1.7 10.7 %collective-permute-start = (bf16[5,64,512]{2,1,0:T(8,128)(2,1)S(1)}, bf16[5,64,512]{2,1,0:T(8,128)(2,1)S(1)}, u32[]{:S(2)}, u32[]{:S(2)}) collective-permute-start(bf16[5,64,512]{2,1,0:T(8,128)(2,1)S(1)} %cut_piece.1), channel_id=1, source_target_pairs={{0,1},{1,0},{2,3},{3,2},{4,5},{5,4},{6,7},{7,6},{8,9},{9,8},{10,11... | collective-permute-start | bytes 983048 | tf_op jit(solution)/shard_map/ppermute | solution.py:68
  12.4 8.9 %collective-permute-start.2 = (bf16[5,64,512]{2,1,0:T(8,128)(2,1)S(1)}, bf16[5,64,512]{2,1,0:T(8,128)(2,1)S(1)}, u32[]{:S(2)}, u32[]{:S(2)}) collective-permute-start(bf16[5,64,512]{2,1,0:T(8,128)(2,1)S(1)} %after.9._.token.refs_14_), channel_id=1, source_target_pairs={{0,8},{2,10},{4,12},{6,14},{8,0},{10,2},{12,4},{14,6},{16,24},{18,... | collective-permute-start | bytes 983048 | tf_op jit(solution)/shard_map/ppermute | solution.py:64
  14.2 8.3 %collective-permute-start.1 = (bf16[5,64,512]{2,1,0:T(8,128)(2,1)S(1)}, bf16[5,64,512]{2,1,0:T(8,128)(2,1)S(1)}, u32[]{:S(2)}, u32[]{:S(2)}) collective-permute-start(bf16[5,64,512]{2,1,0:T(8,128)(2,1)S(1)} %after.9._.token.refs_14_), channel_id=1, source_target_pairs={{0,4},{2,6},{4,0},{6,2},{8,12},{10,14},{12,8},{14,10},{16,20},{18,... | collective-permute-start | bytes 983048 | tf_op jit(solution)/shard_map/ppermute | solution.py:64
  15.7 8.4 %collective-permute-start.3 = (bf16[336,512]{1,0:T(8,128)(2,1)S(1)}, bf16[336,512]{1,0:T(8,128)(2,1)S(1)}, u32[]{:S(2)}, u32[]{:S(2)}) collective-permute-start(bf16[336,512]{1,0:T(8,128)(2,1)S(1)} %after.10), channel_id=1, source_target_pairs={{0,1},{1,0},{2,3},{3,2},{4,5},{5,4},{6,7},{7,6},{8,9},{9,8},{10,11... | collective-permute-start | bytes 1032200 | tf_op jit(solution)/shard_map/ppermute | solution.py:68
  22.6 3.7 %collective-permute-start.5 = (bf16[10,64,512]{2,1,0:T(8,128)(2,1)S(1)}, bf16[10,64,512]{2,1,0:T(8,128)(2,1)S(1)}, u32[]{:S(2)}, u32[]{:S(2)}) collective-permute-start(bf16[10,64,512]{2,1,0:T(8,128)(2,1)S(1)} %both.1.refs_15_), channel_id=1, source_target_pairs={{0,2},{2,0},{4,6},{6,4},{8,10},{10,8},{12,14},{14,12},{16,18},{18,... | collective-permute-start | bytes 1966088 | tf_op jit(solution)/shard_map/ppermute | solution.py:64
  24.1 2.1 %collective-permute-start.6 = (bf16[336,512]{1,0:T(8,128)(2,1)S(1)}, bf16[336,512]{1,0:T(8,128)(2,1)S(1)}, u32[]{:S(2)}, u32[]{:S(2)}) collective-permute-start(bf16[336,512]{1,0:T(8,128)(2,1)S(1)} %collective-permute-done.3.refs_16_), channel_id=1, source_target_pairs={{0,2},{2,0},{4,6},{6,4},{8,10},{10,8},{12,14},{14,12},{16,18},{18,... | collective-permute-start | bytes 1032200 | tf_op jit(solution)/shard_map/ppermute | solution.py:64
  24.1 2.1 %collective-permute-start.4 = (bf16[5,64,512]{2,1,0:T(8,128)(2,1)S(1)}, bf16[5,64,512]{2,1,0:T(8,128)(2,1)S(1)}, u32[]{:S(2)}, u32[]{:S(2)}) collective-permute-start(bf16[5,64,512]{2,1,0:T(8,128)(2,1)S(1)} %after.9._.token.refs_14_), channel_id=1, source_target_pairs={{0,2},{2,0},{4,6},{6,4},{8,10},{10,8},{12,14},{14,12},{16,18},{18,... | collective-permute-start | bytes 983048 | tf_op jit(solution)/shard_map/ppermute | solution.py:64
  26.2 23.0 %copy-start.1 = (f32[512]{0:T(512)S(1)}, f32[512]{0:T(512)}, u32[]{:S(2)}) copy-start(f32[512]{0:T(512)} %param.19) | copy-start | bytes 6148
  26.2 23.0 %copy-start.3 = (s32[4]{0:T(128)S(1)}, s32[4]{0:T(128)}, u32[]{:S(2)}) copy-start(s32[4]{0:T(128)} %species.1) | copy-start | bytes 52
  26.3 23.0 %copy-start.4 = (s32[16]{0:T(128)S(1)}, s32[16]{0:T(128)}, u32[]{:S(2)}) copy-start(s32[16]{0:T(128)} %counts.1) | copy-start | bytes 196
  49.0 4.2 %collective-permute-start.7 = (bf16[2048,512]{1,0:T(8,128)(2,1)S(1)}, bf16[2048,512]{1,0:T(8,128)(2,1)S(1)}, u32[]{:S(2)}, u32[]{:S(2)}) collective-permute-start(bf16[2048,512]{1,0:T(8,128)(2,1)S(1)} %get-tuple-element.94), channel_id=1, source_target_pairs={{0,2},{2,0},{4,6},{6,4},{8,10},{10,8},{12,14},{14,12},{16,18},{18,... | collective-permute-start | bytes 6291464 | tf_op jit(solution)/shard_map/ppermute | solution.py:64
  53.2 3.0 %copy-start.2 = (s32[5]{0:T(128)S(1)}, s32[5]{0:T(128)}, u32[]{:S(2)}) copy-start(s32[5]{0:T(128)} %get-tuple-element.85.other_table.table) | copy-start | bytes 64
  53.7 14.2 %collective-permute-start.10 = (bf16[512,512]{1,0:T(8,128)(2,1)S(1)}, bf16[512,512]{1,0:T(8,128)(2,1)S(1)}, u32[]{:S(2)}, u32[]{:S(2)}) collective-permute-start(bf16[512,512]{1,0:T(8,128)(2,1)S(1)} %get-tuple-element.100), channel_id=1, source_target_pairs={{0,4},{1,5},{2,6},{3,7},{4,0},{5,1},{6,2},{7,3},{8,12},{9,13},{10,... | collective-permute-start | bytes 1572872 | tf_op jit(solution)/shard_map/ppermute | solution.py:817
  54.8 13.9 %collective-permute-start.9 = (bf16[512,512]{1,0:T(8,128)(2,1)S(1)}, bf16[512,512]{1,0:T(8,128)(2,1)S(1)}, u32[]{:S(2)}, u32[]{:S(2)}) collective-permute-start(bf16[512,512]{1,0:T(8,128)(2,1)S(1)} %get-tuple-element.96.refs_0_), channel_id=1, source_target_pairs={{0,1},{1,0},{2,3},{3,2},{4,5},{5,4},{6,7},{7,6},{8,9},{9,8},{10,11... | collective-permute-start | bytes 1572872 | tf_op jit(solution)/shard_map/ppermute | solution.py:817
  61.4 15.8 %collective-permute-start.11 = (bf16[1536,512]{1,0:T(8,128)(2,1)S(1)}, bf16[1536,512]{1,0:T(8,128)(2,1)S(1)}, u32[]{:S(2)}, u32[]{:S(2)}) collective-permute-start(bf16[1536,512]{1,0:T(8,128)(2,1)S(1)} %get-tuple-element.105), channel_id=1, source_target_pairs={{0,2},{2,0},{4,6},{6,4},{8,10},{10,8},{12,14},{14,12},{16,18},{18,... | collective-permute-start | bytes 4718600 | tf_op jit(solution)/shard_map/ppermute | solution.py:64
  65.3 6.1 %collective-permute-start.8 = (bf16[1040,512]{1,0:T(8,128)(2,1)S(1)}, bf16[1040,512]{1,0:T(8,128)(2,1)S(1)}, u32[]{:S(2)}, u32[]{:S(2)}) collective-permute-start(bf16[1040,512]{1,0:T(8,128)(2,1)S(1)} %get-tuple-element.98), channel_id=1, source_target_pairs={{0,2},{2,0},{4,6},{6,4},{8,10},{10,8},{12,14},{14,12},{16,18},{18,... | collective-permute-start | bytes 3194888 | tf_op jit(solution)/shard_map/ppermute | solution.py:64
  68.8 7.5 %collective-permute-start.12 = (bf16[256,512]{1,0:T(8,128)(2,1)S(1)}, bf16[256,512]{1,0:T(8,128)(2,1)S(1)}, u32[]{:S(2)}, u32[]{:S(2)}) collective-permute-start(bf16[256,512]{1,0:T(8,128)(2,1)S(1)} %get-tuple-element.106), channel_id=1, source_target_pairs={{0,4},{1,5},{2,6},{3,7},{4,0},{5,1},{6,2},{7,3},{8,12},{9,13},{10,... | collective-permute-start | bytes 786440 | tf_op jit(solution)/shard_map/ppermute | solution.py:817
  69.9 7.1 %collective-permute-start.13 = (bf16[256,512]{1,0:T(8,128)(2,1)S(1)}, bf16[256,512]{1,0:T(8,128)(2,1)S(1)}, u32[]{:S(2)}, u32[]{:S(2)}) collective-permute-start(bf16[256,512]{1,0:T(8,128)(2,1)S(1)} %get-tuple-element.107), channel_id=1, source_target_pairs={{0,1},{1,0},{2,3},{3,2},{4,5},{5,4},{6,7},{7,6},{8,9},{9,8},{10,11... | collective-permute-start | bytes 786440 | tf_op jit(solution)/shard_map/ppermute | solution.py:817
  71.7 15.3 %collective-permute-start.16 = (bf16[528,512]{1,0:T(8,128)(2,1)S(1)}, bf16[528,512]{1,0:T(8,128)(2,1)S(1)}, u32[]{:S(2)}, u32[]{:S(2)}) collective-permute-start(bf16[528,512]{1,0:T(8,128)(2,1)S(1)} %get-tuple-element.113), channel_id=1, source_target_pairs={{0,8},{1,9},{2,10},{3,11},{4,12},{5,13},{6,14},{7,15},{8,0},{9,1},... | collective-permute-start | bytes 1622024 | tf_op jit(solution)/shard_map/ppermute | solution.py:817
  77.4 9.5 %collective-permute-start.14 = (bf16[384,512]{1,0:T(8,128)(2,1)S(1)}, bf16[384,512]{1,0:T(8,128)(2,1)S(1)}, u32[]{:S(2)}, u32[]{:S(2)}) collective-permute-start(bf16[384,512]{1,0:T(8,128)(2,1)S(1)} %get-tuple-element.111), channel_id=1, source_target_pairs={{0,1},{1,0},{2,3},{3,2},{4,5},{5,4},{6,7},{7,6},{8,9},{9,8},{10,11... | collective-permute-start | bytes 1179656 | tf_op jit(solution)/shard_map/ppermute | solution.py:817
  79.0 8.7 %collective-permute-start.15 = (bf16[384,512]{1,0:T(8,128)(2,1)S(1)}, bf16[384,512]{1,0:T(8,128)(2,1)S(1)}, u32[]{:S(2)}, u32[]{:S(2)}) collective-permute-start(bf16[384,512]{1,0:T(8,128)(2,1)S(1)} %get-tuple-element.112), channel_id=1, source_target_pairs={{0,4},{1,5},{2,6},{3,7},{4,0},{5,1},{6,2},{7,3},{8,12},{9,13},{10,... | collective-permute-start | bytes 1179656 | tf_op jit(solution)/shard_map/ppermute | solution.py:817
  79.9 10.2 %collective-permute-start.19 = (bf16[256,512]{1,0:T(8,128)(2,1)S(1)}, bf16[256,512]{1,0:T(8,128)(2,1)S(1)}, u32[]{:S(2)}, u32[]{:S(2)}) collective-permute-start(bf16[256,512]{1,0:T(8,128)(2,1)S(1)} %get-tuple-element.119), channel_id=1, source_target_pairs={{0,8},{1,9},{2,10},{3,11},{4,12},{5,13},{6,14},{7,15},{8,0},{9,1},... | collective-permute-start | bytes 786440 | tf_op jit(solution)/shard_map/ppermute | solution.py:817
  87.9 8.0 %collective-permute-start.18 = (bf16[336,512]{1,0:T(8,128)(2,1)S(1)}, bf16[336,512]{1,0:T(8,128)(2,1)S(1)}, u32[]{:S(2)}, u32[]{:S(2)}) collective-permute-start(bf16[336,512]{1,0:T(8,128)(2,1)S(1)} %get-tuple-element.117), channel_id=1, source_target_pairs={{0,1},{1,0},{2,3},{3,2},{4,5},{5,4},{6,7},{7,6},{8,9},{9,8},{10,11... | collective-permute-start | bytes 1032200 | tf_op jit(solution)/shard_map/ppermute | solution.py:817
  88.5 7.1 %collective-permute-start.17 = (bf16[320,512]{1,0:T(8,128)(2,1)S(1)}, bf16[320,512]{1,0:T(8,128)(2,1)S(1)}, u32[]{:S(2)}, u32[]{:S(2)}) collective-permute-start(bf16[320,512]{1,0:T(8,128)(2,1)S(1)} %get-tuple-element.116), channel_id=1, source_target_pairs={{0,4},{1,5},{2,6},{3,7},{4,0},{5,1},{6,2},{7,3},{8,12},{9,13},{10,... | collective-permute-start | bytes 983048 | tf_op jit(solution)/shard_map/ppermute | solution.py:817
  90.2 9.0 %collective-permute-start.23 = (bf16[128,512]{1,0:T(8,128)(2,1)S(1)}, bf16[128,512]{1,0:T(8,128)(2,1)S(1)}, u32[]{:S(2)}, u32[]{:S(2)}) collective-permute-start(bf16[128,512]{1,0:T(8,128)(2,1)S(1)} %get-tuple-element.129), channel_id=1, source_target_pairs={{0,16},{1,17},{2,18},{3,19},{4,20},{5,21},{6,22},{7,23},{8,24},{9,... | collective-permute-start | bytes 393224 | tf_op jit(solution)/shard_map/ppermute | solution.py:817
  96.0 6.7 %collective-permute-start.20 = (bf16[192,512]{1,0:T(8,128)(2,1)S(1)}, bf16[192,512]{1,0:T(8,128)(2,1)S(1)}, u32[]{:S(2)}, u32[]{:S(2)}) collective-permute-start(bf16[192,512]{1,0:T(8,128)(2,1)S(1)} %get-tuple-element.121), channel_id=1, source_target_pairs={{0,8},{1,9},{2,10},{3,11},{4,12},{5,13},{6,14},{7,15},{8,0},{9,1},... | collective-permute-start | bytes 589832 | tf_op jit(solution)/shard_map/ppermute | solution.py:817
  96.4 4.3 %collective-permute-start.22 = (bf16[64,512]{1,0:T(8,128)(2,1)S(1)}, bf16[64,512]{1,0:T(8,128)(2,1)S(1)}, u32[]{:S(2)}, u32[]{:S(2)}) collective-permute-start(bf16[64,512]{1,0:T(8,128)(2,1)S(1)} %get-tuple-element.126), channel_id=1, source_target_pairs={{0,1},{1,0},{2,3},{3,2},{4,5},{5,4},{6,7},{7,6},{8,9},{9,8},{10,11... | collective-permute-start | bytes 196616 | tf_op jit(solution)/shard_map/ppermute | solution.py:817
  98.3 4.4 %collective-permute-start.21 = (bf16[80,512]{1,0:T(8,128)(2,1)S(1)}, bf16[80,512]{1,0:T(8,128)(2,1)S(1)}, u32[]{:S(2)}, u32[]{:S(2)}) collective-permute-start(bf16[80,512]{1,0:T(8,128)(2,1)S(1)} %get-tuple-element.125), channel_id=1, source_target_pairs={{0,4},{1,5},{2,6},{3,7},{4,0},{5,1},{6,2},{7,3},{8,12},{9,13},{10,... | collective-permute-start | bytes 245768 | tf_op jit(solution)/shard_map/ppermute | solution.py:817
  102.8 8.4 %collective-permute-start.24 = (bf16[176,512]{1,0:T(8,128)(2,1)S(1)}, bf16[176,512]{1,0:T(8,128)(2,1)S(1)}, u32[]{:S(2)}, u32[]{:S(2)}) collective-permute-start(bf16[176,512]{1,0:T(8,128)(2,1)S(1)} %get-tuple-element.130), channel_id=1, source_target_pairs={{0,16},{1,17},{2,18},{3,19},{4,20},{5,21},{6,22},{7,23},{8,24},{9,... | collective-permute-start | bytes 540680 | tf_op jit(solution)/shard_map/ppermute | solution.py:817

commit v4 on v3

--- a/solution.py
+++ b/solution.py
@@ -505,15 +505,13 @@
 
     size = out_block // 2
 
-    @pl.loop(0, chunks // 2)
-    def _(pair):
+    for pair in range(chunks // 2):
         for spot in range(2):
             at = pl.multiple_of((pair * 2 + spot) * COLS, COLS)
             result[spot] = contract_rows(act[:, pl.ds(at, COLS)], d_out[...])
             hand_out(spot, at, out_block, [(0, 0, size, 0), (1, size, size, 0)])
 
-    @pl.loop(0, chunks // 2)
-    def _(step):
+    for step in range(chunks // 2):
         shift = size + step * in_block
         for spot in range(2):
             at = pl.multiple_of((spot * (chunks // 2) + step) * COLS, COLS)

time: 112 us -> 112 us (level)
  no operation moved by 1% of the time
where the time goes in v4:
time: 112 us; the launch traced here: 111 us
  Pallas kernels  53.4 us (48%)
  starting transfers between devices  29 us (26%)
  waiting for transfers between devices  28.1 us (25%)
    pallas_call x1, Pallas kernels, fast_shards(): pl.pallas_call(functools.partial(main_kernel, orders, dp_bits, [turn for...  22.1 us
    ppermute x15, starting transfers between devices, swap(): lax.ppermute(value, ('dp', 'tap'), [(i, i ^ mask) for i in range(count)])  19.7 us
    ppermute x15, waiting for transfers between devices, swap(): lax.ppermute(value, ('dp', 'tap'), [(i, i ^ mask) for i in range(count)])  18.8 us
    pallas_call x2, Pallas kernels, terms(): pl.pallas_call(functools.partial(terms_kernel, group, orders, dp_bits, sm...  8.92 us
    ppermute x2, waiting for transfers between devices, swap_tap(): return lax.ppermute(value, 'tap', [(0, 1), (1, 0)])  5.68 us
    ppermute x8, starting transfers between devices, swap_dp(): return lax.ppermute(value, 'dp', [(i, i ^ 1 << bit) for i in range(count)])  4.77 us
    ppermute x2, starting transfers between devices, swap_tap(): return lax.ppermute(value, 'tap', [(0, 1), (1, 0)])  4.49 us
    pallas_call x1, Pallas kernels, fast_shards(): pl.pallas_call(input_far_kernel, out_shape=[pltpu.HBM(rows_f, F32), vmem(...  4.44 us
  transfers between devices with their start and end apart: 25, of which 18 were waited for; matrix products, arithmetic and copies ran while one was open for 0% of the time, Pallas kernels for 26%

profile of v4, /device:TPU:0, one launch (start us, length us, event | category | flops | bytes accessed | tf_op | source)
XLA Modules:
  0.0 111.4 jit_solution(13480379532764912088)
XLA Ops:
  0.7 1.0 cut_piece.1
  1.7 3.0 %collective-permute-start = (bf16[5,64,512]{2,1,0:T(8,128)(2,1)S(1)}, bf16[5,64,512]{2,1,0:T(8,128)(2,1)S(1)}, u32[]{:S(2)}, u32[]{:S(2)}) collective-permute-start(bf16[5,64,512]{2,1,0:T(8,128)(2,1)S(1)} %cut_piece.1), channel_id=1, source_target_pairs={{0,1},{1,0},{2,3},{3,2},{4,5},{5,4},{6,7},{7,6},{8,9},{9,8},{10,11... | collective-permute-start | bytes 983048 | tf_op jit(solution)/shard_map/ppermute | solution.py:68
  4.7 3.5 %load.1 = (bf16[2,640,512]{2,1,0:T(8,128)(2,1)S(1)}, bf16[5,512,512]{2,1,0:T(8,128)(2,1)S(1)}, bf16[512,2048]{1,0:T(8,128)(2,1)S(1)}, bf16[336,512]{1,0:T(8,128)(2,1)S(1)}) custom-call(s32[5]{0:T(128)S(1)} %copy-done, bf16[2048,512]{1,0:T(8,128)(2,1)} %x_hbm.1, bf16[5,512,512]{2,1,0:T(8,128)(2,1)} %weight_hbm.3, bf16[512,2048]{1,0:T(8,128)(2,1)} %w_in_hbm.1), custom_call_target="tpu_custom_call" | custom-call | bytes 1 | tf_op jit(solution)/shard_map/load/pallas_call | solution.py:917
  8.2 4.2 %collective-permute-done._ = bf16[5,64,512]{2,1,0:T(8,128)(2,1)S(1)} collective-permute-done((bf16[5,64,512]{2,1,0:T(8,128)(2,1)S(1)}, bf16[5,64,512]{2,1,0:T(8,128)(2,1)S(1)}, u32[]{:S(2)}, u32[]{:S(2)}) %collective-permute-start) | collective-permute-done | bytes 327712 | tf_op jit(solution)/shard_map/ppermute | solution.py:68
  12.4 1.8 %collective-permute-start.2 = (bf16[5,64,512]{2,1,0:T(8,128)(2,1)S(1)}, bf16[5,64,512]{2,1,0:T(8,128)(2,1)S(1)}, u32[]{:S(2)}, u32[]{:S(2)}) collective-permute-start(bf16[5,64,512]{2,1,0:T(8,128)(2,1)S(1)} %after.9._.token.refs_14_), channel_id=1, source_target_pairs={{0,8},{2,10},{4,12},{6,14},{8,0},{10,2},{12,4},{14,6},{16,24},{18,... | collective-permute-start | bytes 983048 | tf_op jit(solution)/shard_map/ppermute | solution.py:64
  14.2 1.5 %collective-permute-start.1 = (bf16[5,64,512]{2,1,0:T(8,128)(2,1)S(1)}, bf16[5,64,512]{2,1,0:T(8,128)(2,1)S(1)}, u32[]{:S(2)}, u32[]{:S(2)}) collective-permute-start(bf16[5,64,512]{2,1,0:T(8,128)(2,1)S(1)} %after.9._.token.refs_14_), channel_id=1, source_target_pairs={{0,4},{2,6},{4,0},{6,2},{8,12},{10,14},{12,8},{14,10},{16,20},{18,... | collective-permute-start | bytes 983048 | tf_op jit(solution)/shard_map/ppermute | solution.py:64
  15.7 1.5 %collective-permute-start.3 = (bf16[336,512]{1,0:T(8,128)(2,1)S(1)}, bf16[336,512]{1,0:T(8,128)(2,1)S(1)}, u32[]{:S(2)}, u32[]{:S(2)}) collective-permute-start(bf16[336,512]{1,0:T(8,128)(2,1)S(1)} %after.10), channel_id=1, source_target_pairs={{0,1},{1,0},{2,3},{3,2},{4,5},{5,4},{6,7},{7,6},{8,9},{9,8},{10,11... | collective-permute-start | bytes 1032200 | tf_op jit(solution)/shard_map/ppermute | solution.py:68
  17.2 3.4 %own_conv.1 = (f32[1024,512]{1,0:T(8,128)S(1)}, f32[8,128]{1,0:T(8,128)S(1)}) custom-call(s32[5]{0:T(128)S(1)} %copy-done, bf16[2,640,512]{2,1,0:T(8,128)(2,1)S(1)} %get-tuple-element.78.token.x_pad.refs_2_, bf16[5,512,512]{2,1,0:T(8,128)(2,1)S(1)} %get-tuple-element.79.weight, bf16[5,64,512]{2,1,0:T(8,128)(2,1)S(1)} %after.9._.token.refs_14_), custom_call_target="tpu_custom_call" | custom-call | bytes 1 | tf_op jit(solution)/shard_map/own_conv/pallas_call | solution.py:933
  21.3 1.2 %collective-permute-done.1.over_one = bf16[5,64,512]{2,1,0:T(8,128)(2,1)S(1)} collective-permute-done((bf16[5,64,512]{2,1,0:T(8,128)(2,1)S(1)}, bf16[5,64,512]{2,1,0:T(8,128)(2,1)S(1)}, u32[]{:S(2)}, u32[]{:S(2)}) %collective-permute-start.1) | collective-permute-done | bytes 327712 | tf_op jit(solution)/shard_map/ppermute | solution.py:64
  22.6 1.5 %collective-permute-done.3.refs_16_ = bf16[336,512]{1,0:T(8,128)(2,1)S(1)} collective-permute-done((bf16[336,512]{1,0:T(8,128)(2,1)S(1)}, bf16[336,512]{1,0:T(8,128)(2,1)S(1)}, u32[]{:S(2)}, u32[]{:S(2)}) %collective-permute-start.3) | collective-permute-done | bytes 344096 | tf_op jit(solution)/shard_map/ppermute | solution.py:68
  24.6 1.6 %collective-permute-done.4.refs_17_ = bf16[5,64,512]{2,1,0:T(8,128)(2,1)S(1)} collective-permute-done((bf16[5,64,512]{2,1,0:T(8,128)(2,1)S(1)}, bf16[5,64,512]{2,1,0:T(8,128)(2,1)S(1)}, u32[]{:S(2)}, u32[]{:S(2)}) %collective-permute-start.4) | collective-permute-done | bytes 327712 | tf_op jit(solution)/shard_map/ppermute | solution.py:64
  26.3 22.1 %main_rows.1 = (bf16[1024,512]{1,0:T(8,128)(2,1)}, f32[1024,512]{1,0:T(8,128)S(1)}, f32[1024,512]{1,0:T(8,128)S(1)}, bf16[1024,2048]{1,0:T(8,128)(2,1)S(1)}, bf1...) custom-call(s32[4]{0:T(128)} %species.1, ...), custom_call_target="tpu_custom_call" | custom-call | bytes 1 | tf_op jit(solution)/shard_map/main_rows/pallas_call | solution.py:946
  48.6 3.9 %back_rows.1 = (bf16[2,640,512]{2,1,0:T(8,128)(2,1)S(1)}, f32[1024,512]{1,0:T(8,128)S(1)}, f32[16,512]{1,0:T(8,128)S(1)}) custom-call(s32[4]{0:T(128)S(1)} %copy-done.3, s32[16]{0:T(128)S(1)} %copy-done.4, bf16[1024,512]{1,0:T(8,128)(2,1)S(1)} %get-tuple-element.86.grad_in, bf16[512,2048]{1,0:T(8,128)(2,1)S(1)} %get-tuple-element.81.refs_5_.w_in, ...), custom_call_target="tpu_custom_call" | custom-call | bytes 1 | tf_op jit(solution)/shard_map/back_rows/pallas_call | solution.py:999
  53.1 1.0 collective-permute-start.10
  54.2 1.5 %collective-permute-start.9 = (bf16[512,512]{1,0:T(8,128)(2,1)S(1)}, bf16[512,512]{1,0:T(8,128)(2,1)S(1)}, u32[]{:S(2)}, u32[]{:S(2)}) collective-permute-start(bf16[512,512]{1,0:T(8,128)(2,1)S(1)} %get-tuple-element.96.refs_0_), channel_id=1, source_target_pairs={{0,1},{1,0},{2,3},{3,2},{4,5},{5,4},{6,7},{7,6},{8,9},{9,8},{10,11... | collective-permute-start | bytes 1572872 | tf_op jit(solution)/shard_map/ppermute | solution.py:815
  55.7 5.3 %terms_a.1 = (f32[1536,512]{1,0:T(8,128)S(1)}, bf16[1536,512]{1,0:T(8,128)(2,1)S(1)}) custom-call(s32[5]{0:T(128)S(1)} %copy-done, s32[5]{0:T(128)S(1)} %copy-done.2, bf16[2,640,512]{2,1,0:T(8,128)(2,1)S(1)} %get-tuple-element.78.token.x_pad.refs_2_, bf16[2,640,512]{2,1,0:T(8,128)(2,1)S(1)} %get-tuple-element.91.d_pad, ...), custom_call_target="tpu_custom_call" | custom-call | bytes 1 | tf_op jit(solution)/shard_map/terms_a/pallas_call | solution.py:1031
  61.1 3.6 %terms_b.1 = (f32[1024,512]{1,0:T(8,128)S(1)}, bf16[1040,512]{1,0:T(8,128)(2,1)S(1)}) custom-call(s32[5]{0:T(128)S(1)} %copy-done, s32[5]{0:T(128)S(1)} %copy-done.2, bf16[2,640,512]{2,1,0:T(8,128)(2,1)S(1)} %get-tuple-element.78.token.x_pad.refs_2_, bf16[2,640,512]{2,1,0:T(8,128)(2,1)S(1)} %get-tuple-element.91.d_pad, ...), custom_call_target="tpu_custom_call" | custom-call | bytes 1 | tf_op jit(solution)/shard_map/terms_b/pallas_call | solution.py:1031
  65.2 2.1 %collective-permute-done.10.refs_1_ = bf16[512,512]{1,0:T(8,128)(2,1)S(1)} collective-permute-done((bf16[512,512]{1,0:T(8,128)(2,1)S(1)}, bf16[512,512]{1,0:T(8,128)(2,1)S(1)}, u32[]{:S(2)}, u32[]{:S(2)}) %collective-permute-start.10) | collective-permute-done | bytes 524320 | tf_op jit(solution)/shard_map/ppermute | solution.py:815
  68.2 1.1 %collective-permute-start.12 = (bf16[256,512]{1,0:T(8,128)(2,1)S(1)}, bf16[256,512]{1,0:T(8,128)(2,1)S(1)}, u32[]{:S(2)}, u32[]{:S(2)}) collective-permute-start(bf16[256,512]{1,0:T(8,128)(2,1)S(1)} %get-tuple-element.106), channel_id=1, source_target_pairs={{0,4},{1,5},{2,6},{3,7},{4,0},{5,1},{6,2},{7,3},{8,12},{9,13},{10,... | collective-permute-start | bytes 786440 | tf_op jit(solution)/shard_map/ppermute | solution.py:815
  69.3 1.5 %collective-permute-start.13 = (bf16[256,512]{1,0:T(8,128)(2,1)S(1)}, bf16[256,512]{1,0:T(8,128)(2,1)S(1)}, u32[]{:S(2)}, u32[]{:S(2)}) collective-permute-start(bf16[256,512]{1,0:T(8,128)(2,1)S(1)} %get-tuple-element.107), channel_id=1, source_target_pairs={{0,1},{1,0},{2,3},{3,2},{4,5},{5,4},{6,7},{7,6},{8,9},{9,8},{10,11... | collective-permute-start | bytes 786440 | tf_op jit(solution)/shard_map/ppermute | solution.py:815
  71.6 3.4 %input_near.1.refs_3_.base = f32[1024,512]{1,0:T(8,128)S(1)} custom-call(s32[5]{0:T(128)S(1)} %copy-done, bf16[2,640,512]{2,1,0:T(8,128)(2,1)S(1)} %get-tuple-element.91.d_pad, f32[1024,512]{1,0:T(8,128)S(1)} %get-tuple-element.92.base, bf16[5,512,512]{2,1,0:T(8,128)(2,1)S(1)} %get-tuple-element.79.weight, f32[512,512]{1,0:T(8,128)S(1)} %get-tuple-element.103._.refs_4_), custom_call_target="tpu_custom_call" | custom-call | bytes 1 | tf_op jit(solution)/shard_map/input_near/pallas_call | solution.py:1076
  76.8 1.6 %collective-permute-start.14 = (bf16[384,512]{1,0:T(8,128)(2,1)S(1)}, bf16[384,512]{1,0:T(8,128)(2,1)S(1)}, u32[]{:S(2)}, u32[]{:S(2)}) collective-permute-start(bf16[384,512]{1,0:T(8,128)(2,1)S(1)} %get-tuple-element.111), channel_id=1, source_target_pairs={{0,1},{1,0},{2,3},{3,2},{4,5},{5,4},{6,7},{7,6},{8,9},{9,8},{10,11... | collective-permute-start | bytes 1179656 | tf_op jit(solution)/shard_map/ppermute | solution.py:815
  78.4 1.0 collective-permute-start.15
  79.8 4.4 %input_far.1 = (f32[1024,512]{1,0:T(8,128)}, f32[8,128]{1,0:T(8,128)S(1)}) custom-call(s32[5]{0:T(128)S(1)} %copy-done.2, bf16[2,640,512]{2,1,0:T(8,128)(2,1)S(1)} %get-tuple-element.91.d_pad, f32[1024,512]{1,0:T(8,128)S(1)} %input_near.1.refs_3_.base, bf16[5,512,512]{2,1,0:T(8,128)(2,1)S(1)} %get-tuple-element.104.weight, ...), custom_call_target="tpu_custom_call" | custom-call | bytes 1 | tf_op jit(solution)/shard_map/input_far/pallas_call | solution.py:1094
  84.3 2.1 %collective-permute-done.16.refs_2_ = bf16[528,512]{1,0:T(8,128)(2,1)S(1)} collective-permute-done((bf16[528,512]{1,0:T(8,128)(2,1)S(1)}, bf16[528,512]{1,0:T(8,128)(2,1)S(1)}, u32[]{:S(2)}, u32[]{:S(2)}) %collective-permute-start.16) | collective-permute-done | bytes 540704 | tf_op jit(solution)/shard_map/ppermute | solution.py:815
  89.6 3.4 %collective-permute-start.23 = (bf16[128,512]{1,0:T(8,128)(2,1)S(1)}, bf16[128,512]{1,0:T(8,128)(2,1)S(1)}, u32[]{:S(2)}, u32[]{:S(2)}) collective-permute-start(bf16[128,512]{1,0:T(8,128)(2,1)S(1)} %get-tuple-element.129), channel_id=1, source_target_pairs={{0,16},{1,17},{2,18},{3,19},{4,20},{5,21},{6,22},{7,23},{8,24},{9,... | collective-permute-start | bytes 393224 | tf_op jit(solution)/shard_map/ppermute | solution.py:815
  93.0 2.0 %collective-permute-done.17.refs_0_ = bf16[320,512]{1,0:T(8,128)(2,1)S(1)} collective-permute-done((bf16[320,512]{1,0:T(8,128)(2,1)S(1)}, bf16[320,512]{1,0:T(8,128)(2,1)S(1)}, u32[]{:S(2)}, u32[]{:S(2)}) %collective-permute-start.17) | collective-permute-done | bytes 327712 | tf_op jit(solution)/shard_map/ppermute | solution.py:815
  95.8 1.9 %collective-permute-start.22 = (bf16[64,512]{1,0:T(8,128)(2,1)S(1)}, bf16[64,512]{1,0:T(8,128)(2,1)S(1)}, u32[]{:S(2)}, u32[]{:S(2)}) collective-permute-start(bf16[64,512]{1,0:T(8,128)(2,1)S(1)} %get-tuple-element.126), channel_id=1, source_target_pairs={{0,1},{1,0},{2,3},{3,2},{4,5},{5,4},{6,7},{7,6},{8,9},{9,8},{10,11... | collective-permute-start | bytes 196616 | tf_op jit(solution)/shard_map/ppermute | solution.py:815
  98.7 1.4 %collective-permute-done.22.refs_2_ = bf16[64,512]{1,0:T(8,128)(2,1)S(1)} collective-permute-done((bf16[64,512]{1,0:T(8,128)(2,1)S(1)}, bf16[64,512]{1,0:T(8,128)(2,1)S(1)}, u32[]{:S(2)}, u32[]{:S(2)}) %collective-permute-start.22) | collective-permute-done | bytes 65568 | tf_op jit(solution)/shard_map/ppermute | solution.py:815
  100.1 2.0 %collective-permute-done.21.refs_1_ = bf16[80,512]{1,0:T(8,128)(2,1)S(1)} collective-permute-done((bf16[80,512]{1,0:T(8,128)(2,1)S(1)}, bf16[80,512]{1,0:T(8,128)(2,1)S(1)}, u32[]{:S(2)}, u32[]{:S(2)}) %collective-permute-start.21) | collective-permute-done | bytes 81952 | tf_op jit(solution)/shard_map/ppermute | solution.py:815
  102.2 2.9 %collective-permute-start.24 = (bf16[176,512]{1,0:T(8,128)(2,1)S(1)}, bf16[176,512]{1,0:T(8,128)(2,1)S(1)}, u32[]{:S(2)}, u32[]{:S(2)}) collective-permute-start(bf16[176,512]{1,0:T(8,128)(2,1)S(1)} %get-tuple-element.130), channel_id=1, source_target_pairs={{0,16},{1,17},{2,18},{3,19},{4,20},{5,21},{6,22},{7,23},{8,24},{9,... | collective-permute-start | bytes 540680 | tf_op jit(solution)/shard_map/ppermute | solution.py:815
  105.1 5.4 %collective-permute-done.24.got = bf16[176,512]{1,0:T(8,128)(2,1)S(1)} collective-permute-done((bf16[176,512]{1,0:T(8,128)(2,1)S(1)}, bf16[176,512]{1,0:T(8,128)(2,1)S(1)}, u32[]{:S(2)}, u32[]{:S(2)}) %collective-permute-start.24) | collective-permute-done | bytes 180256 | tf_op jit(solution)/shard_map/ppermute | solution.py:815
  (60 shorter events, 12.4 us)
Async XLA Ops:
  0.6 4.0 %copy-start = (s32[5]{0:T(128)S(1)}, s32[5]{0:T(128)}, u32[]{:S(2)}) copy-start(s32[5]{0:T(128)} %table.5) | copy-start | bytes 64
  1.7 10.7 %collective-permute-start = (bf16[5,64,512]{2,1,0:T(8,128)(2,1)S(1)}, bf16[5,64,512]{2,1,0:T(8,128)(2,1)S(1)}, u32[]{:S(2)}, u32[]{:S(2)}) collective-permute-start(bf16[5,64,512]{2,1,0:T(8,128)(2,1)S(1)} %cut_piece.1), channel_id=1, source_target_pairs={{0,1},{1,0},{2,3},{3,2},{4,5},{5,4},{6,7},{7,6},{8,9},{9,8},{10,11... | collective-permute-start | bytes 983048 | tf_op jit(solution)/shard_map/ppermute | solution.py:68
  12.4 8.9 %collective-permute-start.2 = (bf16[5,64,512]{2,1,0:T(8,128)(2,1)S(1)}, bf16[5,64,512]{2,1,0:T(8,128)(2,1)S(1)}, u32[]{:S(2)}, u32[]{:S(2)}) collective-permute-start(bf16[5,64,512]{2,1,0:T(8,128)(2,1)S(1)} %after.9._.token.refs_14_), channel_id=1, source_target_pairs={{0,8},{2,10},{4,12},{6,14},{8,0},{10,2},{12,4},{14,6},{16,24},{18,... | collective-permute-start | bytes 983048 | tf_op jit(solution)/shard_map/ppermute | solution.py:64
  14.2 8.3 %collective-permute-start.1 = (bf16[5,64,512]{2,1,0:T(8,128)(2,1)S(1)}, bf16[5,64,512]{2,1,0:T(8,128)(2,1)S(1)}, u32[]{:S(2)}, u32[]{:S(2)}) collective-permute-start(bf16[5,64,512]{2,1,0:T(8,128)(2,1)S(1)} %after.9._.token.refs_14_), channel_id=1, source_target_pairs={{0,4},{2,6},{4,0},{6,2},{8,12},{10,14},{12,8},{14,10},{16,20},{18,... | collective-permute-start | bytes 983048 | tf_op jit(solution)/shard_map/ppermute | solution.py:64
  15.7 8.4 %collective-permute-start.3 = (bf16[336,512]{1,0:T(8,128)(2,1)S(1)}, bf16[336,512]{1,0:T(8,128)(2,1)S(1)}, u32[]{:S(2)}, u32[]{:S(2)}) collective-permute-start(bf16[336,512]{1,0:T(8,128)(2,1)S(1)} %after.10), channel_id=1, source_target_pairs={{0,1},{1,0},{2,3},{3,2},{4,5},{5,4},{6,7},{7,6},{8,9},{9,8},{10,11... | collective-permute-start | bytes 1032200 | tf_op jit(solution)/shard_map/ppermute | solution.py:68
  22.6 3.7 %collective-permute-start.5 = (bf16[10,64,512]{2,1,0:T(8,128)(2,1)S(1)}, bf16[10,64,512]{2,1,0:T(8,128)(2,1)S(1)}, u32[]{:S(2)}, u32[]{:S(2)}) collective-permute-start(bf16[10,64,512]{2,1,0:T(8,128)(2,1)S(1)} %both.1.refs_15_), channel_id=1, source_target_pairs={{0,2},{2,0},{4,6},{6,4},{8,10},{10,8},{12,14},{14,12},{16,18},{18,... | collective-permute-start | bytes 1966088 | tf_op jit(solution)/shard_map/ppermute | solution.py:64
  24.1 2.1 %collective-permute-start.6 = (bf16[336,512]{1,0:T(8,128)(2,1)S(1)}, bf16[336,512]{1,0:T(8,128)(2,1)S(1)}, u32[]{:S(2)}, u32[]{:S(2)}) collective-permute-start(bf16[336,512]{1,0:T(8,128)(2,1)S(1)} %collective-permute-done.3.refs_16_), channel_id=1, source_target_pairs={{0,2},{2,0},{4,6},{6,4},{8,10},{10,8},{12,14},{14,12},{16,18},{18,... | collective-permute-start | bytes 1032200 | tf_op jit(solution)/shard_map/ppermute | solution.py:64
  24.1 2.1 %collective-permute-start.4 = (bf16[5,64,512]{2,1,0:T(8,128)(2,1)S(1)}, bf16[5,64,512]{2,1,0:T(8,128)(2,1)S(1)}, u32[]{:S(2)}, u32[]{:S(2)}) collective-permute-start(bf16[5,64,512]{2,1,0:T(8,128)(2,1)S(1)} %after.9._.token.refs_14_), channel_id=1, source_target_pairs={{0,2},{2,0},{4,6},{6,4},{8,10},{10,8},{12,14},{14,12},{16,18},{18,... | collective-permute-start | bytes 983048 | tf_op jit(solution)/shard_map/ppermute | solution.py:64
  26.2 22.4 %copy-start.1 = (f32[512]{0:T(512)S(1)}, f32[512]{0:T(512)}, u32[]{:S(2)}) copy-start(f32[512]{0:T(512)} %param.19) | copy-start | bytes 6148
  26.2 22.4 %copy-start.3 = (s32[4]{0:T(128)S(1)}, s32[4]{0:T(128)}, u32[]{:S(2)}) copy-start(s32[4]{0:T(128)} %species.1) | copy-start | bytes 52
  26.3 22.4 %copy-start.4 = (s32[16]{0:T(128)S(1)}, s32[16]{0:T(128)}, u32[]{:S(2)}) copy-start(s32[16]{0:T(128)} %counts.1) | copy-start | bytes 196
  48.4 4.2 %collective-permute-start.7 = (bf16[2048,512]{1,0:T(8,128)(2,1)S(1)}, bf16[2048,512]{1,0:T(8,128)(2,1)S(1)}, u32[]{:S(2)}, u32[]{:S(2)}) collective-permute-start(bf16[2048,512]{1,0:T(8,128)(2,1)S(1)} %get-tuple-element.94), channel_id=1, source_target_pairs={{0,2},{2,0},{4,6},{6,4},{8,10},{10,8},{12,14},{14,12},{16,18},{18,... | collective-permute-start | bytes 6291464 | tf_op jit(solution)/shard_map/ppermute | solution.py:64
  52.6 3.0 %copy-start.2 = (s32[5]{0:T(128)S(1)}, s32[5]{0:T(128)}, u32[]{:S(2)}) copy-start(s32[5]{0:T(128)} %get-tuple-element.85.other_table.table) | copy-start | bytes 64
  53.1 14.2 %collective-permute-start.10 = (bf16[512,512]{1,0:T(8,128)(2,1)S(1)}, bf16[512,512]{1,0:T(8,128)(2,1)S(1)}, u32[]{:S(2)}, u32[]{:S(2)}) collective-permute-start(bf16[512,512]{1,0:T(8,128)(2,1)S(1)} %get-tuple-element.100), channel_id=1, source_target_pairs={{0,4},{1,5},{2,6},{3,7},{4,0},{5,1},{6,2},{7,3},{8,12},{9,13},{10,... | collective-permute-start | bytes 1572872 | tf_op jit(solution)/shard_map/ppermute | solution.py:815
  54.2 13.9 %collective-permute-start.9 = (bf16[512,512]{1,0:T(8,128)(2,1)S(1)}, bf16[512,512]{1,0:T(8,128)(2,1)S(1)}, u32[]{:S(2)}, u32[]{:S(2)}) collective-permute-start(bf16[512,512]{1,0:T(8,128)(2,1)S(1)} %get-tuple-element.96.refs_0_), channel_id=1, source_target_pairs={{0,1},{1,0},{2,3},{3,2},{4,5},{5,4},{6,7},{7,6},{8,9},{9,8},{10,11... | collective-permute-start | bytes 1572872 | tf_op jit(solution)/shard_map/ppermute | solution.py:815
  61.0 15.5 %collective-permute-start.11 = (bf16[1536,512]{1,0:T(8,128)(2,1)S(1)}, bf16[1536,512]{1,0:T(8,128)(2,1)S(1)}, u32[]{:S(2)}, u32[]{:S(2)}) collective-permute-start(bf16[1536,512]{1,0:T(8,128)(2,1)S(1)} %get-tuple-element.105), channel_id=1, source_target_pairs={{0,2},{2,0},{4,6},{6,4},{8,10},{10,8},{12,14},{14,12},{16,18},{18,... | collective-permute-start | bytes 4718600 | tf_op jit(solution)/shard_map/ppermute | solution.py:64
  64.7 6.1 %collective-permute-start.8 = (bf16[1040,512]{1,0:T(8,128)(2,1)S(1)}, bf16[1040,512]{1,0:T(8,128)(2,1)S(1)}, u32[]{:S(2)}, u32[]{:S(2)}) collective-permute-start(bf16[1040,512]{1,0:T(8,128)(2,1)S(1)} %get-tuple-element.98), channel_id=1, source_target_pairs={{0,2},{2,0},{4,6},{6,4},{8,10},{10,8},{12,14},{14,12},{16,18},{18,... | collective-permute-start | bytes 3194888 | tf_op jit(solution)/shard_map/ppermute | solution.py:64
  68.2 7.5 %collective-permute-start.12 = (bf16[256,512]{1,0:T(8,128)(2,1)S(1)}, bf16[256,512]{1,0:T(8,128)(2,1)S(1)}, u32[]{:S(2)}, u32[]{:S(2)}) collective-permute-start(bf16[256,512]{1,0:T(8,128)(2,1)S(1)} %get-tuple-element.106), channel_id=1, source_target_pairs={{0,4},{1,5},{2,6},{3,7},{4,0},{5,1},{6,2},{7,3},{8,12},{9,13},{10,... | collective-permute-start | bytes 786440 | tf_op jit(solution)/shard_map/ppermute | solution.py:815
  69.3 7.1 %collective-permute-start.13 = (bf16[256,512]{1,0:T(8,128)(2,1)S(1)}, bf16[256,512]{1,0:T(8,128)(2,1)S(1)}, u32[]{:S(2)}, u32[]{:S(2)}) collective-permute-start(bf16[256,512]{1,0:T(8,128)(2,1)S(1)} %get-tuple-element.107), channel_id=1, source_target_pairs={{0,1},{1,0},{2,3},{3,2},{4,5},{5,4},{6,7},{7,6},{8,9},{9,8},{10,11... | collective-permute-start | bytes 786440 | tf_op jit(solution)/shard_map/ppermute | solution.py:815
  71.1 15.3 %collective-permute-start.16 = (bf16[528,512]{1,0:T(8,128)(2,1)S(1)}, bf16[528,512]{1,0:T(8,128)(2,1)S(1)}, u32[]{:S(2)}, u32[]{:S(2)}) collective-permute-start(bf16[528,512]{1,0:T(8,128)(2,1)S(1)} %get-tuple-element.113), channel_id=1, source_target_pairs={{0,8},{1,9},{2,10},{3,11},{4,12},{5,13},{6,14},{7,15},{8,0},{9,1},... | collective-permute-start | bytes 1622024 | tf_op jit(solution)/shard_map/ppermute | solution.py:815
  76.8 9.5 %collective-permute-start.14 = (bf16[384,512]{1,0:T(8,128)(2,1)S(1)}, bf16[384,512]{1,0:T(8,128)(2,1)S(1)}, u32[]{:S(2)}, u32[]{:S(2)}) collective-permute-start(bf16[384,512]{1,0:T(8,128)(2,1)S(1)} %get-tuple-element.111), channel_id=1, source_target_pairs={{0,1},{1,0},{2,3},{3,2},{4,5},{5,4},{6,7},{7,6},{8,9},{9,8},{10,11... | collective-permute-start | bytes 1179656 | tf_op jit(solution)/shard_map/ppermute | solution.py:815
  78.4 8.7 %collective-permute-start.15 = (bf16[384,512]{1,0:T(8,128)(2,1)S(1)}, bf16[384,512]{1,0:T(8,128)(2,1)S(1)}, u32[]{:S(2)}, u32[]{:S(2)}) collective-permute-start(bf16[384,512]{1,0:T(8,128)(2,1)S(1)} %get-tuple-element.112), channel_id=1, source_target_pairs={{0,4},{1,5},{2,6},{3,7},{4,0},{5,1},{6,2},{7,3},{8,12},{9,13},{10,... | collective-permute-start | bytes 1179656 | tf_op jit(solution)/shard_map/ppermute | solution.py:815
  79.3 10.2 %collective-permute-start.19 = (bf16[256,512]{1,0:T(8,128)(2,1)S(1)}, bf16[256,512]{1,0:T(8,128)(2,1)S(1)}, u32[]{:S(2)}, u32[]{:S(2)}) collective-permute-start(bf16[256,512]{1,0:T(8,128)(2,1)S(1)} %get-tuple-element.119), channel_id=1, source_target_pairs={{0,8},{1,9},{2,10},{3,11},{4,12},{5,13},{6,14},{7,15},{8,0},{9,1},... | collective-permute-start | bytes 786440 | tf_op jit(solution)/shard_map/ppermute | solution.py:815
  87.3 8.0 %collective-permute-start.18 = (bf16[336,512]{1,0:T(8,128)(2,1)S(1)}, bf16[336,512]{1,0:T(8,128)(2,1)S(1)}, u32[]{:S(2)}, u32[]{:S(2)}) collective-permute-start(bf16[336,512]{1,0:T(8,128)(2,1)S(1)} %get-tuple-element.117), channel_id=1, source_target_pairs={{0,1},{1,0},{2,3},{3,2},{4,5},{5,4},{6,7},{7,6},{8,9},{9,8},{10,11... | collective-permute-start | bytes 1032200 | tf_op jit(solution)/shard_map/ppermute | solution.py:815
  87.9 7.1 %collective-permute-start.17 = (bf16[320,512]{1,0:T(8,128)(2,1)S(1)}, bf16[320,512]{1,0:T(8,128)(2,1)S(1)}, u32[]{:S(2)}, u32[]{:S(2)}) collective-permute-start(bf16[320,512]{1,0:T(8,128)(2,1)S(1)} %get-tuple-element.116), channel_id=1, source_target_pairs={{0,4},{1,5},{2,6},{3,7},{4,0},{5,1},{6,2},{7,3},{8,12},{9,13},{10,... | collective-permute-start | bytes 983048 | tf_op jit(solution)/shard_map/ppermute | solution.py:815
  89.6 9.0 %collective-permute-start.23 = (bf16[128,512]{1,0:T(8,128)(2,1)S(1)}, bf16[128,512]{1,0:T(8,128)(2,1)S(1)}, u32[]{:S(2)}, u32[]{:S(2)}) collective-permute-start(bf16[128,512]{1,0:T(8,128)(2,1)S(1)} %get-tuple-element.129), channel_id=1, source_target_pairs={{0,16},{1,17},{2,18},{3,19},{4,20},{5,21},{6,22},{7,23},{8,24},{9,... | collective-permute-start | bytes 393224 | tf_op jit(solution)/shard_map/ppermute | solution.py:815
  95.4 6.7 %collective-permute-start.20 = (bf16[192,512]{1,0:T(8,128)(2,1)S(1)}, bf16[192,512]{1,0:T(8,128)(2,1)S(1)}, u32[]{:S(2)}, u32[]{:S(2)}) collective-permute-start(bf16[192,512]{1,0:T(8,128)(2,1)S(1)} %get-tuple-element.121), channel_id=1, source_target_pairs={{0,8},{1,9},{2,10},{3,11},{4,12},{5,13},{6,14},{7,15},{8,0},{9,1},... | collective-permute-start | bytes 589832 | tf_op jit(solution)/shard_map/ppermute | solution.py:815
  95.8 4.3 %collective-permute-start.22 = (bf16[64,512]{1,0:T(8,128)(2,1)S(1)}, bf16[64,512]{1,0:T(8,128)(2,1)S(1)}, u32[]{:S(2)}, u32[]{:S(2)}) collective-permute-start(bf16[64,512]{1,0:T(8,128)(2,1)S(1)} %get-tuple-element.126), channel_id=1, source_target_pairs={{0,1},{1,0},{2,3},{3,2},{4,5},{5,4},{6,7},{7,6},{8,9},{9,8},{10,11... | collective-permute-start | bytes 196616 | tf_op jit(solution)/shard_map/ppermute | solution.py:815
  97.6 4.4 %collective-permute-start.21 = (bf16[80,512]{1,0:T(8,128)(2,1)S(1)}, bf16[80,512]{1,0:T(8,128)(2,1)S(1)}, u32[]{:S(2)}, u32[]{:S(2)}) collective-permute-start(bf16[80,512]{1,0:T(8,128)(2,1)S(1)} %get-tuple-element.125), channel_id=1, source_target_pairs={{0,4},{1,5},{2,6},{3,7},{4,0},{5,1},{6,2},{7,3},{8,12},{9,13},{10,... | collective-permute-start | bytes 245768 | tf_op jit(solution)/shard_map/ppermute | solution.py:815
  102.2 8.4 %collective-permute-start.24 = (bf16[176,512]{1,0:T(8,128)(2,1)S(1)}, bf16[176,512]{1,0:T(8,128)(2,1)S(1)}, u32[]{:S(2)}, u32[]{:S(2)}) collective-permute-start(bf16[176,512]{1,0:T(8,128)(2,1)S(1)} %get-tuple-element.130), channel_id=1, source_target_pairs={{0,16},{1,17},{2,18},{3,19},{4,20},{5,21},{6,22},{7,23},{8,24},{9,... | collective-permute-start | bytes 540680 | tf_op jit(solution)/shard_map/ppermute | solution.py:815
